TPU v7x, 32 devices: a whole 2x2x4 slice. The times are simulated.
32 devices in a mesh: seq: 8 (over z, y), section: 4 (over x, core).
Axes of the slice: x: 2, y: 2, z: 4, core: 2. Of those that a mesh axis runs over, the one named last changes fastest.
Arguments:
- acts: bfloat16 [2048, 1408], P('seq'), may hold values from -6 to 6
- pre_act: bfloat16 [2048, 1536], P('seq', 'section'), may hold values from -6 to 6
- emb_grad: bfloat16 [1024, 1536], P('seq', 'section'), may hold values from -6 to 6
- filters: bfloat16 [7040, 1536], P('seq', 'section'), may hold values from -0.0625 to 0.0625
Outputs:
- input_grad: bfloat16 [2048, 1408], P('seq', 'section')
- filter_grad: float32 [7040, 1536], P('seq', 'section')
All inputs are finite; a program needn't handle non-finite values.
Results may differ from a plain program's by a relative error of at most 0.0049.
Values may be sent and summed in bfloat16 or wider, within the bound.
No kernel may reach another device: no remote copies, remote signals or barrier semaphores. Data moves between devices by JAX's collectives and lax.ppermute only.
A program may use at most 128 MiB of HBM per device.

v0:
```python
import math

import jax
import jax.numpy as jnp
from jax import lax
from jax.sharding import PartitionSpec as P

KERNEL = 5
SEQS = 1


def with_halo(shard, sides, width):
    for axis, dim in sides:
        size, length = (lax.axis_size(axis), shard.shape[dim])
        up = [(i, (i + 1) % size) for i in range(size - 1)]
        down = [(j, i) for i, j in up]
        last = lax.slice_in_dim(shard, length - width, length, axis=dim)
        first = lax.slice_in_dim(shard, 0, width, axis=dim)
        before = lax.ppermute(last, axis, up)
        after = lax.ppermute(first, axis, down)
        shard = jnp.concatenate([before, shard, after], axis=dim)
    return shard


def gelu_slope(value):
    cumul = 0.5 * (1.0 + lax.erf(value * 0.7071067811865476))
    dens = jnp.exp(-0.5 * value * value) * 0.3989422804014327
    return cumul + value * dens


def shards(acts, pre_act, emb_grad, filters):
    rows = acts.shape[0]
    c_in = acts.shape[1]
    upward = jnp.repeat(emb_grad.astype(jnp.float32), 2, axis=0) * 0.5
    zvalue = pre_act.astype(jnp.float32)
    dz_grad = (upward * gelu_slope(zvalue)).astype(jnp.bfloat16)
    total_rows = rows * lax.axis_size("seq")
    length = total_rows // SEQS
    first = lax.axis_index("seq") * rows
    positions = first - 2 + jnp.arange(rows + 4, dtype=jnp.int32)
    inside = (jnp.floor_divide(positions, length) == first // length).astype(jnp.bfloat16)[:, None]
    scale_value = 1.0 / math.sqrt(total_rows)
    grad_rim = with_halo(dz_grad, (("seq", 0),), 2) * inside
    whole_term = (
        jnp.concatenate(
            [
                jnp.einsum(
                    "rc,ro->co",
                    acts,
                    grad_rim[4 - k : 4 - k + rows],
                    preferred_element_type=jnp.float32,
                )
                for k in range(KERNEL)
            ],
            axis=0,
        )
        * scale_value
    )
    piece = lax.all_gather(filters, "seq", axis=0, tiled=True)
    width = piece.shape[0]
    product = jnp.einsum("ro,no->rn", grad_rim, piece, preferred_element_type=jnp.float32)
    tap_of = jnp.arange(width, dtype=jnp.int32) // c_in
    total = jnp.zeros((rows, width), jnp.float32)
    for k in range(KERNEL):
        total = total + jnp.where((tap_of == k)[None, :], product[4 - k : 4 - k + rows], 0.0)
    partial_input = total.reshape(rows, KERNEL, c_in).sum(axis=1)
    input_grad = lax.psum_scatter(partial_input, "section", scatter_dimension=1, tiled=True).astype(
        jnp.bfloat16
    )
    filter_grad = lax.psum_scatter(whole_term, "seq", scatter_dimension=0, tiled=True)
    return (input_grad, filter_grad)


def solution(mesh):
    in_specs = (P("seq", None), P("seq", "section"), P("seq", "section"), P("seq", "section"))
    out_specs = (P("seq", "section"), P("seq", "section"))
    return jax.shard_map(shards, mesh=mesh, in_specs=in_specs, out_specs=out_specs, check_vma=False)
```

profile of v0, /device:TPU:1, one launch (start us, length us, event | category | flops | bytes accessed | tf_op | source)
XLA Modules:
  0.0 344.8 jit_solution(9335022377954916858)
XLA Ops:
  7.2 0.7 all-gather.2.cloned.1.call-update
  8.0 0.9 convert_multiply_fusion.4
  8.9 0.1 broadcast_in_dim.46
  9.0 0.3 mul.55
  9.3 1.1 fusion.16
  10.4 4.0 %collective-permute-start = (bf16[2,384]{1,0:T(2,128)(2,1)S(1)}, bf16[2,384]{1,0:T(2,128)(2,1)S(1)}, u32[]{:S(2)}, u32[]{:S(2)}) collective-permute-start(bf16[2,384]{1,0:T(2,128)(2,1)S(1)} %get-tuple-element.8), channel_id=1, source_target_pairs={{0,4},{4,8},{8,12},{12,16},{16,20},{20,24},{24,28},{1,5},{5,9},{9,... | collective-permute-start | bytes 4616 | tf_op jit(solution)/shard_map/ppermute | solution.py:19
  14.4 1.3 collective-permute-start.1
  15.8 2.9 collective-permute-done.1
  18.7 0.1 maximum_multiply_fusion
  18.9 2.0 fusion.8
  20.9 2.0 fusion.7
  22.8 76.9 %all-gather.2.cloned.1.call-done = bf16[7040,384]{1,0:T(8,128)(2,1)} async-done(((bf16[880,384]{1,0:T(8,128)(2,1)}), bf16[7040,384]{1,0:T(8,128)(2,1)}) %all-gather.2.cloned.1.call-update) | async-done | bytes 5406736 | tf_op jit(solution)/shard_map/all_gather | solution.py:59
  99.7 4.7 %fusion.30 = f32[260,7040]{1,0:T(8,128)S(1)} fusion(bf16[7040,384]{1,0:T(8,128)(2,1)} %all-gather.2.cloned.1.call-done, bf16[2,384]{1,0:T(2,128)(2,1)S(1)} %collective-permute-done.1, bf16[256,384]{1,0:T(8,128)(2,1)S(1)} %fusion.16, bf16[2,384]{1,0:T(2,128)(2,1)S(1)} %collective-permute-done, bf16[260]{0:T(512)(128)(2,1)S(1)} %fusion.29), kind=kOutput, calls=%fused_computation.62 | convolution fusion | flops 1406545920 | bytes 12928520 | tf_op jit(solution)/shard_map/ro,no->rn/dot_general | solution.py:61
  104.4 6.0 %fusion = f32[256,7040]{1,0:T(8,128)} fusion(f32[260,7040]{1,0:T(8,128)S(1)} %fusion.30, pred[7040]{0:T(1024)(128)(4,1)S(1)} %get-tuple-element.10, pred[7040]{0:T(1024)(128)(4,1)S(1)} %get-tuple-element.11, pred[7040]{0:T(1024)(128)(4,1)S(1)} %get-tuple-element.12, pred[7040]{0:T(1024)(128)(4,1)S(1)} %broadcast_compare_fusion.4, ...), kind=kLoop, calls=%fused_computation.1 | loop fusion | flops 16220160 | bytes 43288960 | tf_op jit(solution)/shard_map/add | solution.py:65
  110.5 8.6 %copy.9 = f32[256,7040]{0,1:T(8,128)} copy(f32[256,7040]{1,0:T(8,128)} %fusion) | data formatting | bytes 14417920 | tf_op jit(solution)/shard_map/add | solution.py:65
  119.0 4.8 %reduce_sum.9 = f32[256,1408]{0,1:T(8,128)} reduce(f32[256,5,1408]{0,2,1:T(8,128)} %bitcast.28, f32[]{:T(128)} %constant.61.clone.1), dimensions={1}, to_apply=%region_0.1 | reduce | flops 1441792 | bytes 8650756 | tf_op jit(solution)/shard_map/reduce_sum | solution.py:66
  123.9 0.0 reduce-scatter.7.cloned.1.call-start
  123.9 1.9 fusion.6
  125.8 1.9 fusion.5
  127.7 1.9 fusion.4
  129.6 9.4 %broadcast_multiply_fusion = f32[7040,384]{0,1:T(8,128)} fusion(f32[7040,384]{0,1:T(8,128)} %fusion.4), kind=kLoop, calls=%fused_computation.9 | loop fusion | flops 2703360 | bytes 21626880 | tf_op jit(solution)/shard_map/mul | solution.py:45
  139.0 12.1 %copy.11 = f32[7040,384]{1,0:T(8,128)} copy(f32[7040,384]{0,1:T(8,128)} %broadcast_multiply_fusion) | data formatting | bytes 21626880
  151.2 1.7 convert_element_type.23
  152.8 185.4 %reduce-scatter.7.cloned.1.call-done = f32[880,384]{1,0:T(8,128)} async-done(((f32[7040,384]{1,0:T(8,128)}), f32[880,384]{1,0:T(8,128)}) %reduce-scatter.7.cloned.1.call-update) | async-done | bytes 1351696
  (13 shorter events, 0.2 us)
Async XLA Ops:
  7.2 11.7 %copy-start = (bf16[256,1408]{1,0:T(8,128)(2,1)S(1)}, bf16[256,1408]{1,0:T(8,128)(2,1)}, u32[]{:S(2)}) copy-start(bf16[256,1408]{1,0:T(8,128)(2,1)} %param.4) | copy-start | bytes 2162692
  7.2 92.6 %all-gather.2.cloned.1.call-start = ((), (), s32[]{:S(2)}) async-start(), calls=%async_computation.2 | async-start | bytes 6082560 | tf_op jit(solution)/shard_map/all_gather | solution.py:59
  7.9 143.3 %reduce-scatter.5.cloned.1.call-start = ((), (), s32[]{:S(2)}) async-start(), calls=%async_computation.3 | async-start | bytes 1802240 | tf_op jit(solution)/shard_map/reduce_scatter | solution.py:67
  10.4 5.4 %collective-permute-start = (bf16[2,384]{1,0:T(2,128)(2,1)S(1)}, bf16[2,384]{1,0:T(2,128)(2,1)S(1)}, u32[]{:S(2)}, u32[]{:S(2)}) collective-permute-start(bf16[2,384]{1,0:T(2,128)(2,1)S(1)} %get-tuple-element.8), channel_id=1, source_target_pairs={{0,4},{4,8},{8,12},{12,16},{16,20},{20,24},{24,28},{1,5},{5,9},{9,... | collective-permute-start | bytes 4616 | tf_op jit(solution)/shard_map/ppermute | solution.py:19
  14.4 4.3 %collective-permute-start.1 = (bf16[2,384]{1,0:T(2,128)(2,1)S(1)}, bf16[2,384]{1,0:T(2,128)(2,1)S(1)}, u32[]{:S(2)}, u32[]{:S(2)}) collective-permute-start(bf16[2,384]{1,0:T(2,128)(2,1)S(1)} %get-tuple-element.9), channel_id=1, source_target_pairs={{4,0},{8,4},{12,8},{16,12},{20,16},{24,20},{28,24},{5,1},{9,5},{13... | collective-permute-start | bytes 4616 | tf_op jit(solution)/shard_map/ppermute | solution.py:20
  123.9 214.3 %reduce-scatter.7.cloned.1.call-start = ((), (), s32[]{:S(2)}) async-start(), calls=%async_computation.4 | async-start | bytes 12165120
Sparse Core Ops, SparseCore 0:
  10.2 89.5 all-gather.1
  124.0 26.3 reduce-scatter.4
  155.0 183.1 reduce-scatter.6
where the time goes:
time: 346 us; the launch traced here: 345 us
  waiting for transfers between devices  266 us (77%)
  other arithmetic  24.1 us (7%)
  local copies, waits for them, and re-layouts  21.1 us (6%)
  matrix products  14.3 us (4%)
  between operations  13.9 us (4%)
  starting transfers between devices  5.38 us (2%)
    unnamed x4, waiting for transfers between devices  186 us
    all_gather x1, waiting for transfers between devices, shards(): piece = lax.all_gather(filters, 'seq', axis=0, tiled=True)  76.9 us
    unnamed x3, local copies, waits for them, and re-layouts  12.1 us
    dot_general x5, matrix products, shards(): jnp.einsum('rc,ro->co', acts, grad_rim[4 - k:4 - k + rows], preferred_ele...  9.63 us
    mul x1, other arithmetic, shards(): jnp.concatenate([jnp.einsum('rc,ro->co', acts, grad_rim[4 - k:4 - k + row...  9.42 us
    add x1, local copies, waits for them, and re-layouts, shards(): total + jnp.where((tap_of == k)[None, :], product[4 - k:4 - k + rows], 0.0)  8.59 us
  transfers between devices with their start and end apart: 5, of which 3 were waited for; matrix products, arithmetic and copies ran while one was open for 10% of the time, Pallas kernels for 0%

commit v1 on v0

v1 whole, which is shorter than its diff:
```python
import functools
import math

import jax
import jax.numpy as jnp
from jax import lax
from jax.experimental import pallas as pl
from jax.experimental.pallas import tpu as pltpu
from jax.sharding import PartitionSpec as P

KERNEL = 5
SEQS = 1
F32 = jnp.float32
BF16 = jnp.bfloat16


def with_halo(shard, sides, width):
    for axis, dim in sides:
        size, length = (lax.axis_size(axis), shard.shape[dim])
        up = [(i, (i + 1) % size) for i in range(size - 1)]
        down = [(j, i) for i, j in up]
        last = lax.slice_in_dim(shard, length - width, length, axis=dim)
        first = lax.slice_in_dim(shard, 0, width, axis=dim)
        before = lax.ppermute(last, axis, up)
        after = lax.ppermute(first, axis, down)
        shard = jnp.concatenate([before, shard, after], axis=dim)
    return shard


def gelu_slope(value):
    cumul = 0.5 * (1.0 + lax.erf(value * 0.7071067811865476))
    dens = jnp.exp(-0.5 * value * value) * 0.3989422804014327
    return cumul + value * dens


def dz_block(pre_act, emb_grad):
    upward = jnp.repeat(emb_grad.astype(F32), 2, axis=0) * 0.5
    return (upward * gelu_slope(pre_act.astype(F32))).astype(BF16)


def shards_any(acts, pre_act, emb_grad, filters):
    rows = acts.shape[0]
    c_in = acts.shape[1]
    dz_grad = dz_block(pre_act, emb_grad)
    total_rows = rows * lax.axis_size("seq")
    length = total_rows // SEQS
    first = lax.axis_index("seq") * rows
    positions = first - 2 + jnp.arange(rows + 4, dtype=jnp.int32)
    inside = (jnp.floor_divide(positions, length) == first // length).astype(BF16)[:, None]
    scale_value = 1.0 / math.sqrt(total_rows)
    grad_rim = with_halo(dz_grad, (("seq", 0),), 2) * inside
    whole_term = (
        jnp.concatenate(
            [
                jnp.einsum(
                    "rc,ro->co",
                    acts,
                    grad_rim[4 - k : 4 - k + rows],
                    preferred_element_type=F32,
                )
                for k in range(KERNEL)
            ],
            axis=0,
        )
        * scale_value
    )
    piece = lax.all_gather(filters, "seq", axis=0, tiled=True)
    width = piece.shape[0]
    product = jnp.einsum("ro,no->rn", grad_rim, piece, preferred_element_type=F32)
    tap_of = jnp.arange(width, dtype=jnp.int32) // c_in
    total = jnp.zeros((rows, width), F32)
    for k in range(KERNEL):
        total = total + jnp.where((tap_of == k)[None, :], product[4 - k : 4 - k + rows], 0.0)
    partial_input = total.reshape(rows, KERNEL, c_in).sum(axis=1)
    input_grad = lax.psum_scatter(partial_input, "section", scatter_dimension=1, tiled=True).astype(BF16)
    filter_grad = lax.psum_scatter(whole_term, "seq", scatter_dimension=0, tiled=True)
    return (input_grad, filter_grad)


TAPS = (((0, 0), (0, 1), (1, 0), (1, 1), (2, 0)), ((2, 0), (3, 1), (3, 0), (4, 1), (4, 0)))


def coords():
    i, j = lax.axis_index("seq"), lax.axis_index("section")
    return i // 4, (i // 2) % 2, i % 2, j // 2, j % 2


def everyone(place):
    pairs = []
    for g in range(32):
        h, zl, y, x, c = (g >> 4) & 1, (g >> 3) & 1, (g >> 2) & 1, (g >> 1) & 1, g & 1
        h, zl, y, x, c = place(h, zl, y, x, c)
        pairs.append((g, h * 16 + zl * 8 + y * 4 + x * 2 + c))
    return pairs


def send(value, place):
    return lax.ppermute(value, ("seq", "section"), everyone(place))


def along_seq(value, place):
    return lax.ppermute(value, "seq", [(i, place(i)) for i in range(8)])


def in_half(value, step):
    return along_seq(value, lambda i: 4 * (i // 4) + (i % 4 + step) % 4)


SWAP_C = lambda h, zl, y, x, c: (h, zl, y, x, 1 - c)
SWAP_X = lambda h, zl, y, x, c: (h, zl, y, 1 - x, c)


def turn(a, b):
    return lambda h, zl, y, x, c: (h ^ a, c, y ^ b, x, zl)


def input_kernel(rows, unit, at, *refs):
    dz_refs, w_refs, (out_ref, dz_ref), (weights, parts) = refs[:8], refs[8:13], refs[13:15], refs[15:]
    h, zl, y, c = at[0], at[1], at[2], at[4]
    q = 2 * zl + y
    z = 2 * h + zl
    for s in range(8):
        block = 2 * lax.rem(z + 4 - s // 2, 4) + (y ^ (s % 2))
        dz_ref[pl.ds(pl.multiple_of(block * rows, rows), rows), :] = dz_refs[s][...]
    for m in range(5):
        weights[lax.rem(q + 5 - m, 5)] = w_refs[m][...]
    total = 8 * rows
    for v in range(5):
        parts[v, 0:8, :] = jnp.zeros((8, unit), F32)
        parts[v, 8 + total : 16 + total, :] = jnp.zeros((8, unit), F32)

    @pl.loop(0, 8)
    def _(t):
        start = pl.multiple_of(t * rows, rows)
        left = dz_ref[pl.ds(start, rows), :]
        for v in range(5):
            parts[v, pl.ds(start + 8, rows), :] = lax.dot_general(
                left, weights[v], (((1,), (1,)), ((), ())), preferred_element_type=F32
            )

    for half in range(2):

        @pl.when(h == half)
        def _():
            for t in range(8):
                sums = [None, None]
                for v, (tap, which) in enumerate(TAPS[half]):
                    first = 8 + t * rows + 2 - tap
                    term = parts[v, first : first + rows, :]
                    sums[which] = term if sums[which] is None else sums[which] + term
                away = ((t // 2) % 2) ^ c
                for which in range(2):
                    out_ref[away, which ^ half, 2 * (t // 4) + t % 2] = sums[which].astype(BF16)


def left_kernel(rows, unit, at, s00, s10, s01, s11, out_ref, lines):
    h, zl, y, x, c = at[0], at[1], at[2], at[3], at[4]
    for xr, cr, ref in ((0, 0, s00), (1, 0, s10), (0, 1, s01), (1, 1, s11)):
        which = x ^ xr ^ h
        for a in range(2):
            for b in range(2):
                block = 4 * (h ^ a) + 2 * (c ^ cr) + (y ^ b)
                lines[which, :, pl.ds(pl.multiple_of(block * rows, rows), rows)] = ref[2 * a + b].astype(F32).T
    total = 8 * rows
    place = lax.broadcasted_iota(jnp.int32, (unit, total), 1)
    for half in range(2):

        @pl.when(h == half)
        def _():
            for v, (tap, which) in enumerate(TAPS[half]):
                line = lines[which]
                if tap != 2:
                    line = pltpu.roll(line, (2 - tap) % total, 1)
                    fits = (place + (tap - 2) >= 0) & (place + (tap - 2) < total)
                    line = jnp.where(fits, line, 0.0)
                out_ref[v] = line.astype(BF16)


def vmem(n):
    return [pl.BlockSpec(memory_space=pltpu.VMEM)] * n


def shards_block(acts, pre_act, emb_grad, filters):
    rows, c_in = acts.shape
    wide = filters.shape[1]
    unit = c_in // 8
    total = 8 * rows
    h, zl, y, x, c = coords()
    q = 2 * zl + y
    at = jnp.stack([h, zl, y, x, c]).astype(jnp.int32)
    scale = 1.0 / math.sqrt(total)
    part = functools.partial(lax.dynamic_index_in_dim, axis=0, keepdims=False)

    dz = dz_block(pre_act, emb_grad)
    blocks = [dz] + [along_seq(dz, lambda i, s=s: (i + 2 * s) % 8) for s in (1, 2, 3)]
    pairs = []
    for block in blocks:
        pairs += [block, along_seq(block, lambda i: i ^ 1)]

    own = [filters[m * unit : (m + 1) * unit] for m in range(5)]
    weights = [own[0]] + [in_half(own[m], m) for m in (1, 2, 3)] + [own[4]]

    mine = lax.dynamic_slice_in_dim(acts, 2 * unit * (2 * x + c), 2 * unit, axis=1)
    halves = jnp.stack([mine[:, :unit], mine[:, unit:]])
    got = jnp.stack([send(part(halves, y ^ b), turn(a, b)) for a in range(2) for b in range(2)])
    other = send(got, SWAP_X)
    far, far_other = send(got, SWAP_C), send(other, SWAP_C)
    left = pl.pallas_call(
        functools.partial(left_kernel, rows, unit),
        out_shape=jax.ShapeDtypeStruct((5, unit, total), BF16),
        in_specs=[pl.BlockSpec(memory_space=pltpu.SMEM)] + vmem(4),
        out_specs=vmem(1)[0],
        scratch_shapes=[pltpu.VMEM((2, unit, total), F32)],
        compiler_params=pltpu.CompilerParams(vmem_limit_bytes=48 << 20),
        cost_estimate=pl.CostEstimate(flops=0, bytes_accessed=6 << 20, transcendentals=0),
        name="left",
    )(at, got, other, far, far_other)

    partial, dz_all = pl.pallas_call(
        functools.partial(input_kernel, rows, unit),
        out_shape=(
            jax.ShapeDtypeStruct((2, 2, 4, rows, unit), BF16),
            jax.ShapeDtypeStruct((total, wide), BF16),
        ),
        in_specs=[pl.BlockSpec(memory_space=pltpu.SMEM)] + vmem(13),
        out_specs=tuple(vmem(2)),
        scratch_shapes=[pltpu.VMEM((5, unit, wide), BF16), pltpu.VMEM((5, total + 16, unit), F32)],
        compiler_params=pltpu.CompilerParams(vmem_limit_bytes=48 << 20),
        cost_estimate=pl.CostEstimate(flops=2 * total * 5 * unit * wide, bytes_accessed=6 << 20, transcendentals=0),
        name="input",
    )(at, *pairs, *weights)

    summed = partial[0].astype(F32) + send(partial[1], SWAP_C).astype(F32)
    crossed = send(part(summed, 1 - x).astype(BF16), SWAP_X)
    ready = (part(summed, x) + crossed.astype(F32)).astype(BF16)
    units = []
    for b in range(2):
        came = [send(part(ready, 2 * (h ^ a) + (y ^ b)), turn(a, b)).astype(F32) for a in range(2)]
        units.append((came[0] + came[1]).astype(BF16))
    input_grad = jnp.where(y == 0, jnp.concatenate(units, axis=1), jnp.concatenate(units[::-1], axis=1))

    grads = jnp.dot(left.reshape(5 * unit, total), dz_all, preferred_element_type=F32).reshape(5, unit, wide) * scale
    pieces = [part(grads, q)]
    for m in (1, 2, 3):
        pieces.append(in_half(part(grads, (q + 5 - m) % 5).astype(BF16), -m).astype(F32))
    pieces.append(part(grads, q + 1))
    return input_grad, jnp.concatenate(pieces, axis=0)


def solution(mesh):
    in_specs = (P("seq", None), P("seq", "section"), P("seq", "section"), P("seq", "section"))
    out_specs = (P("seq", "section"), P("seq", "section"))
    block = mesh.shape["seq"] == 8 and mesh.shape["section"] == 4
    body = shards_block if block else shards_any
    return jax.shard_map(body, mesh=mesh, in_specs=in_specs, out_specs=out_specs, check_vma=False)
```

time: 346 us -> 130 us (0.38)
  waiting for transfers between devices: 266 us -> 36.7 us
  starting transfers between devices: 5.38 us -> 44 us
  other arithmetic: 24.1 us -> 4.29 us
  between operations: 13.9 us -> 0.99 us
  matrix products: 14.3 us -> 3.13 us
  local copies, waits for them, and re-layouts: 21.1 us -> 31.3 us
  Pallas kernels: 0 us -> 8.64 us
    unnamed x4 -> x0, waiting for transfers between devices: 186 us -> none
    all_gather x1 -> x0, waiting for transfers between devices: 76.9 us -> none  [shards(): piece = lax.all_gather(filters, 'seq', axis=0, tiled=True)]
    ppermute x2 -> x26, starting transfers between devices: 5.27 us -> 44 us  [the longest x13 28.1 us: send(): return lax.ppermute(value, ('seq', 'section'), everyone(place))]
    ppermute x2 -> x26, waiting for transfers between devices: 2.91 us -> 36.7 us  [the longest x13 22.7 us: along_seq(): return lax.ppermute(value, 'seq', [(i, place(i)) for i in range(8)])]
    dot_general x6 -> x1, matrix products: 14.3 us -> 3.13 us  [shards_block(): jnp.dot(left.reshape(5 * unit, total), dz_all, preferred_element_type=F32)]
    mul x3 -> x1, other arithmetic: 10.4 us -> 0.02 us  [dz_block(): upward = jnp.repeat(emb_grad.astype(F32), 2, axis=0) * 0.5]
    pallas_call x0 -> x2, Pallas kernels: none -> 8.64 us  [the longest x1 5.86 us: shards_block(): pl.pallas_call(functools.partial(input_kernel, rows, unit), out_shape=(ja...]
    add x1 -> x0, local copies, waits for them, and re-layouts: 8.59 us -> none  [shards(): total + jnp.where((tap_of == k)[None, :], product[4 - k:4 - k + rows], 0.0)]
  transfers between devices with their start and end apart: 5 -> 26, of which waited for: 3 -> 10; matrix products, arithmetic and copies ran while one was open for 10% -> 13% of each run, Pallas kernels for 0% -> 7%
where the time goes in v1:
time: 130 us; the launch traced here: 129 us
  starting transfers between devices  44 us (34%)
  waiting for transfers between devices  36.7 us (28%)
  local copies, waits for them, and re-layouts  31.3 us (24%)
  Pallas kernels  8.64 us (7%)
  other arithmetic  4.29 us (3%)
  matrix products  3.13 us (2%)
    ppermute x13, starting transfers between devices, send(): return lax.ppermute(value, ('seq', 'section'), everyone(place))  28.1 us
    ppermute x13, waiting for transfers between devices, along_seq(): return lax.ppermute(value, 'seq', [(i, place(i)) for i in range(8)])  22.7 us
    unnamed x55, local copies, waits for them, and re-layouts  20 us
    ppermute x13, starting transfers between devices, along_seq(): return lax.ppermute(value, 'seq', [(i, place(i)) for i in range(8)])  15.9 us
    ppermute x13, waiting for transfers between devices, send(): return lax.ppermute(value, ('seq', 'section'), everyone(place))  14.1 us
    pallas_call x1, Pallas kernels, shards_block(): pl.pallas_call(functools.partial(input_kernel, rows, unit), out_shape=(ja...  5.86 us
    squeeze x2, local copies, waits for them, and re-layouts, shards_block(): summed = partial[0].astype(F32) + send(partial[1], SWAP_C).astype(F32)  3.25 us
    dot_general x1, matrix products, shards_block(): jnp.dot(left.reshape(5 * unit, total), dz_all, preferred_element_type=F32)  3.13 us
  transfers between devices with their start and end apart: 26, of which 10 were waited for; matrix products, arithmetic and copies ran while one was open for 13% of the time, Pallas kernels for 7%

profile of v1, /device:TPU:1, one launch (start us, length us, event | category | flops | bytes accessed | tf_op | source)
XLA Modules:
  0.0 129.1 jit_solution(334503318176267907)
XLA Ops:
  2.1 5.7 %collective-permute-start.19 = (bf16[256,176]{1,0:T(8,128)(2,1)S(1)}, bf16[256,176]{1,0:T(8,128)(2,1)S(1)}, u32[]{:S(2)}, u32[]{:S(2)}) collective-permute-start(bf16[256,176]{1,0:T(8,128)(2,1)S(1)} %get-tuple-element.21), channel_id=1, source_target_pairs={{0,20},{1,28},{2,22},{3,30},{4,16},{5,24},{6,18},{7,26},{8,21},{9,... | collective-permute-start | bytes 270344 | tf_op jit(solution)/shard_map/ppermute | solution.py:98
  8.4 3.2 %collective-permute-start.16 = (bf16[256,176]{1,0:T(8,128)(2,1)S(1)}, bf16[256,176]{1,0:T(8,128)(2,1)S(1)}, u32[]{:S(2)}, u32[]{:S(2)}) collective-permute-start(bf16[256,176]{1,0:T(8,128)(2,1)S(1)} %get-tuple-element.20), channel_id=1, source_target_pairs={{0,0},{1,8},{2,2},{3,10},{4,4},{5,12},{6,6},{7,14},{8,1},{9,9},{10... | collective-permute-start | bytes 270344 | tf_op jit(solution)/shard_map/ppermute | solution.py:98
  15.6 4.8 %collective-permute-start.3 = (bf16[256,384]{1,0:T(8,128)(2,1)S(1)}, bf16[256,384]{1,0:T(8,128)(2,1)S(1)}, u32[]{:S(2)}, u32[]{:S(2)}) collective-permute-start(bf16[256,384]{1,0:T(8,128)(2,1)S(1)} %fusion.14.refs_0_), channel_id=1, source_target_pairs={{0,16},{4,20},{8,24},{12,28},{16,0},{20,4},{24,8},{28,12},{1,17},{... | collective-permute-start | bytes 589832 | tf_op jit(solution)/shard_map/ppermute | solution.py:102
  20.4 1.6 %collective-permute-start.5 = (bf16[256,384]{1,0:T(8,128)(2,1)S(1)}, bf16[256,384]{1,0:T(8,128)(2,1)S(1)}, u32[]{:S(2)}, u32[]{:S(2)}) collective-permute-start(bf16[256,384]{1,0:T(8,128)(2,1)S(1)} %fusion.14.refs_0_), channel_id=1, source_target_pairs={{0,24},{4,28},{8,0},{12,4},{16,8},{20,12},{24,16},{28,20},{1,25},{... | collective-permute-start | bytes 589832 | tf_op jit(solution)/shard_map/ppermute | solution.py:102
  24.3 11.4 %collective-permute-done.8.refs_10_ = bf16[176,384]{1,0:T(8,128)(2,1)S(1)} collective-permute-done((bf16[176,384]{1,0:T(8,128)(2,1)S(1)}, bf16[176,384]{1,0:T(8,128)(2,1)S(1)}, u32[]{:S(2)}, u32[]{:S(2)}) %collective-permute-start.8) | collective-permute-done | bytes 135200 | tf_op jit(solution)/shard_map/ppermute | solution.py:102
  37.7 3.5 %collective-permute-done.9.refs_11_ = bf16[176,384]{1,0:T(8,128)(2,1)S(1)} collective-permute-done((bf16[176,384]{1,0:T(8,128)(2,1)S(1)}, bf16[176,384]{1,0:T(8,128)(2,1)S(1)}, u32[]{:S(2)}, u32[]{:S(2)}) %collective-permute-start.9) | collective-permute-done | bytes 135200 | tf_op jit(solution)/shard_map/ppermute | solution.py:102
  41.8 1.8 %collective-permute-start = (bf16[256,384]{1,0:T(8,128)(2,1)S(1)}, bf16[256,384]{1,0:T(8,128)(2,1)S(1)}, u32[]{:S(2)}, u32[]{:S(2)}) collective-permute-start(bf16[256,384]{1,0:T(8,128)(2,1)S(1)} %fusion.14.refs_0_), channel_id=1, source_target_pairs={{0,4},{4,0},{8,12},{12,8},{16,20},{20,16},{24,28},{28,24},{1,5},{5... | collective-permute-start | bytes 589832 | tf_op jit(solution)/shard_map/ppermute | solution.py:102
  47.9 4.1 %collective-permute-start.21 = (bf16[4,256,176]{2,1,0:T(8,128)(2,1)S(1)}, bf16[4,256,176]{2,1,0:T(8,128)(2,1)}, u32[]{:S(2)}, u32[]{:S(2)}) collective-permute-start(bf16[4,256,176]{2,1,0:T(8,128)(2,1)S(1)} %pad_maximum_fusion.s00), channel_id=1, source_target_pairs={{0,1},{1,0},{2,3},{3,2},{4,5},{5,4},{6,7},{7,6},{8,9},{9,8},{10,11... | collective-permute-start | bytes 1081352 | tf_op jit(solution)/shard_map/ppermute | solution.py:98
  52.7 2.8 %collective-permute-done.4.refs_5_ = bf16[256,384]{1,0:T(8,128)(2,1)S(1)} collective-permute-done((bf16[256,384]{1,0:T(8,128)(2,1)S(1)}, bf16[256,384]{1,0:T(8,128)(2,1)S(1)}, u32[]{:S(2)}, u32[]{:S(2)}) %collective-permute-start.4) | collective-permute-done | bytes 196640 | tf_op jit(solution)/shard_map/ppermute | solution.py:102
  56.2 3.5 %collective-permute-done.6.refs_7_ = bf16[256,384]{1,0:T(8,128)(2,1)S(1)} collective-permute-done((bf16[256,384]{1,0:T(8,128)(2,1)S(1)}, bf16[256,384]{1,0:T(8,128)(2,1)S(1)}, u32[]{:S(2)}, u32[]{:S(2)}) %collective-permute-start.6) | collective-permute-done | bytes 196640 | tf_op jit(solution)/shard_map/ppermute | solution.py:102
  70.5 5.9 %input.1 = (bf16[2,2,4,256,176]{4,3,2,1,0:T(8,128)(2,1)S(1)}, bf16[2048,384]{1,0:T(8,128)(2,1)S(1)}) custom-call(s32[5]{0:T(128)S(1)} %stack.47.at, bf16[256,384]{1,0:T(8,128)(2,1)S(1)} %fusion.14.refs_0_, bf16[256,384]{1,0:T(8,128)(2,1)S(1)} %copy-done.8, bf16[256,384]{1,0:T(8,128)(2,1)S(1)} %copy-done.2, bf16[256,384]{1,0:T(8,128)(2,1)S(1)} %copy-done.10, ...), custom_call_target="tpu_custom_call" | custom-call | flops 1384120320 | bytes 6291456 | tf_op jit(solution)/shard_map/input/pallas_call | solution.py:219
  78.6 2.2 %copy.10 = bf16[2,4,256,176]{2,3,1,0:T(8,128)(2,1)} copy(bf16[2,4,256,176]{3,2,1,0:T(8,128)(2,1)} %slice_bitcast_fusion) | data formatting | bytes 1441792 | tf_op jit(solution)/shard_map/squeeze | solution.py:233
  80.8 2.3 %collective-permute-start.10 = (bf16[2,4,256,176]{2,3,1,0:T(8,128)(2,1)}, bf16[2,4,256,176]{2,3,1,0:T(8,128)(2,1)}, u32[]{:S(2)}, u32[]{:S(2)}) collective-permute-start(bf16[2,4,256,176]{2,3,1,0:T(8,128)(2,1)} %copy.10), channel_id=1, source_target_pairs={{0,1},{1,0},{2,3},{3,2},{4,5},{5,4},{6,7},{7,6},{8,9},{9,8},{10,11... | collective-permute-start | bytes 2162696 | tf_op jit(solution)/shard_map/ppermute | solution.py:98
  83.2 2.8 %left.1 = bf16[5,176,2048]{2,1,0:T(8,128)(2,1)S(1)} custom-call(s32[5]{0:T(128)S(1)} %stack.47.at, bf16[4,256,176]{2,1,0:T(8,128)(2,1)S(1)} %pad_maximum_fusion.s00, bf16[4,256,176]{2,1,0:T(8,128)(2,1)S(1)} %collective-permute-done.20.s10, bf16[4,256,176]{2,1,0:T(8,128)(2,1)} %collective-permute-done.21.s01, bf16[4,256,176]{2,1,0:T(8,128)(2,1)} %collective-permute-done.22.s11), custom_call_target="tpu_custom_call" | custom-call | bytes 6291456 | tf_op jit(solution)/shard_map/left/pallas_call | solution.py:208
  86.0 3.1 %fusion.2 = f32[5,176,384]{2,1,0:T(8,128)} fusion(bf16[5,176,2048]{2,1,0:T(8,128)(2,1)S(1)} %left.1, bf16[2048,384]{1,0:T(8,128)(2,1)S(1)} %copy-done.22), kind=kOutput, calls=%fused_computation.3 | convolution fusion | flops 1384458240 | bytes 6529024 | tf_op jit(solution)/shard_map/dot_general | solution.py:242
  90.3 2.1 %collective-permute-start.23 = (bf16[176,384]{1,0:T(8,128)(2,1)S(1)}, bf16[176,384]{1,0:T(8,128)(2,1)S(1)}, u32[]{:S(2)}, u32[]{:S(2)}) collective-permute-start(bf16[176,384]{1,0:T(8,128)(2,1)S(1)} %get-tuple-element.8), channel_id=1, source_target_pairs={{0,12},{4,0},{8,4},{12,8},{16,28},{20,16},{24,20},{28,24},{1,13},{... | collective-permute-start | bytes 405512 | tf_op jit(solution)/shard_map/ppermute | solution.py:102
  93.9 1.4 %collective-permute-done.23 = bf16[176,384]{1,0:T(8,128)(2,1)S(1)} collective-permute-done((bf16[176,384]{1,0:T(8,128)(2,1)S(1)}, bf16[176,384]{1,0:T(8,128)(2,1)S(1)}, u32[]{:S(2)}, u32[]{:S(2)}) %collective-permute-start.23) | collective-permute-done | bytes 135200 | tf_op jit(solution)/shard_map/ppermute | solution.py:102
  96.5 2.2 %copy.11 = bf16[2,4,256,176]{3,2,1,0:T(8,128)(2,1)} copy(bf16[2,4,256,176]{2,3,1,0:T(8,128)(2,1)} %collective-permute-done.10) | data formatting | bytes 1441792 | tf_op jit(solution)/shard_map/ppermute | solution.py:98
  98.7 1.4 %convert_add_fusion = f32[2,4,256,176]{3,2,1,0:T(8,128)S(1)} fusion(bf16[2,4,256,176]{3,2,1,0:T(8,128)(2,1)} %copy.11, bf16[2,2,4,256,176]{4,3,2,1,0:T(8,128)(2,1)S(1)} %get-tuple-element.4), kind=kLoop, calls=%fused_computation | loop fusion | flops 1081344 | bytes 2883584 | tf_op jit(solution)/shard_map/add | solution.py:233
  102.9 9.5 %collective-permute-done.11 = bf16[4,256,176]{2,1,0:T(8,128)(2,1)S(1)} collective-permute-done((bf16[4,256,176]{2,1,0:T(8,128)(2,1)S(1)}, bf16[4,256,176]{2,1,0:T(8,128)(2,1)S(1)}, u32[]{:S(2)}, u32[]{:S(2)}) %collective-permute-start.11) | collective-permute-done | bytes 360480 | tf_op jit(solution)/shard_map/ppermute | solution.py:98
  112.6 6.9 %collective-permute-start.15 = (bf16[256,176]{0,1:T(8,128)(2,1)S(1)}, bf16[256,176]{0,1:T(8,128)(2,1)S(1)}, u32[]{:S(2)}, u32[]{:S(2)}) collective-permute-start(bf16[256,176]{0,1:T(8,128)(2,1)S(1)} %bitcast.52), channel_id=1, source_target_pairs={{0,20},{1,28},{2,22},{3,30},{4,16},{5,24},{6,18},{7,26},{8,21},{9,... | collective-permute-start | bytes 270344 | tf_op jit(solution)/shard_map/ppermute | solution.py:98
  119.7 1.7 %bitcast_dynamic-update-slice_fusion = f32[880,384]{1,0:T(8,128)} fusion(f32[880,384]{1,0:T(8,128)} %convert_dynamic-update-slice_fusion, f32[5,176,384]{2,1,0:T(8,128)} %fusion.2, s32[]{:T(128)S(6)} %select_n.117), kind=kLoop, calls=%fused_computation.26 | loop fusion | bytes 540676 | tf_op jit(solution)/shard_map/concatenate | solution.py:247
  121.7 2.7 %collective-permute-start.12 = (bf16[256,176]{0,1:T(8,128)(2,1)S(1)}, bf16[256,176]{0,1:T(8,128)(2,1)S(1)}, u32[]{:S(2)}, u32[]{:S(2)}) collective-permute-start(bf16[256,176]{0,1:T(8,128)(2,1)S(1)} %bitcast.55), channel_id=1, source_target_pairs={{0,0},{1,8},{2,2},{3,10},{4,4},{5,12},{6,6},{7,14},{8,1},{9,9},{10... | collective-permute-start | bytes 270344 | tf_op jit(solution)/shard_map/ppermute | solution.py:98
  124.9 2.5 %collective-permute-done.13 = bf16[256,176]{0,1:T(8,128)(2,1)S(1)} collective-permute-done((bf16[256,176]{0,1:T(8,128)(2,1)S(1)}, bf16[256,176]{0,1:T(8,128)(2,1)S(1)}, u32[]{:S(2)}, u32[]{:S(2)}) %collective-permute-start.13) | collective-permute-done | bytes 90144 | tf_op jit(solution)/shard_map/ppermute | solution.py:98
  (114 shorter events, 38.8 us)
Async XLA Ops:
  2.1 12.1 %collective-permute-start.19 = (bf16[256,176]{1,0:T(8,128)(2,1)S(1)}, bf16[256,176]{1,0:T(8,128)(2,1)S(1)}, u32[]{:S(2)}, u32[]{:S(2)}) collective-permute-start(bf16[256,176]{1,0:T(8,128)(2,1)S(1)} %get-tuple-element.21), channel_id=1, source_target_pairs={{0,20},{1,28},{2,22},{3,30},{4,16},{5,24},{6,18},{7,26},{8,21},{9,... | collective-permute-start | bytes 270344 | tf_op jit(solution)/shard_map/ppermute | solution.py:98
  7.8 12.6 %collective-permute-start.17 = (bf16[256,176]{1,0:T(8,128)(2,1)S(1)}, bf16[256,176]{1,0:T(8,128)(2,1)S(1)}, u32[]{:S(2)}, u32[]{:S(2)}) collective-permute-start(bf16[256,176]{1,0:T(8,128)(2,1)S(1)} %get-tuple-element.21), channel_id=1, source_target_pairs={{0,4},{1,12},{2,6},{3,14},{4,0},{5,8},{6,2},{7,10},{8,5},{9,13},{1... | collective-permute-start | bytes 270344 | tf_op jit(solution)/shard_map/ppermute | solution.py:98
  7.8 7.8 %collective-permute-start.18 = (bf16[256,176]{1,0:T(8,128)(2,1)S(1)}, bf16[256,176]{1,0:T(8,128)(2,1)S(1)}, u32[]{:S(2)}, u32[]{:S(2)}) collective-permute-start(bf16[256,176]{1,0:T(8,128)(2,1)S(1)} %get-tuple-element.20), channel_id=1, source_target_pairs={{0,16},{1,24},{2,18},{3,26},{4,20},{5,28},{6,22},{7,30},{8,17},{9,... | collective-permute-start | bytes 270344 | tf_op jit(solution)/shard_map/ppermute | solution.py:98
  8.4 13.7 %collective-permute-start.16 = (bf16[256,176]{1,0:T(8,128)(2,1)S(1)}, bf16[256,176]{1,0:T(8,128)(2,1)S(1)}, u32[]{:S(2)}, u32[]{:S(2)}) collective-permute-start(bf16[256,176]{1,0:T(8,128)(2,1)S(1)} %get-tuple-element.20), channel_id=1, source_target_pairs={{0,0},{1,8},{2,2},{3,10},{4,4},{5,12},{6,6},{7,14},{8,1},{9,9},{10... | collective-permute-start | bytes 270344 | tf_op jit(solution)/shard_map/ppermute | solution.py:98
  12.3 10.2 %collective-permute-start.7 = (bf16[176,384]{1,0:T(8,128)(2,1)S(1)}, bf16[176,384]{1,0:T(8,128)(2,1)S(1)}, u32[]{:S(2)}, u32[]{:S(2)}) collective-permute-start(bf16[176,384]{1,0:T(8,128)(2,1)S(1)} %get-tuple-element.13), channel_id=1, source_target_pairs={{0,4},{4,8},{8,12},{12,0},{16,20},{20,24},{24,28},{28,16},{1,5},{5... | collective-permute-start | bytes 405512 | tf_op jit(solution)/shard_map/ppermute | solution.py:102
  14.2 29.4 %collective-permute-start.1 = (bf16[256,384]{1,0:T(8,128)(2,1)S(1)}, bf16[256,384]{1,0:T(8,128)(2,1)S(1)}, u32[]{:S(2)}, u32[]{:S(2)}) collective-permute-start(bf16[256,384]{1,0:T(8,128)(2,1)S(1)} %fusion.14.refs_0_), channel_id=1, source_target_pairs={{0,8},{4,12},{8,16},{12,20},{16,24},{20,28},{24,0},{28,4},{1,9},{5... | collective-permute-start | bytes 589832 | tf_op jit(solution)/shard_map/ppermute | solution.py:102
  15.6 28.7 %collective-permute-start.3 = (bf16[256,384]{1,0:T(8,128)(2,1)S(1)}, bf16[256,384]{1,0:T(8,128)(2,1)S(1)}, u32[]{:S(2)}, u32[]{:S(2)}) collective-permute-start(bf16[256,384]{1,0:T(8,128)(2,1)S(1)} %fusion.14.refs_0_), channel_id=1, source_target_pairs={{0,16},{4,20},{8,24},{12,28},{16,0},{20,4},{24,8},{28,12},{1,17},{... | collective-permute-start | bytes 589832 | tf_op jit(solution)/shard_map/ppermute | solution.py:102
  20.4 26.0 %collective-permute-start.5 = (bf16[256,384]{1,0:T(8,128)(2,1)S(1)}, bf16[256,384]{1,0:T(8,128)(2,1)S(1)}, u32[]{:S(2)}, u32[]{:S(2)}) collective-permute-start(bf16[256,384]{1,0:T(8,128)(2,1)S(1)} %fusion.14.refs_0_), channel_id=1, source_target_pairs={{0,24},{4,28},{8,0},{12,4},{16,8},{20,12},{24,16},{28,20},{1,25},{... | collective-permute-start | bytes 589832 | tf_op jit(solution)/shard_map/ppermute | solution.py:102
  22.0 13.7 %collective-permute-start.8 = (bf16[176,384]{1,0:T(8,128)(2,1)S(1)}, bf16[176,384]{1,0:T(8,128)(2,1)S(1)}, u32[]{:S(2)}, u32[]{:S(2)}) collective-permute-start(bf16[176,384]{1,0:T(8,128)(2,1)S(1)} %get-tuple-element.12), channel_id=1, source_target_pairs={{0,8},{4,12},{8,0},{12,4},{16,24},{20,28},{24,16},{28,20},{1,9},{5... | collective-permute-start | bytes 405512 | tf_op jit(solution)/shard_map/ppermute | solution.py:102
  23.2 28.9 %collective-permute-start.20 = (bf16[4,256,176]{2,1,0:T(8,128)(2,1)S(1)}, bf16[4,256,176]{2,1,0:T(8,128)(2,1)S(1)}, u32[]{:S(2)}, u32[]{:S(2)}) collective-permute-start(bf16[4,256,176]{2,1,0:T(8,128)(2,1)S(1)} %pad_maximum_fusion.s00), channel_id=1, source_target_pairs={{0,2},{1,3},{2,0},{3,1},{4,6},{5,7},{6,4},{7,5},{8,10},{9,11},{10,... | collective-permute-start | bytes 1081352 | tf_op jit(solution)/shard_map/ppermute | solution.py:98
  41.8 5.4 %collective-permute-start = (bf16[256,384]{1,0:T(8,128)(2,1)S(1)}, bf16[256,384]{1,0:T(8,128)(2,1)S(1)}, u32[]{:S(2)}, u32[]{:S(2)}) collective-permute-start(bf16[256,384]{1,0:T(8,128)(2,1)S(1)} %fusion.14.refs_0_), channel_id=1, source_target_pairs={{0,4},{4,0},{8,12},{12,8},{16,20},{20,16},{24,28},{28,24},{1,5},{5... | collective-permute-start | bytes 589832 | tf_op jit(solution)/shard_map/ppermute | solution.py:102
  43.6 8.5 %collective-permute-start.2 = (bf16[256,384]{1,0:T(8,128)(2,1)S(1)}, bf16[256,384]{1,0:T(8,128)(2,1)S(1)}, u32[]{:S(2)}, u32[]{:S(2)}) collective-permute-start(bf16[256,384]{1,0:T(8,128)(2,1)S(1)} %collective-permute-done.1.refs_2_), channel_id=1, source_target_pairs={{0,4},{4,0},{8,12},{12,8},{16,20},{20,16},{24,28},{28,24},{1,5},{5... | collective-permute-start | bytes 589832 | tf_op jit(solution)/shard_map/ppermute | solution.py:102
  44.3 11.2 %collective-permute-start.4 = (bf16[256,384]{1,0:T(8,128)(2,1)S(1)}, bf16[256,384]{1,0:T(8,128)(2,1)S(1)}, u32[]{:S(2)}, u32[]{:S(2)}) collective-permute-start(bf16[256,384]{1,0:T(8,128)(2,1)S(1)} %collective-permute-done.3.refs_4_), channel_id=1, source_target_pairs={{0,4},{4,0},{8,12},{12,8},{16,20},{20,16},{24,28},{28,24},{1,5},{5... | collective-permute-start | bytes 589832 | tf_op jit(solution)/shard_map/ppermute | solution.py:102
  46.4 13.3 %collective-permute-start.6 = (bf16[256,384]{1,0:T(8,128)(2,1)S(1)}, bf16[256,384]{1,0:T(8,128)(2,1)S(1)}, u32[]{:S(2)}, u32[]{:S(2)}) collective-permute-start(bf16[256,384]{1,0:T(8,128)(2,1)S(1)} %collective-permute-done.5.refs_6_), channel_id=1, source_target_pairs={{0,4},{4,0},{8,12},{12,8},{16,20},{20,16},{24,28},{28,24},{1,5},{5... | collective-permute-start | bytes 589832 | tf_op jit(solution)/shard_map/ppermute | solution.py:102
  47.9 35.3 %collective-permute-start.21 = (bf16[4,256,176]{2,1,0:T(8,128)(2,1)S(1)}, bf16[4,256,176]{2,1,0:T(8,128)(2,1)}, u32[]{:S(2)}, u32[]{:S(2)}) collective-permute-start(bf16[4,256,176]{2,1,0:T(8,128)(2,1)S(1)} %pad_maximum_fusion.s00), channel_id=1, source_target_pairs={{0,1},{1,0},{2,3},{3,2},{4,5},{5,4},{6,7},{7,6},{8,9},{9,8},{10,11... | collective-permute-start | bytes 1081352 | tf_op jit(solution)/shard_map/ppermute | solution.py:98
  52.1 31.1 %collective-permute-start.22 = (bf16[4,256,176]{2,1,0:T(8,128)(2,1)S(1)}, bf16[4,256,176]{2,1,0:T(8,128)(2,1)}, u32[]{:S(2)}, u32[]{:S(2)}) collective-permute-start(bf16[4,256,176]{2,1,0:T(8,128)(2,1)S(1)} %collective-permute-done.20.s10), channel_id=1, source_target_pairs={{0,1},{1,0},{2,3},{3,2},{4,5},{5,4},{6,7},{7,6},{8,9},{9,8},{10,11... | collective-permute-start | bytes 1081352 | tf_op jit(solution)/shard_map/ppermute | solution.py:98
  80.8 15.6 %collective-permute-start.10 = (bf16[2,4,256,176]{2,3,1,0:T(8,128)(2,1)}, bf16[2,4,256,176]{2,3,1,0:T(8,128)(2,1)}, u32[]{:S(2)}, u32[]{:S(2)}) collective-permute-start(bf16[2,4,256,176]{2,3,1,0:T(8,128)(2,1)} %copy.10), channel_id=1, source_target_pairs={{0,1},{1,0},{2,3},{3,2},{4,5},{5,4},{6,7},{7,6},{8,9},{9,8},{10,11... | collective-permute-start | bytes 2162696 | tf_op jit(solution)/shard_map/ppermute | solution.py:98
  92.4 9.1 %collective-permute-start.24 = (bf16[176,384]{1,0:T(8,128)(2,1)S(1)}, bf16[176,384]{1,0:T(8,128)(2,1)S(1)}, u32[]{:S(2)}, u32[]{:S(2)}) collective-permute-start(bf16[176,384]{1,0:T(8,128)(2,1)S(1)} %get-tuple-element.7), channel_id=1, source_target_pairs={{0,8},{4,12},{8,0},{12,4},{16,24},{20,28},{24,16},{28,20},{1,9},{5... | collective-permute-start | bytes 405512 | tf_op jit(solution)/shard_map/ppermute | solution.py:102
  93.0 9.2 %collective-permute-start.25 = (bf16[176,384]{1,0:T(8,128)(2,1)S(1)}, bf16[176,384]{1,0:T(8,128)(2,1)S(1)}, u32[]{:S(2)}, u32[]{:S(2)}) collective-permute-start(bf16[176,384]{1,0:T(8,128)(2,1)S(1)} %get-tuple-element.6), channel_id=1, source_target_pairs={{0,4},{4,8},{8,12},{12,0},{16,20},{20,24},{24,28},{28,16},{1,5},{5... | collective-permute-start | bytes 405512 | tf_op jit(solution)/shard_map/ppermute | solution.py:102
  100.2 12.1 %collective-permute-start.11 = (bf16[4,256,176]{2,1,0:T(8,128)(2,1)S(1)}, bf16[4,256,176]{2,1,0:T(8,128)(2,1)S(1)}, u32[]{:S(2)}, u32[]{:S(2)}) collective-permute-start(bf16[4,256,176]{2,1,0:T(8,128)(2,1)S(1)} %fusion.6), channel_id=1, source_target_pairs={{0,2},{1,3},{2,0},{3,1},{4,6},{5,7},{6,4},{7,5},{8,10},{9,11},{10,... | collective-permute-start | bytes 1081352 | tf_op jit(solution)/shard_map/ppermute | solution.py:98
  112.6 11.8 %collective-permute-start.15 = (bf16[256,176]{0,1:T(8,128)(2,1)S(1)}, bf16[256,176]{0,1:T(8,128)(2,1)S(1)}, u32[]{:S(2)}, u32[]{:S(2)}) collective-permute-start(bf16[256,176]{0,1:T(8,128)(2,1)S(1)} %bitcast.52), channel_id=1, source_target_pairs={{0,20},{1,28},{2,22},{3,30},{4,16},{5,24},{6,18},{7,26},{8,21},{9,... | collective-permute-start | bytes 270344 | tf_op jit(solution)/shard_map/ppermute | solution.py:98
  119.7 5.2 %collective-permute-start.14 = (bf16[256,176]{0,1:T(8,128)(2,1)S(1)}, bf16[256,176]{0,1:T(8,128)(2,1)S(1)}, u32[]{:S(2)}, u32[]{:S(2)}) collective-permute-start(bf16[256,176]{0,1:T(8,128)(2,1)S(1)} %bitcast.53), channel_id=1, source_target_pairs={{0,4},{1,12},{2,6},{3,14},{4,0},{5,8},{6,2},{7,10},{8,5},{9,13},{1... | collective-permute-start | bytes 270344 | tf_op jit(solution)/shard_map/ppermute | solution.py:98
  121.5 5.9 %collective-permute-start.13 = (bf16[256,176]{0,1:T(8,128)(2,1)S(1)}, bf16[256,176]{0,1:T(8,128)(2,1)S(1)}, u32[]{:S(2)}, u32[]{:S(2)}) collective-permute-start(bf16[256,176]{0,1:T(8,128)(2,1)S(1)} %bitcast.54), channel_id=1, source_target_pairs={{0,16},{1,24},{2,18},{3,26},{4,20},{5,28},{6,22},{7,30},{8,17},{9,... | collective-permute-start | bytes 270344 | tf_op jit(solution)/shard_map/ppermute | solution.py:98
  121.7 6.6 %collective-permute-start.12 = (bf16[256,176]{0,1:T(8,128)(2,1)S(1)}, bf16[256,176]{0,1:T(8,128)(2,1)S(1)}, u32[]{:S(2)}, u32[]{:S(2)}) collective-permute-start(bf16[256,176]{0,1:T(8,128)(2,1)S(1)} %bitcast.55), channel_id=1, source_target_pairs={{0,0},{1,8},{2,2},{3,10},{4,4},{5,12},{6,6},{7,14},{8,1},{9,9},{10... | collective-permute-start | bytes 270344 | tf_op jit(solution)/shard_map/ppermute | solution.py:98
  (29 other events, 64.0 us)

commit v2 on v0

v2 whole, which is shorter than its diff:
```python
import functools
import math

import jax
import jax.numpy as jnp
from jax import lax
from jax.experimental import pallas as pl
from jax.experimental.pallas import tpu as pltpu
from jax.sharding import PartitionSpec as P

KERNEL = 5
SEQS = 1
F32 = jnp.float32
BF16 = jnp.bfloat16


def with_halo(shard, sides, width):
    for axis, dim in sides:
        size, length = (lax.axis_size(axis), shard.shape[dim])
        up = [(i, (i + 1) % size) for i in range(size - 1)]
        down = [(j, i) for i, j in up]
        last = lax.slice_in_dim(shard, length - width, length, axis=dim)
        first = lax.slice_in_dim(shard, 0, width, axis=dim)
        before = lax.ppermute(last, axis, up)
        after = lax.ppermute(first, axis, down)
        shard = jnp.concatenate([before, shard, after], axis=dim)
    return shard


def gelu_slope(value):
    cumul = 0.5 * (1.0 + lax.erf(value * 0.7071067811865476))
    dens = jnp.exp(-0.5 * value * value) * 0.3989422804014327
    return cumul + value * dens


def dz_block(pre_act, emb_grad):
    upward = jnp.repeat(emb_grad.astype(F32), 2, axis=0) * 0.5
    return (upward * gelu_slope(pre_act.astype(F32))).astype(BF16)


def shards_any(acts, pre_act, emb_grad, filters):
    rows = acts.shape[0]
    c_in = acts.shape[1]
    dz_grad = dz_block(pre_act, emb_grad)
    total_rows = rows * lax.axis_size("seq")
    length = total_rows // SEQS
    first = lax.axis_index("seq") * rows
    positions = first - 2 + jnp.arange(rows + 4, dtype=jnp.int32)
    inside = (jnp.floor_divide(positions, length) == first // length).astype(BF16)[:, None]
    scale_value = 1.0 / math.sqrt(total_rows)
    grad_rim = with_halo(dz_grad, (("seq", 0),), 2) * inside
    whole_term = (
        jnp.concatenate(
            [
                jnp.einsum(
                    "rc,ro->co",
                    acts,
                    grad_rim[4 - k : 4 - k + rows],
                    preferred_element_type=F32,
                )
                for k in range(KERNEL)
            ],
            axis=0,
        )
        * scale_value
    )
    piece = lax.all_gather(filters, "seq", axis=0, tiled=True)
    width = piece.shape[0]
    product = jnp.einsum("ro,no->rn", grad_rim, piece, preferred_element_type=F32)
    tap_of = jnp.arange(width, dtype=jnp.int32) // c_in
    total = jnp.zeros((rows, width), F32)
    for k in range(KERNEL):
        total = total + jnp.where((tap_of == k)[None, :], product[4 - k : 4 - k + rows], 0.0)
    partial_input = total.reshape(rows, KERNEL, c_in).sum(axis=1)
    input_grad = lax.psum_scatter(partial_input, "section", scatter_dimension=1, tiled=True).astype(BF16)
    filter_grad = lax.psum_scatter(whole_term, "seq", scatter_dimension=0, tiled=True)
    return (input_grad, filter_grad)


TAPS = (((0, 0), (0, 1), (1, 0), (1, 1), (2, 0)), ((2, 0), (3, 1), (3, 0), (4, 1), (4, 0)))


def coords():
    i, j = lax.axis_index("seq"), lax.axis_index("section")
    return i // 4, (i // 2) % 2, i % 2, j // 2, j % 2


def send(value, place):
    pairs = []
    for g in range(32):
        h, zl, y, x, c = (g >> 4) & 1, (g >> 3) & 1, (g >> 2) & 1, (g >> 1) & 1, g & 1
        h, zl, y, x, c = place(h, zl, y, x, c)
        pairs.append((g, h * 16 + zl * 8 + y * 4 + x * 2 + c))
    return lax.ppermute(value, ("seq", "section"), pairs)


def in_half(value, step):
    return lax.ppermute(value, "seq", [(i, 4 * (i // 4) + (i % 4 + step) % 4) for i in range(8)])


SWAP_H = lambda h, zl, y, x, c: (1 - h, zl, y, x, c)
SWAP_Z = lambda h, zl, y, x, c: (h, 1 - zl, y, x, c)
SWAP_Y = lambda h, zl, y, x, c: (h, zl, 1 - y, x, c)
SWAP_X = lambda h, zl, y, x, c: (h, zl, y, 1 - x, c)
SWAP_C = lambda h, zl, y, x, c: (h, zl, y, x, 1 - c)


def turn(a, b):
    return lambda h, zl, y, x, c: (h ^ a, c, y ^ b, x, zl)


def dz_kernel(pre_ref, emb_ref, out_ref):
    rows, half = pre_ref.shape[0], emb_ref.shape[0]
    row = lax.broadcasted_iota(jnp.int32, (rows, half), 0)
    pair = lax.broadcasted_iota(jnp.int32, (rows, half), 1)
    twice = (row // 2 == pair).astype(BF16)
    up = jnp.dot(twice, emb_ref[...], preferred_element_type=F32) * 0.5
    out_ref[...] = (up * gelu_slope(pre_ref[...].astype(F32))).astype(BF16)


def units_kernel(unit, filters_ref, *out_refs):
    for m, ref in enumerate(out_refs):
        ref[...] = filters_ref[m * unit : (m + 1) * unit, :]


def cut_kernel(unit, acts_ref, *out_refs):
    _, _, y, x, c = coords()
    for j in range(4):

        @pl.when(2 * x + c == j)
        def _():
            for s in range(2):
                first = (2 * j + s) * unit
                value = acts_ref[:, first : first + unit].astype(F32).T.astype(BF16)
                for b, ref in enumerate(out_refs):

                    @pl.when(y ^ b == s)
                    def _():
                        ref[...] = value


def join_kernel(*refs):
    for n, ref in enumerate(refs[:-1]):
        refs[-1][n] = ref[...]


def input_kernel(rows, unit, *refs):
    dz_refs, w_refs, (keep_ref, away_ref, dz_ref) = refs[:8], refs[8:13], refs[13:16]
    weights, runs, arrived = refs[16:]
    h, zl, y, _, c = coords()
    q = 2 * zl + y
    copies = []
    for s in range(8):
        block = 4 * (h ^ (s // 4)) + 2 * (zl ^ ((s // 2) % 2)) + (y ^ (s % 2))
        there = dz_ref.at[pl.ds(pl.multiple_of(block * rows, rows), rows), :]
        copies.append(pltpu.make_async_copy(dz_refs[s], there, arrived.at[s]))
    for m in range(5):
        there = weights.at[pl.ds(pl.multiple_of(lax.rem(q + 5 - m, 5) * unit, 16), unit), :]
        copies.append(pltpu.make_async_copy(w_refs[m], there, arrived.at[8 + m]))
    for copy in copies:
        copy.start()
    for copy in copies:
        copy.wait()

    long = 2 * rows
    for r in range(4):
        run = runs.at[2 * (r // 2) + ((r % 2) ^ c)]
        lines = slice(max(r * long - 8, 0), min((r + 1) * long + 8, 4 * long))
        value = dz_ref[lines, :].astype(F32)
        if r == 0:
            value = jnp.concatenate([jnp.zeros((8, value.shape[1]), F32), value], axis=0)
        if r == 3:
            value = jnp.concatenate([value, jnp.zeros((8, value.shape[1]), F32)], axis=0)
        run[...] = value

    for half in range(2):

        @pl.when(h == half)
        def _():
            for t in range(8):
                sums = [None, None]
                for tap in range(2 * half, 2 * half + 3):
                    first = 8 + (t % 2) * rows + 2 - tap
                    shifted = runs[t // 2, first : first + rows, :].astype(BF16)
                    slots = [v for v in range(5) if TAPS[half][v][0] == tap]
                    term = lax.dot_general(
                        weights[slots[0] * unit : (slots[-1] + 1) * unit, :],
                        shifted,
                        (((1,), (1,)), ((), ())),
                        preferred_element_type=F32,
                    )
                    for n, v in enumerate(slots):
                        which = TAPS[half][v][1]
                        one = term[n * unit : (n + 1) * unit]
                        sums[which] = one if sums[which] is None else sums[which] + one
                for which in range(2):
                    ref = away_ref if (t // 2) % 2 else keep_ref
                    ref[which ^ half, 2 * (t // 4) + t % 2] = sums[which].astype(ref.dtype)


def cores_kernel(keep_ref, came_ref, keep_out, away_out):
    x = coords()[3]
    keep_out[...] = keep_ref[x] + came_ref[x].astype(F32)
    away_out[...] = (keep_ref[1 - x] + came_ref[1 - x].astype(F32)).astype(BF16)


def owners_kernel(keep_ref, came_ref, *out_refs):
    h, _, y, _, _ = coords()
    for n, ref in enumerate(out_refs):
        block = 2 * (h ^ (n // 2)) + (y ^ (n % 2))
        ref[...] = (keep_ref[block] + came_ref[block].astype(F32)).astype(BF16)


def last_kernel(unit, *refs):
    y, out_ref = coords()[2], refs[4]
    for b in range(2):
        first = pl.multiple_of((y ^ b) * unit, 16)
        out_ref[pl.ds(first, unit), :] = (refs[b][...].astype(F32) + refs[2 + b][...].astype(F32)).astype(BF16)


def left_kernel(rows, unit, s00, s10, s01, s11, out_ref, lines):
    h, _, y, x, c = coords()
    for xr, cr, ref in ((0, 0, s00), (1, 0, s10), (0, 1, s01), (1, 1, s11)):
        which = x ^ xr ^ h
        for a in range(2):
            for b in range(2):
                block = 4 * (h ^ a) + 2 * (c ^ cr) + (y ^ b)
                lines[which, :, pl.ds(pl.multiple_of(block * rows, rows), rows)] = ref[2 * a + b].astype(F32)
    total = 8 * rows
    place = lax.broadcasted_iota(jnp.int32, (unit, total), 1)
    for half in range(2):

        @pl.when(h == half)
        def _():
            for v, (tap, which) in enumerate(TAPS[half]):
                line = lines[which]
                if tap != 2:
                    line = pltpu.roll(line, (2 - tap) % total, 1)
                    fits = (place + (tap - 2) >= 0) & (place + (tap - 2) < total)
                    line = jnp.where(fits, line, 0.0)
                out_ref[v] = line.astype(BF16)


def filter_kernel(scale, left_ref, dz_ref, first_ref, s1_ref, s2_ref, s3_ref, last_ref):
    _, zl, y, _, _ = coords()
    for m, ref in enumerate((first_ref, s1_ref, s2_ref, s3_ref, last_ref)):
        slot = lax.rem(2 * zl + y + 5 - m, 5)
        grad = jnp.dot(left_ref[slot], dz_ref[...], preferred_element_type=F32) * scale
        ref[...] = grad.astype(ref.dtype)


def home_kernel(unit, first_ref, s1_ref, s2_ref, s3_ref, last_ref, out_ref):
    for m, ref in enumerate((first_ref, s1_ref, s2_ref, s3_ref, last_ref)):
        out_ref[m * unit : (m + 1) * unit, :] = ref[...].astype(F32)


def call(kernel, name, shapes, args, scratch=(), flops=0, mib=16, anywhere=False):
    many = isinstance(shapes, tuple)
    spec = pl.BlockSpec(memory_space=pltpu.VMEM)
    nbytes = sum(a.size * a.dtype.itemsize for a in args + (shapes if many else (shapes,)))
    return pl.pallas_call(
        kernel,
        out_shape=shapes,
        in_specs=[pl.BlockSpec(memory_space=pl.ANY) if anywhere else spec] * len(args),
        out_specs=(spec,) * len(shapes) if many else spec,
        scratch_shapes=list(scratch),
        compiler_params=pltpu.CompilerParams(vmem_limit_bytes=mib << 20),
        cost_estimate=pl.CostEstimate(flops=flops, bytes_accessed=nbytes, transcendentals=0),
        name=name,
    )(*args)


def shards_block(acts, pre_act, emb_grad, filters):
    rows, c_in = acts.shape
    wide = filters.shape[1]
    unit = c_in // 8
    total = 8 * rows
    flops = 2 * total * 5 * unit * wide
    shape = jax.ShapeDtypeStruct
    block, weight, pos = shape((rows, wide), BF16), shape((unit, wide), BF16), shape((unit, rows), BF16)

    tie = lax.optimization_barrier
    dz = call(dz_kernel, "dz", block, (pre_act, emb_grad), mib=8)
    own0, own1 = call(functools.partial(cut_kernel, unit), "cut", (pos, pos), (acts,), mib=8)
    dz_h, dz_z, dz_y = send(dz, SWAP_H), send(dz, SWAP_Z), send(dz, SWAP_Y)
    t11, t01 = send(own1, turn(1, 1)), send(own1, turn(0, 1))

    dz_h, dz_z, dz_y, t11, t01, own0, filters = tie((dz_h, dz_z, dz_y, t11, t01, own0, filters))
    dz_hz, dz_zy, dz_hy = send(dz_h, SWAP_Z), send(dz_z, SWAP_Y), send(dz_h, SWAP_Y)
    t10, t00 = send(own0, turn(1, 0)), send(own0, turn(0, 0))
    units = call(functools.partial(units_kernel, unit), "units", (weight,) * 5, (filters,), mib=4)

    dz_hz, dz_zy, dz_hy, t10, t00, *units = tie((dz_hz, dz_zy, dz_hy, t10, t00, *units))
    dz_hzy = send(dz_hz, SWAP_Y)
    weights = tuple(in_half(w, m) if m in (1, 2, 3) else w for m, w in enumerate(units))
    got = call(join_kernel, "join", shape((4, unit, rows), BF16), (t00, t01, t10, t11), mib=4)
    other = send(got, SWAP_X)

    dz_hzy, other, *weights = tie((dz_hzy, other, *weights))
    far, far_other = send(got, SWAP_C), send(other, SWAP_C)
    left = call(
        functools.partial(left_kernel, rows, unit),
        "left",
        shape((5, unit, total), BF16),
        (got, other, far, far_other),
        scratch=[pltpu.VMEM((2, unit, total), F32)],
    )
    blocks = (dz, dz_y, dz_z, dz_zy, dz_h, dz_hy, dz_hz, dz_hzy)

    keep, away, dz_all = call(
        functools.partial(input_kernel, rows, unit),
        "input",
        (shape((2, 4, unit, rows), F32), shape((2, 4, unit, rows), BF16), shape((total, wide), BF16)),
        blocks + tuple(weights),
        scratch=[
            pltpu.VMEM((5 * unit, wide), BF16),
            pltpu.VMEM((4, 2 * rows + 16, wide), F32),
            pltpu.SemaphoreType.DMA((13,)),
        ],
        flops=flops,
        anywhere=True,
    )

    keep, away = call(
        cores_kernel,
        "cores",
        (shape((4, unit, rows), F32), shape((4, unit, rows), BF16)),
        (keep, send(away, SWAP_C)),
    )
    ready = call(owners_kernel, "owners", (pos,) * 4, (keep, send(away, SWAP_X)))
    came = tuple(send(r, turn(n // 2, n % 2)) for n, r in enumerate(ready))
    input_grad = call(functools.partial(last_kernel, unit), "last", shape((2 * unit, rows), BF16), came, mib=4).T

    grads = call(
        functools.partial(filter_kernel, 1.0 / math.sqrt(total)),
        "filter",
        tuple(shape((unit, wide), F32 if m in (0, 4) else BF16) for m in range(5)),
        (left, dz_all),
        flops=flops,
    )
    grads = tuple(in_half(grad, -m) if m in (1, 2, 3) else grad for m, grad in enumerate(grads))
    filter_grad = call(functools.partial(home_kernel, unit), "home", shape((5 * unit, wide), F32), grads, mib=8)
    return input_grad, filter_grad


def solution(mesh):
    in_specs = (P("seq", None), P("seq", "section"), P("seq", "section"), P("seq", "section"))
    out_specs = (P("seq", "section"), P("seq", "section"))
    block = mesh.shape["seq"] == 8 and mesh.shape["section"] == 4
    body = shards_block if block else shards_any
    return jax.shard_map(body, mesh=mesh, in_specs=in_specs, out_specs=out_specs, check_vma=False)
```

time: 346 us -> 79 us (0.23)
  waiting for transfers between devices: 266 us -> 30.4 us
  starting transfers between devices: 5.38 us -> 31.7 us
  other arithmetic: 24.1 us -> 0 us
  local copies, waits for them, and re-layouts: 21.1 us -> 4.01 us
  matrix products: 14.3 us -> 0 us
  between operations: 13.9 us -> 0.76 us
  Pallas kernels: 0 us -> 11.9 us
    unnamed x4 -> x0, waiting for transfers between devices: 186 us -> none
    all_gather x1 -> x0, waiting for transfers between devices: 76.9 us -> none  [shards(): piece = lax.all_gather(filters, 'seq', axis=0, tiled=True)]
    ppermute x2 -> x26, waiting for transfers between devices: 2.91 us -> 30.4 us  [the longest x20 20.8 us: send(): return lax.ppermute(value, ('seq', 'section'), pairs)]
    ppermute x2 -> x26, starting transfers between devices: 5.27 us -> 31.7 us  [the longest x20 27.5 us: send(): return lax.ppermute(value, ('seq', 'section'), pairs)]
    dot_general x6 -> x0, matrix products: 14.3 us -> none  [the longest x5 9.63 us: shards(): jnp.einsum('rc,ro->co', acts, grad_rim[4 - k:4 - k + rows], preferred_ele...]
    pallas_call x0 -> x11, Pallas kernels: none -> 11.9 us  [call(): pl.pallas_call(kernel, out_shape=shapes, in_specs=[pl.BlockSpec(memory_sp...]
    mul x3 -> x0, other arithmetic: 10.4 us -> none  [the longest x1 9.42 us: shards(): jnp.concatenate([jnp.einsum('rc,ro->co', acts, grad_rim[4 - k:4 - k + row...]
    add x1 -> x0, local copies, waits for them, and re-layouts: 8.59 us -> none  [shards(): total + jnp.where((tap_of == k)[None, :], product[4 - k:4 - k + rows], 0.0)]
  transfers between devices with their start and end apart: 5 -> 26, of which waited for: 3 -> 10; matrix products, arithmetic and copies ran while one was open for 10% -> 0% of each run, Pallas kernels for 0% -> 7%
where the time goes in v2:
time: 79 us; the launch traced here: 78.8 us
  starting transfers between devices  31.7 us (40%)
  waiting for transfers between devices  30.4 us (38%)
  Pallas kernels  11.9 us (15%)
  local copies, waits for them, and re-layouts  4.01 us (5%)
    ppermute x20, starting transfers between devices, send(): return lax.ppermute(value, ('seq', 'section'), pairs)  27.5 us
    ppermute x20, waiting for transfers between devices, send(): return lax.ppermute(value, ('seq', 'section'), pairs)  20.8 us
    pallas_call x11, Pallas kernels, call(): pl.pallas_call(kernel, out_shape=shapes, in_specs=[pl.BlockSpec(memory_sp...  11.9 us
    ppermute x6, waiting for transfers between devices, in_half(): lax.ppermute(value, 'seq', [(i, 4 * (i // 4) + (i % 4 + step) % 4) for i...  9.55 us
    ppermute x6, starting transfers between devices, in_half(): lax.ppermute(value, 'seq', [(i, 4 * (i // 4) + (i % 4 + step) % 4) for i...  4.12 us
    unnamed x8, local copies, waits for them, and re-layouts  4.01 us
  transfers between devices with their start and end apart: 26, of which 10 were waited for; matrix products, arithmetic and copies ran while one was open for 0% of the time, Pallas kernels for 7%

profile of v2, /device:TPU:1, one launch (start us, length us, event | category | flops | bytes accessed | tf_op | source)
XLA Modules:
  0.0 78.8 jit_solution(15013103310563442743)
XLA Ops:
  2.7 3.2 %collective-permute-start = (bf16[256,384]{1,0:T(8,128)(2,1)S(1)}, bf16[256,384]{1,0:T(8,128)(2,1)S(1)}, u32[]{:S(2)}, u32[]{:S(2)}) collective-permute-start(bf16[256,384]{1,0:T(8,128)(2,1)S(1)} %dz.1.refs_0_), channel_id=1, source_target_pairs={{0,16},{1,17},{2,18},{3,19},{4,20},{5,21},{6,22},{7,23},{8,24},{9,... | collective-permute-start | bytes 589832 | tf_op jit(solution)/shard_map/ppermute | solution.py:94
  5.9 1.3 %collective-permute-start.1 = (bf16[256,384]{1,0:T(8,128)(2,1)S(1)}, bf16[256,384]{1,0:T(8,128)(2,1)S(1)}, u32[]{:S(2)}, u32[]{:S(2)}) collective-permute-start(bf16[256,384]{1,0:T(8,128)(2,1)S(1)} %dz.1.refs_0_), channel_id=1, source_target_pairs={{0,8},{1,9},{2,10},{3,11},{4,12},{5,13},{6,14},{7,15},{8,0},{9,1},... | collective-permute-start | bytes 589832 | tf_op jit(solution)/shard_map/ppermute | solution.py:94
  7.2 1.2 %collective-permute-start.2 = (bf16[256,384]{1,0:T(8,128)(2,1)S(1)}, bf16[256,384]{1,0:T(8,128)(2,1)S(1)}, u32[]{:S(2)}, u32[]{:S(2)}) collective-permute-start(bf16[256,384]{1,0:T(8,128)(2,1)S(1)} %dz.1.refs_0_), channel_id=1, source_target_pairs={{0,4},{1,5},{2,6},{3,7},{4,0},{5,1},{6,2},{7,3},{8,12},{9,13},{10,... | collective-permute-start | bytes 589832 | tf_op jit(solution)/shard_map/ppermute | solution.py:94
  11.6 7.8 %collective-permute-done.3.refs_3_ = bf16[176,256]{1,0:T(8,128)(2,1)S(1)} collective-permute-done((bf16[176,256]{1,0:T(8,128)(2,1)S(1)}, bf16[176,256]{1,0:T(8,128)(2,1)S(1)}, u32[]{:S(2)}, u32[]{:S(2)}) %collective-permute-start.3) | collective-permute-done | bytes 90144 | tf_op jit(solution)/shard_map/ppermute | solution.py:94
  20.1 1.2 %collective-permute-start.6 = (bf16[256,384]{1,0:T(8,128)(2,1)S(1)}, bf16[256,384]{1,0:T(8,128)(2,1)S(1)}, u32[]{:S(2)}, u32[]{:S(2)}) collective-permute-start(bf16[256,384]{1,0:T(8,128)(2,1)S(1)} %collective-permute-done.1.refs_2_), channel_id=1, source_target_pairs={{0,4},{1,5},{2,6},{3,7},{4,0},{5,1},{6,2},{7,3},{8,12},{9,13},{10,... | collective-permute-start | bytes 589832 | tf_op jit(solution)/shard_map/ppermute | solution.py:94
  21.6 4.5 %collective-permute-start.8 = (bf16[176,256]{1,0:T(8,128)(2,1)S(1)}, bf16[176,256]{1,0:T(8,128)(2,1)S(1)}, u32[]{:S(2)}, u32[]{:S(2)}) collective-permute-start(bf16[176,256]{1,0:T(8,128)(2,1)S(1)} %get-tuple-element.52), channel_id=1, source_target_pairs={{0,16},{1,24},{2,18},{3,26},{4,20},{5,28},{6,22},{7,30},{8,17},{9,... | collective-permute-start | bytes 270344 | tf_op jit(solution)/shard_map/ppermute | solution.py:94
  26.1 1.9 %collective-permute-start.9 = (bf16[176,256]{1,0:T(8,128)(2,1)S(1)}, bf16[176,256]{1,0:T(8,128)(2,1)S(1)}, u32[]{:S(2)}, u32[]{:S(2)}) collective-permute-start(bf16[176,256]{1,0:T(8,128)(2,1)S(1)} %get-tuple-element.52), channel_id=1, source_target_pairs={{0,0},{1,8},{2,2},{3,10},{4,4},{5,12},{6,6},{7,14},{8,1},{9,9},{10... | collective-permute-start | bytes 270344 | tf_op jit(solution)/shard_map/ppermute | solution.py:94
  29.2 1.9 %collective-permute-done.8.refs_2_ = bf16[176,256]{1,0:T(8,128)(2,1)S(1)} collective-permute-done((bf16[176,256]{1,0:T(8,128)(2,1)S(1)}, bf16[176,256]{1,0:T(8,128)(2,1)S(1)}, u32[]{:S(2)}, u32[]{:S(2)}) %collective-permute-start.8) | collective-permute-done | bytes 90144 | tf_op jit(solution)/shard_map/ppermute | solution.py:94
  32.1 1.3 %collective-permute-start.11 = (bf16[4,176,256]{2,1,0:T(8,128)(2,1)S(1)}, bf16[4,176,256]{2,1,0:T(8,128)(2,1)S(1)}, u32[]{:S(2)}, u32[]{:S(2)}) collective-permute-start(bf16[4,176,256]{2,1,0:T(8,128)(2,1)S(1)} %join.1.s00), channel_id=1, source_target_pairs={{0,2},{1,3},{2,0},{3,1},{4,6},{5,7},{6,4},{7,5},{8,10},{9,11},{10,... | collective-permute-start | bytes 1081352 | tf_op jit(solution)/shard_map/ppermute | solution.py:94
  34.8 1.4 %collective-permute-start.14 = (bf16[176,384]{1,0:T(8,128)(2,1)S(1)}, bf16[176,384]{1,0:T(8,128)(2,1)S(1)}, u32[]{:S(2)}, u32[]{:S(2)}) collective-permute-start(bf16[176,384]{1,0:T(8,128)(2,1)S(1)} %get-tuple-element.69), channel_id=1, source_target_pairs={{0,12},{4,0},{8,4},{12,8},{16,28},{20,16},{24,20},{28,24},{1,13},{... | collective-permute-start | bytes 405512 | tf_op jit(solution)/shard_map/ppermute | solution.py:98
  36.2 6.9 %collective-permute-done.12.refs_9_ = bf16[176,384]{1,0:T(8,128)(2,1)S(1)} collective-permute-done((bf16[176,384]{1,0:T(8,128)(2,1)S(1)}, bf16[176,384]{1,0:T(8,128)(2,1)S(1)}, u32[]{:S(2)}, u32[]{:S(2)}) %collective-permute-start.12) | collective-permute-done | bytes 135200 | tf_op jit(solution)/shard_map/ppermute | solution.py:98
  43.1 2.7 %collective-permute-done.14.refs_11_ = bf16[176,384]{1,0:T(8,128)(2,1)S(1)} collective-permute-done((bf16[176,384]{1,0:T(8,128)(2,1)S(1)}, bf16[176,384]{1,0:T(8,128)(2,1)S(1)}, u32[]{:S(2)}, u32[]{:S(2)}) %collective-permute-start.14) | collective-permute-done | bytes 135200 | tf_op jit(solution)/shard_map/ppermute | solution.py:98
  45.7 5.8 %input.1 = (f32[2,4,176,256]{3,2,1,0:T(8,128)S(1)}, bf16[2,4,176,256]{3,2,1,0:T(8,128)(2,1)S(1)}, bf16[2048,384]{1,0:T(8,128)(2,1)S(1)}) custom-call(bf16[256,384]{1,0:T(8,128)(2,1)S(1)} %dz.1.refs_0_, bf16[256,384]{1,0:T(8,128)(2,1)S(1)} %collective-permute-done.2.refs_1_, bf16[256,384]{1,0:T(8,128)(2,1)S(1)} %collective-permute-done.1.refs_2_, ...), custom_call_target="tpu_custom_call" | custom-call | flops 1384120320 | bytes 5984256 | tf_op jit(solution)/shard_map/input/pallas_call | solution.py:261
  52.8 1.3 %collective-permute-done.15.came_ref = bf16[2,4,176,256]{3,2,1,0:T(8,128)(2,1)S(1)} collective-permute-done((bf16[2,4,176,256]{3,2,1,0:T(8,128)(2,1)S(1)}, bf16[2,4,176,256]{3,2,1,0:T(8,128)(2,1)S(1)}, u32[]{:S(2)}, u32[]{:S(2)}) %collective-permute-start.15) | collective-permute-done | bytes 720928 | tf_op jit(solution)/shard_map/ppermute | solution.py:94
  55.2 1.2 %left.1.left_ref = bf16[5,176,2048]{2,1,0:T(8,128)(2,1)S(1)} custom-call(bf16[4,176,256]{2,1,0:T(8,128)(2,1)S(1)} %join.1.s00, bf16[4,176,256]{2,1,0:T(8,128)(2,1)S(1)} %collective-permute-done.11.s10, bf16[4,176,256]{2,1,0:T(8,128)(2,1)S(1)} %collective-permute-done.21.s01, bf16[4,176,256]{2,1,0:T(8,128)(2,1)S(1)} %collective-permute-done.22.s11), custom_call_target="tpu_custom_call" | custom-call | bytes 5046272 | tf_op jit(solution)/shard_map/left/pallas_call | solution.py:261
  56.3 2.1 %filter.1 = (f32[176,384]{1,0:T(8,128)S(1)}, bf16[176,384]{1,0:T(8,128)(2,1)S(1)}, bf16[176,384]{1,0:T(8,128)(2,1)S(1)}, bf16[176,384]{1,0:T(8,128)(2,1)S(1)}, f32[176,384]{1,0:T(8,128)S(1)}) custom-call(bf16[5,176,2048]{2,1,0:T(8,128)(2,1)S(1)} %left.1.left_ref, bf16[2048,384]{1,0:T(8,128)(2,1)S(1)} %get-tuple-element.86.dz_ref), custom_call_target="tpu_custom_call" | custom-call | flops 1384120320 | bytes 6123520 | tf_op jit(solution)/shard_map/filter/pallas_call | solution.py:261
  58.5 1.7 %collective-permute-start.24 = (bf16[176,384]{1,0:T(8,128)(2,1)S(1)}, bf16[176,384]{1,0:T(8,128)(2,1)S(1)}, u32[]{:S(2)}, u32[]{:S(2)}) collective-permute-start(bf16[176,384]{1,0:T(8,128)(2,1)S(1)} %get-tuple-element.89), channel_id=1, source_target_pairs={{0,8},{4,12},{8,0},{12,4},{16,24},{20,28},{24,16},{28,20},{1,9},{5... | collective-permute-start | bytes 405512 | tf_op jit(solution)/shard_map/ppermute | solution.py:98
  60.2 3.8 %collective-permute-done.16.came_ref = bf16[4,176,256]{2,1,0:T(8,128)(2,1)S(1)} collective-permute-done((bf16[4,176,256]{2,1,0:T(8,128)(2,1)S(1)}, bf16[4,176,256]{2,1,0:T(8,128)(2,1)S(1)}, u32[]{:S(2)}, u32[]{:S(2)}) %collective-permute-start.16) | collective-permute-done | bytes 360480 | tf_op jit(solution)/shard_map/ppermute | solution.py:94
  64.1 2.1 %collective-permute-start.17 = (bf16[176,256]{1,0:T(8,128)(2,1)S(1)}, bf16[176,256]{1,0:T(8,128)(2,1)S(1)}, u32[]{:S(2)}, u32[]{:S(2)}) collective-permute-start(bf16[176,256]{1,0:T(8,128)(2,1)S(1)} %get-tuple-element.81), channel_id=1, source_target_pairs={{0,0},{1,8},{2,2},{3,10},{4,4},{5,12},{6,6},{7,14},{8,1},{9,9},{10... | collective-permute-start | bytes 270344 | tf_op jit(solution)/shard_map/ppermute | solution.py:94
  66.2 1.9 %collective-permute-start.18 = (bf16[176,256]{1,0:T(8,128)(2,1)S(1)}, bf16[176,256]{1,0:T(8,128)(2,1)S(1)}, u32[]{:S(2)}, u32[]{:S(2)}) collective-permute-start(bf16[176,256]{1,0:T(8,128)(2,1)S(1)} %get-tuple-element.82), channel_id=1, source_target_pairs={{0,4},{1,12},{2,6},{3,14},{4,0},{5,8},{6,2},{7,10},{8,5},{9,13},{1... | collective-permute-start | bytes 270344 | tf_op jit(solution)/shard_map/ppermute | solution.py:94
  68.0 3.3 %collective-permute-start.19 = (bf16[176,256]{1,0:T(8,128)(2,1)S(1)}, bf16[176,256]{1,0:T(8,128)(2,1)S(1)}, u32[]{:S(2)}, u32[]{:S(2)}) collective-permute-start(bf16[176,256]{1,0:T(8,128)(2,1)S(1)} %get-tuple-element.83), channel_id=1, source_target_pairs={{0,16},{1,24},{2,18},{3,26},{4,20},{5,28},{6,22},{7,30},{8,17},{9,... | collective-permute-start | bytes 270344 | tf_op jit(solution)/shard_map/ppermute | solution.py:94
  72.4 1.2 %home.1 = f32[880,384]{1,0:T(8,128)} custom-call(f32[176,384]{1,0:T(8,128)S(1)} %get-tuple-element.87.first_ref, bf16[176,384]{1,0:T(8,128)(2,1)S(1)} %collective-permute-done.23.s1_ref, bf16[176,384]{1,0:T(8,128)(2,1)S(1)} %collective-permute-done.24.s2_ref, bf16[176,384]{1,0:T(8,128)(2,1)S(1)} %collective-permute-done.25.s3_ref, ...), custom_call_target="tpu_custom_call" | custom-call | bytes 2297856 | tf_op jit(solution)/shard_map/home/pallas_call | solution.py:261
  73.5 1.9 %collective-permute-done.19.refs_2_ = bf16[176,256]{1,0:T(8,128)(2,1)S(1)} collective-permute-done((bf16[176,256]{1,0:T(8,128)(2,1)S(1)}, bf16[176,256]{1,0:T(8,128)(2,1)S(1)}, u32[]{:S(2)}, u32[]{:S(2)}) %collective-permute-start.19) | collective-permute-done | bytes 90144 | tf_op jit(solution)/shard_map/ppermute | solution.py:94
  75.4 2.6 %collective-permute-done.20.refs_3_ = bf16[176,256]{1,0:T(8,128)(2,1)S(1)} collective-permute-done((bf16[176,256]{1,0:T(8,128)(2,1)S(1)}, bf16[176,256]{1,0:T(8,128)(2,1)S(1)}, u32[]{:S(2)}, u32[]{:S(2)}) %collective-permute-start.20) | collective-permute-done | bytes 90144 | tf_op jit(solution)/shard_map/ppermute | solution.py:94
  (47 shorter events, 13.9 us)
Async XLA Ops:
  2.7 16.7 %collective-permute-start = (bf16[256,384]{1,0:T(8,128)(2,1)S(1)}, bf16[256,384]{1,0:T(8,128)(2,1)S(1)}, u32[]{:S(2)}, u32[]{:S(2)}) collective-permute-start(bf16[256,384]{1,0:T(8,128)(2,1)S(1)} %dz.1.refs_0_), channel_id=1, source_target_pairs={{0,16},{1,17},{2,18},{3,19},{4,20},{5,21},{6,22},{7,23},{8,24},{9,... | collective-permute-start | bytes 589832 | tf_op jit(solution)/shard_map/ppermute | solution.py:94
  5.9 13.5 %collective-permute-start.1 = (bf16[256,384]{1,0:T(8,128)(2,1)S(1)}, bf16[256,384]{1,0:T(8,128)(2,1)S(1)}, u32[]{:S(2)}, u32[]{:S(2)}) collective-permute-start(bf16[256,384]{1,0:T(8,128)(2,1)S(1)} %dz.1.refs_0_), channel_id=1, source_target_pairs={{0,8},{1,9},{2,10},{3,11},{4,12},{5,13},{6,14},{7,15},{8,0},{9,1},... | collective-permute-start | bytes 589832 | tf_op jit(solution)/shard_map/ppermute | solution.py:94
  7.2 12.2 %collective-permute-start.2 = (bf16[256,384]{1,0:T(8,128)(2,1)S(1)}, bf16[256,384]{1,0:T(8,128)(2,1)S(1)}, u32[]{:S(2)}, u32[]{:S(2)}) collective-permute-start(bf16[256,384]{1,0:T(8,128)(2,1)S(1)} %dz.1.refs_0_), channel_id=1, source_target_pairs={{0,4},{1,5},{2,6},{3,7},{4,0},{5,1},{6,2},{7,3},{8,12},{9,13},{10,... | collective-permute-start | bytes 589832 | tf_op jit(solution)/shard_map/ppermute | solution.py:94
  10.0 9.4 %collective-permute-start.3 = (bf16[176,256]{1,0:T(8,128)(2,1)S(1)}, bf16[176,256]{1,0:T(8,128)(2,1)S(1)}, u32[]{:S(2)}, u32[]{:S(2)}) collective-permute-start(bf16[176,256]{1,0:T(8,128)(2,1)S(1)} %get-tuple-element.47), channel_id=1, source_target_pairs={{0,20},{1,28},{2,22},{3,30},{4,16},{5,24},{6,18},{7,26},{8,21},{9,... | collective-permute-start | bytes 270344 | tf_op jit(solution)/shard_map/ppermute | solution.py:94
  11.0 8.4 %collective-permute-start.4 = (bf16[176,256]{1,0:T(8,128)(2,1)S(1)}, bf16[176,256]{1,0:T(8,128)(2,1)S(1)}, u32[]{:S(2)}, u32[]{:S(2)}) collective-permute-start(bf16[176,256]{1,0:T(8,128)(2,1)S(1)} %get-tuple-element.47), channel_id=1, source_target_pairs={{0,4},{1,12},{2,6},{3,14},{4,0},{5,8},{6,2},{7,10},{8,5},{9,13},{1... | collective-permute-start | bytes 270344 | tf_op jit(solution)/shard_map/ppermute | solution.py:94
  19.4 12.6 %collective-permute-start.5 = (bf16[256,384]{1,0:T(8,128)(2,1)S(1)}, bf16[256,384]{1,0:T(8,128)(2,1)S(1)}, u32[]{:S(2)}, u32[]{:S(2)}) collective-permute-start(bf16[256,384]{1,0:T(8,128)(2,1)S(1)} %collective-permute-done.refs_4_), channel_id=1, source_target_pairs={{0,8},{1,9},{2,10},{3,11},{4,12},{5,13},{6,14},{7,15},{8,0},{9,1},... | collective-permute-start | bytes 589832 | tf_op jit(solution)/shard_map/ppermute | solution.py:94
  20.1 11.9 %collective-permute-start.6 = (bf16[256,384]{1,0:T(8,128)(2,1)S(1)}, bf16[256,384]{1,0:T(8,128)(2,1)S(1)}, u32[]{:S(2)}, u32[]{:S(2)}) collective-permute-start(bf16[256,384]{1,0:T(8,128)(2,1)S(1)} %collective-permute-done.1.refs_2_), channel_id=1, source_target_pairs={{0,4},{1,5},{2,6},{3,7},{4,0},{5,1},{6,2},{7,3},{8,12},{9,13},{10,... | collective-permute-start | bytes 589832 | tf_op jit(solution)/shard_map/ppermute | solution.py:94
  21.4 10.7 %collective-permute-start.7 = (bf16[256,384]{1,0:T(8,128)(2,1)S(1)}, bf16[256,384]{1,0:T(8,128)(2,1)S(1)}, u32[]{:S(2)}, u32[]{:S(2)}) collective-permute-start(bf16[256,384]{1,0:T(8,128)(2,1)S(1)} %collective-permute-done.refs_4_), channel_id=1, source_target_pairs={{0,4},{1,5},{2,6},{3,7},{4,0},{5,1},{6,2},{7,3},{8,12},{9,13},{10,... | collective-permute-start | bytes 589832 | tf_op jit(solution)/shard_map/ppermute | solution.py:94
  21.6 9.5 %collective-permute-start.8 = (bf16[176,256]{1,0:T(8,128)(2,1)S(1)}, bf16[176,256]{1,0:T(8,128)(2,1)S(1)}, u32[]{:S(2)}, u32[]{:S(2)}) collective-permute-start(bf16[176,256]{1,0:T(8,128)(2,1)S(1)} %get-tuple-element.52), channel_id=1, source_target_pairs={{0,16},{1,24},{2,18},{3,26},{4,20},{5,28},{6,22},{7,30},{8,17},{9,... | collective-permute-start | bytes 270344 | tf_op jit(solution)/shard_map/ppermute | solution.py:94
  26.1 5.9 %collective-permute-start.9 = (bf16[176,256]{1,0:T(8,128)(2,1)S(1)}, bf16[176,256]{1,0:T(8,128)(2,1)S(1)}, u32[]{:S(2)}, u32[]{:S(2)}) collective-permute-start(bf16[176,256]{1,0:T(8,128)(2,1)S(1)} %get-tuple-element.52), channel_id=1, source_target_pairs={{0,0},{1,8},{2,2},{3,10},{4,4},{5,12},{6,6},{7,14},{8,1},{9,9},{10... | collective-permute-start | bytes 270344 | tf_op jit(solution)/shard_map/ppermute | solution.py:94
  32.1 13.7 %collective-permute-start.11 = (bf16[4,176,256]{2,1,0:T(8,128)(2,1)S(1)}, bf16[4,176,256]{2,1,0:T(8,128)(2,1)S(1)}, u32[]{:S(2)}, u32[]{:S(2)}) collective-permute-start(bf16[4,176,256]{2,1,0:T(8,128)(2,1)S(1)} %join.1.s00), channel_id=1, source_target_pairs={{0,2},{1,3},{2,0},{3,1},{4,6},{5,7},{6,4},{7,5},{8,10},{9,11},{10,... | collective-permute-start | bytes 1081352 | tf_op jit(solution)/shard_map/ppermute | solution.py:94
  33.4 12.4 %collective-permute-start.10 = (bf16[256,384]{1,0:T(8,128)(2,1)S(1)}, bf16[256,384]{1,0:T(8,128)(2,1)S(1)}, u32[]{:S(2)}, u32[]{:S(2)}) collective-permute-start(bf16[256,384]{1,0:T(8,128)(2,1)S(1)} %collective-permute-done.5.refs_6_), channel_id=1, source_target_pairs={{0,4},{1,5},{2,6},{3,7},{4,0},{5,1},{6,2},{7,3},{8,12},{9,13},{10,... | collective-permute-start | bytes 589832 | tf_op jit(solution)/shard_map/ppermute | solution.py:94
  33.8 9.2 %collective-permute-start.12 = (bf16[176,384]{1,0:T(8,128)(2,1)S(1)}, bf16[176,384]{1,0:T(8,128)(2,1)S(1)}, u32[]{:S(2)}, u32[]{:S(2)}) collective-permute-start(bf16[176,384]{1,0:T(8,128)(2,1)S(1)} %get-tuple-element.67), channel_id=1, source_target_pairs={{0,4},{4,8},{8,12},{12,0},{16,20},{20,24},{24,28},{28,16},{1,5},{5... | collective-permute-start | bytes 405512 | tf_op jit(solution)/shard_map/ppermute | solution.py:98
  34.8 8.2 %collective-permute-start.13 = (bf16[176,384]{1,0:T(8,128)(2,1)S(1)}, bf16[176,384]{1,0:T(8,128)(2,1)S(1)}, u32[]{:S(2)}, u32[]{:S(2)}) collective-permute-start(bf16[176,384]{1,0:T(8,128)(2,1)S(1)} %get-tuple-element.68), channel_id=1, source_target_pairs={{0,8},{4,12},{8,0},{12,4},{16,24},{20,28},{24,16},{28,20},{1,9},{5... | collective-permute-start | bytes 405512 | tf_op jit(solution)/shard_map/ppermute | solution.py:98
  34.8 10.9 %collective-permute-start.14 = (bf16[176,384]{1,0:T(8,128)(2,1)S(1)}, bf16[176,384]{1,0:T(8,128)(2,1)S(1)}, u32[]{:S(2)}, u32[]{:S(2)}) collective-permute-start(bf16[176,384]{1,0:T(8,128)(2,1)S(1)} %get-tuple-element.69), channel_id=1, source_target_pairs={{0,12},{4,0},{8,4},{12,8},{16,28},{20,16},{24,20},{28,24},{1,13},{... | collective-permute-start | bytes 405512 | tf_op jit(solution)/shard_map/ppermute | solution.py:98
  52.4 2.8 %collective-permute-start.22 = (bf16[4,176,256]{2,1,0:T(8,128)(2,1)S(1)}, bf16[4,176,256]{2,1,0:T(8,128)(2,1)S(1)}, u32[]{:S(2)}, u32[]{:S(2)}) collective-permute-start(bf16[4,176,256]{2,1,0:T(8,128)(2,1)S(1)} %collective-permute-done.11.s10), channel_id=1, source_target_pairs={{0,1},{1,0},{2,3},{3,2},{4,5},{5,4},{6,7},{7,6},{8,9},{9,8},{10,11... | collective-permute-start | bytes 1081352 | tf_op jit(solution)/shard_map/ppermute | solution.py:94
  54.3 9.7 %collective-permute-start.16 = (bf16[4,176,256]{2,1,0:T(8,128)(2,1)S(1)}, bf16[4,176,256]{2,1,0:T(8,128)(2,1)S(1)}, u32[]{:S(2)}, u32[]{:S(2)}) collective-permute-start(bf16[4,176,256]{2,1,0:T(8,128)(2,1)S(1)} %get-tuple-element.80), channel_id=1, source_target_pairs={{0,2},{1,3},{2,0},{3,1},{4,6},{5,7},{6,4},{7,5},{8,10},{9,11},{10,... | collective-permute-start | bytes 1081352 | tf_op jit(solution)/shard_map/ppermute | solution.py:94
  58.5 9.6 %collective-permute-start.23 = (bf16[176,384]{1,0:T(8,128)(2,1)S(1)}, bf16[176,384]{1,0:T(8,128)(2,1)S(1)}, u32[]{:S(2)}, u32[]{:S(2)}) collective-permute-start(bf16[176,384]{1,0:T(8,128)(2,1)S(1)} %get-tuple-element.88), channel_id=1, source_target_pairs={{0,12},{4,0},{8,4},{12,8},{16,28},{20,16},{24,20},{28,24},{1,13},{... | collective-permute-start | bytes 405512 | tf_op jit(solution)/shard_map/ppermute | solution.py:98
  58.5 12.8 %collective-permute-start.24 = (bf16[176,384]{1,0:T(8,128)(2,1)S(1)}, bf16[176,384]{1,0:T(8,128)(2,1)S(1)}, u32[]{:S(2)}, u32[]{:S(2)}) collective-permute-start(bf16[176,384]{1,0:T(8,128)(2,1)S(1)} %get-tuple-element.89), channel_id=1, source_target_pairs={{0,8},{4,12},{8,0},{12,4},{16,24},{20,28},{24,16},{28,20},{1,9},{5... | collective-permute-start | bytes 405512 | tf_op jit(solution)/shard_map/ppermute | solution.py:98
  60.2 12.1 %collective-permute-start.25 = (bf16[176,384]{1,0:T(8,128)(2,1)S(1)}, bf16[176,384]{1,0:T(8,128)(2,1)S(1)}, u32[]{:S(2)}, u32[]{:S(2)}) collective-permute-start(bf16[176,384]{1,0:T(8,128)(2,1)S(1)} %get-tuple-element.90), channel_id=1, source_target_pairs={{0,4},{4,8},{8,12},{12,0},{16,20},{20,24},{24,28},{28,16},{1,5},{5... | collective-permute-start | bytes 405512 | tf_op jit(solution)/shard_map/ppermute | solution.py:98
  64.1 9.4 %collective-permute-start.17 = (bf16[176,256]{1,0:T(8,128)(2,1)S(1)}, bf16[176,256]{1,0:T(8,128)(2,1)S(1)}, u32[]{:S(2)}, u32[]{:S(2)}) collective-permute-start(bf16[176,256]{1,0:T(8,128)(2,1)S(1)} %get-tuple-element.81), channel_id=1, source_target_pairs={{0,0},{1,8},{2,2},{3,10},{4,4},{5,12},{6,6},{7,14},{8,1},{9,9},{10... | collective-permute-start | bytes 270344 | tf_op jit(solution)/shard_map/ppermute | solution.py:94
  66.2 7.4 %collective-permute-start.18 = (bf16[176,256]{1,0:T(8,128)(2,1)S(1)}, bf16[176,256]{1,0:T(8,128)(2,1)S(1)}, u32[]{:S(2)}, u32[]{:S(2)}) collective-permute-start(bf16[176,256]{1,0:T(8,128)(2,1)S(1)} %get-tuple-element.82), channel_id=1, source_target_pairs={{0,4},{1,12},{2,6},{3,14},{4,0},{5,8},{6,2},{7,10},{8,5},{9,13},{1... | collective-permute-start | bytes 270344 | tf_op jit(solution)/shard_map/ppermute | solution.py:94
  68.0 7.4 %collective-permute-start.19 = (bf16[176,256]{1,0:T(8,128)(2,1)S(1)}, bf16[176,256]{1,0:T(8,128)(2,1)S(1)}, u32[]{:S(2)}, u32[]{:S(2)}) collective-permute-start(bf16[176,256]{1,0:T(8,128)(2,1)S(1)} %get-tuple-element.83), channel_id=1, source_target_pairs={{0,16},{1,24},{2,18},{3,26},{4,20},{5,28},{6,22},{7,30},{8,17},{9,... | collective-permute-start | bytes 270344 | tf_op jit(solution)/shard_map/ppermute | solution.py:94
  71.4 6.7 %collective-permute-start.20 = (bf16[176,256]{1,0:T(8,128)(2,1)S(1)}, bf16[176,256]{1,0:T(8,128)(2,1)S(1)}, u32[]{:S(2)}, u32[]{:S(2)}) collective-permute-start(bf16[176,256]{1,0:T(8,128)(2,1)S(1)} %get-tuple-element.84), channel_id=1, source_target_pairs={{0,20},{1,28},{2,22},{3,30},{4,16},{5,24},{6,18},{7,26},{8,21},{9,... | collective-permute-start | bytes 270344 | tf_op jit(solution)/shard_map/ppermute | solution.py:94
  (6 other events, 9.0 us)

commit v3 on v2

--- a/solution.py
+++ b/solution.py
@@ -101,6 +101,7 @@
 SWAP_H = lambda h, zl, y, x, c: (1 - h, zl, y, x, c)
 SWAP_Z = lambda h, zl, y, x, c: (h, 1 - zl, y, x, c)
 SWAP_Y = lambda h, zl, y, x, c: (h, zl, 1 - y, x, c)
+SWAP_ZY = lambda h, zl, y, x, c: (h, 1 - zl, 1 - y, x, c)
 SWAP_X = lambda h, zl, y, x, c: (h, zl, y, 1 - x, c)
 SWAP_C = lambda h, zl, y, x, c: (h, zl, y, x, 1 - c)
 
@@ -109,18 +110,34 @@
     return lambda h, zl, y, x, c: (h ^ a, c, y ^ b, x, zl)
 
 
-def dz_kernel(pre_ref, emb_ref, out_ref):
-    rows, half = pre_ref.shape[0], emb_ref.shape[0]
+def dz_kernel(pre_hbm, emb_hbm, filters_hbm, out_ref, along_ref, pre_ref, emb_ref, weight_ref, arrived):
+    rows, unit = pre_ref.shape[0], weight_ref.shape[0]
+    first = pl.multiple_of((1 + 2 * coords()[2]) * unit, 16)
+    copies = [
+        pltpu.make_async_copy(emb_hbm, emb_ref, arrived.at[0]),
+        pltpu.make_async_copy(pre_hbm, pre_ref, arrived.at[1]),
+        pltpu.make_async_copy(filters_hbm.at[pl.ds(first, unit), :], weight_ref, arrived.at[2]),
+    ]
+    for copy in copies:
+        copy.start()
+    half = emb_ref.shape[0]
     row = lax.broadcasted_iota(jnp.int32, (rows, half), 0)
     pair = lax.broadcasted_iota(jnp.int32, (rows, half), 1)
     twice = (row // 2 == pair).astype(BF16)
+    for copy in copies:
+        copy.wait()
     up = jnp.dot(twice, emb_ref[...], preferred_element_type=F32) * 0.5
-    out_ref[...] = (up * gelu_slope(pre_ref[...].astype(F32))).astype(BF16)
-
-
-def units_kernel(unit, filters_ref, *out_refs):
-    for m, ref in enumerate(out_refs):
+    value = (up * gelu_slope(pre_ref[...].astype(F32))).astype(BF16)
+    out_ref[...] = value
+    along_ref[:rows] = value
+    along_ref[rows:] = weight_ref[...]
+
+
+def units_kernel(unit, filters_ref, first_ref, middle_ref, last_ref, across_ref):
+    for m, ref in ((0, first_ref), (2, middle_ref), (4, last_ref)):
         ref[...] = filters_ref[m * unit : (m + 1) * unit, :]
+    first = pl.multiple_of((3 - 2 * coords()[2]) * unit, 16)
+    across_ref[...] = filters_ref[pl.ds(first, unit), :]
 
 
 def cut_kernel(unit, acts_ref, *out_refs):
@@ -144,44 +161,41 @@
         refs[-1][n] = ref[...]
 
 
-def input_kernel(rows, unit, *refs):
-    dz_refs, w_refs, (keep_ref, away_ref, dz_ref) = refs[:8], refs[8:13], refs[13:16]
-    weights, runs, arrived = refs[16:]
-    h, zl, y, _, c = coords()
-    q = 2 * zl + y
-    copies = []
-    for s in range(8):
-        block = 4 * (h ^ (s // 4)) + 2 * (zl ^ ((s // 2) % 2)) + (y ^ (s % 2))
-        there = dz_ref.at[pl.ds(pl.multiple_of(block * rows, rows), rows), :]
-        copies.append(pltpu.make_async_copy(dz_refs[s], there, arrived.at[s]))
-    for m in range(5):
-        there = weights.at[pl.ds(pl.multiple_of(lax.rem(q + 5 - m, 5) * unit, 16), unit), :]
-        copies.append(pltpu.make_async_copy(w_refs[m], there, arrived.at[8 + m]))
-    for copy in copies:
-        copy.start()
-    for copy in copies:
-        copy.wait()
-
-    long = 2 * rows
-    for r in range(4):
-        run = runs.at[2 * (r // 2) + ((r % 2) ^ c)]
-        lines = slice(max(r * long - 8, 0), min((r + 1) * long + 8, 4 * long))
-        value = dz_ref[lines, :].astype(F32)
-        if r == 0:
-            value = jnp.concatenate([jnp.zeros((8, value.shape[1]), F32), value], axis=0)
-        if r == 3:
-            value = jnp.concatenate([value, jnp.zeros((8, value.shape[1]), F32)], axis=0)
-        run[...] = value
-
+EDGE = 16
+
+
+def place_dz(rows, ref, s):
+    h, zl, y, _, _ = coords()
+    block = 4 * (h ^ (s // 4)) + 2 * (zl ^ ((s // 2) % 2)) + (y ^ (s % 2))
+    return ref.at[pl.ds(pl.multiple_of(block * rows + EDGE, EDGE), rows), :]
+
+
+def gather_kernel(rows, *refs):
+    out_ref = refs[-1]
+    zeros = jnp.zeros((EDGE, out_ref.shape[1]), BF16)
+    out_ref[:EDGE] = zeros
+    out_ref[EDGE + 8 * rows :] = zeros
+    for s, ref in enumerate(refs[:-1]):
+        place_dz(rows, out_ref, s)[...] = ref[:rows]
+
+
+def input_terms(rows, unit, dz_ref, weights, out_ref, side):
+    h, _, _, _, c = coords()
     for half in range(2):
 
         @pl.when(h == half)
         def _():
-            for t in range(8):
+            for n in range(4):
+                first = (4 * (n // 2) + 2 * (c ^ side) + n % 2) * rows
+                first = pl.multiple_of(first, EDGE)
+                window = dz_ref[pl.ds(first, rows + 2 * EDGE), :]
+                exact = window.astype(F32)
                 sums = [None, None]
                 for tap in range(2 * half, 2 * half + 3):
-                    first = 8 + (t % 2) * rows + 2 - tap
-                    shifted = runs[t // 2, first : first + rows, :].astype(BF16)
+                    if tap == 2:
+                        shifted = window[EDGE : EDGE + rows]
+                    else:
+                        shifted = exact[EDGE + 2 - tap : EDGE + 2 - tap + rows].astype(BF16)
                     slots = [v for v in range(5) if TAPS[half][v][0] == tap]
                     term = lax.dot_general(
                         weights[slots[0] * unit : (slots[-1] + 1) * unit, :],
@@ -189,26 +203,39 @@
                         (((1,), (1,)), ((), ())),
                         preferred_element_type=F32,
                     )
-                    for n, v in enumerate(slots):
+                    for k, v in enumerate(slots):
                         which = TAPS[half][v][1]
-                        one = term[n * unit : (n + 1) * unit]
+                        one = term[k * unit : (k + 1) * unit]
                         sums[which] = one if sums[which] is None else sums[which] + one
                 for which in range(2):
-                    ref = away_ref if (t // 2) % 2 else keep_ref
-                    ref[which ^ half, 2 * (t // 4) + t % 2] = sums[which].astype(ref.dtype)
-
-
-def cores_kernel(keep_ref, came_ref, keep_out, away_out):
+                    out_ref[(n // 2) ^ half, which ^ half, n % 2] = sums[which].astype(out_ref.dtype)
+
+
+def away_kernel(rows, unit, most_ref, dz_last, *refs):
+    w_refs, (dz_ref, weights, out_ref) = refs[:5], refs[5:]
+    _, zl, y, _, _ = coords()
+    place_dz(rows, dz_ref, 7)[...] = dz_last[...]
+    for m, ref in zip((0, 2, 4, 1 + 2 * y, 3 - 2 * y), w_refs):
+        slot = lax.rem(2 * zl + y + 5 - m, 5)
+        first = ref.shape[0] - unit
+        weights[pl.ds(pl.multiple_of(slot * unit, EDGE), unit), :] = ref[first:]
+    input_terms(rows, unit, dz_ref, weights, out_ref, 1)
+
+
+def keep_kernel(rows, unit, dz_ref, weights, out_ref):
+    input_terms(rows, unit, dz_ref, weights, out_ref, 0)
+
+
+def cores_kernel(a, keep_ref, came_ref, keep_out, away_out):
     x = coords()[3]
-    keep_out[...] = keep_ref[x] + came_ref[x].astype(F32)
-    away_out[...] = (keep_ref[1 - x] + came_ref[1 - x].astype(F32)).astype(BF16)
+    keep_out[...] = keep_ref[a, x] + came_ref[a, x].astype(F32)
+    away_out[...] = (keep_ref[a, 1 - x] + came_ref[a, 1 - x].astype(F32)).astype(BF16)
 
 
 def owners_kernel(keep_ref, came_ref, *out_refs):
-    h, _, y, _, _ = coords()
-    for n, ref in enumerate(out_refs):
-        block = 2 * (h ^ (n // 2)) + (y ^ (n % 2))
-        ref[...] = (keep_ref[block] + came_ref[block].astype(F32)).astype(BF16)
+    y = coords()[2]
+    for b, ref in enumerate(out_refs):
+        ref[...] = (keep_ref[y ^ b] + came_ref[y ^ b].astype(F32)).astype(BF16)
 
 
 def last_kernel(unit, *refs):
@@ -245,7 +272,7 @@
     _, zl, y, _, _ = coords()
     for m, ref in enumerate((first_ref, s1_ref, s2_ref, s3_ref, last_ref)):
         slot = lax.rem(2 * zl + y + 5 - m, 5)
-        grad = jnp.dot(left_ref[slot], dz_ref[...], preferred_element_type=F32) * scale
+        grad = jnp.dot(left_ref[slot], dz_ref[EDGE:-EDGE, :], preferred_element_type=F32) * scale
         ref[...] = grad.astype(ref.dtype)
 
 
@@ -254,7 +281,7 @@
         out_ref[m * unit : (m + 1) * unit, :] = ref[...].astype(F32)
 
 
-def call(kernel, name, shapes, args, scratch=(), flops=0, mib=16, anywhere=False):
+def call(kernel, name, shapes, args, scratch=(), flops=0, mib=16, anywhere=False, alias={}):
     many = isinstance(shapes, tuple)
     spec = pl.BlockSpec(memory_space=pltpu.VMEM)
     nbytes = sum(a.size * a.dtype.itemsize for a in args + (shapes if many else (shapes,)))
@@ -264,8 +291,9 @@
         in_specs=[pl.BlockSpec(memory_space=pl.ANY) if anywhere else spec] * len(args),
         out_specs=(spec,) * len(shapes) if many else spec,
         scratch_shapes=list(scratch),
+        input_output_aliases=alias,
         compiler_params=pltpu.CompilerParams(vmem_limit_bytes=mib << 20),
-        cost_estimate=pl.CostEstimate(flops=flops, bytes_accessed=nbytes, transcendentals=0),
+        cost_estimate=pl.CostEstimate(flops=0, bytes_accessed=1024, transcendentals=0),
         name=name,
     )(*args)
 
@@ -280,24 +308,41 @@
     block, weight, pos = shape((rows, wide), BF16), shape((unit, wide), BF16), shape((unit, rows), BF16)
 
     tie = lax.optimization_barrier
-    dz = call(dz_kernel, "dz", block, (pre_act, emb_grad), mib=8)
+    dz, along = call(
+        dz_kernel,
+        "dz",
+        (block, shape((rows + unit, wide), BF16)),
+        (pre_act, emb_grad, filters),
+        scratch=[
+            pltpu.VMEM(pre_act.shape, BF16),
+            pltpu.VMEM(emb_grad.shape, BF16),
+            pltpu.VMEM((unit, wide), BF16),
+            pltpu.SemaphoreType.DMA((3,)),
+        ],
+        mib=60,
+        anywhere=True,
+    )
     own0, own1 = call(functools.partial(cut_kernel, unit), "cut", (pos, pos), (acts,), mib=8)
-    dz_h, dz_z, dz_y = send(dz, SWAP_H), send(dz, SWAP_Z), send(dz, SWAP_Y)
+    dz_h, dz_z, dz_y = send(dz, SWAP_H), send(dz, SWAP_Z), send(along, SWAP_Y)
     t11, t01 = send(own1, turn(1, 1)), send(own1, turn(0, 1))
 
-    dz_h, dz_z, dz_y, t11, t01, own0, filters = tie((dz_h, dz_z, dz_y, t11, t01, own0, filters))
-    dz_hz, dz_zy, dz_hy = send(dz_h, SWAP_Z), send(dz_z, SWAP_Y), send(dz_h, SWAP_Y)
+    dz_zy = send(dz_z, SWAP_Y)
+    dz_h, dz_y, t11, t01, own0, filters = tie((dz_h, dz_y, t11, t01, own0, filters))
+    dz_hz, dz_hy = send(dz_h, SWAP_Z), send(dz_h, SWAP_Y)
     t10, t00 = send(own0, turn(1, 0)), send(own0, turn(0, 0))
-    units = call(functools.partial(units_kernel, unit), "units", (weight,) * 5, (filters,), mib=4)
+    units = call(functools.partial(units_kernel, unit), "units", (weight,) * 4, (filters,), mib=4)
 
     dz_hz, dz_zy, dz_hy, t10, t00, *units = tie((dz_hz, dz_zy, dz_hy, t10, t00, *units))
-    dz_hzy = send(dz_hz, SWAP_Y)
-    weights = tuple(in_half(w, m) if m in (1, 2, 3) else w for m, w in enumerate(units))
     got = call(join_kernel, "join", shape((4, unit, rows), BF16), (t00, t01, t10, t11), mib=4)
     other = send(got, SWAP_X)
-
-    dz_hzy, other, *weights = tie((dz_hzy, other, *weights))
-    far, far_other = send(got, SWAP_C), send(other, SWAP_C)
+    dz_hzy = send(dz_hz, SWAP_Y)
+    w0, w2, w4, wd = units
+    w2, wd = send(w2, SWAP_Z), send(wd, SWAP_ZY)
+    far = send(got, SWAP_C)
+
+    weights = (w0, w2, w4, wd, dz_y)
+    dz_hzy, other, far, *weights = tie((dz_hzy, other, far, *weights))
+    far_other = send(other, SWAP_C)
     left = call(
         functools.partial(left_kernel, rows, unit),
         "left",
@@ -305,30 +350,41 @@
         (got, other, far, far_other),
         scratch=[pltpu.VMEM((2, unit, total), F32)],
     )
-    blocks = (dz, dz_y, dz_z, dz_zy, dz_h, dz_hy, dz_hz, dz_hzy)
-
-    keep, away, dz_all = call(
-        functools.partial(input_kernel, rows, unit),
-        "input",
-        (shape((2, 4, unit, rows), F32), shape((2, 4, unit, rows), BF16), shape((total, wide), BF16)),
-        blocks + tuple(weights),
-        scratch=[
-            pltpu.VMEM((5 * unit, wide), BF16),
-            pltpu.VMEM((4, 2 * rows + 16, wide), F32),
-            pltpu.SemaphoreType.DMA((13,)),
-        ],
-        flops=flops,
-        anywhere=True,
-    )
-
-    keep, away = call(
-        cores_kernel,
-        "cores",
-        (shape((4, unit, rows), F32), shape((4, unit, rows), BF16)),
-        (keep, send(away, SWAP_C)),
-    )
-    ready = call(owners_kernel, "owners", (pos,) * 4, (keep, send(away, SWAP_X)))
-    came = tuple(send(r, turn(n // 2, n % 2)) for n, r in enumerate(ready))
+    padded = shape((total + 2 * EDGE, wide), BF16)
+    most = call(
+        functools.partial(gather_kernel, rows),
+        "gather",
+        padded,
+        (dz, dz_y, dz_z, dz_zy, dz_h, dz_hy, dz_hz),
+        mib=8,
+    )
+    dz_all, ordered, away = call(
+        functools.partial(away_kernel, rows, unit),
+        "away",
+        (padded, shape((5 * unit, wide), BF16), shape((2, 2, 2, unit, rows), BF16)),
+        (most, dz_hzy) + tuple(weights),
+        flops=flops // 2,
+        alias={0: 0},
+    )
+    keep = call(
+        functools.partial(keep_kernel, rows, unit),
+        "keep",
+        shape((2, 2, 2, unit, rows), F32),
+        (dz_all, ordered),
+        flops=flops // 2,
+    )
+
+    came = send(away, SWAP_C)
+    parts = (shape((2, unit, rows), F32), shape((2, unit, rows), BF16))
+    keep_far, far = call(functools.partial(cores_kernel, 1), "cores_far", parts, (keep, came))
+    keep, came, keep_far = tie((keep, came, keep_far))
+    keep_near, near = call(functools.partial(cores_kernel, 0), "cores_near", parts, (keep, came))
+    far, near = send(far, SWAP_X), send(near, SWAP_X)
+    far_blocks = call(owners_kernel, "far", (pos,) * 2, (keep_far, far), mib=8)
+    near_blocks = call(owners_kernel, "near", (pos,) * 2, (keep_near, near), mib=8)
+    far_blocks = [send(block, turn(1, b)) for b, block in enumerate(far_blocks)]
+    near_blocks = [send(block, turn(0, b)) for b, block in enumerate(near_blocks)]
+    came = tuple(far_blocks + near_blocks)
     input_grad = call(functools.partial(last_kernel, unit), "last", shape((2 * unit, rows), BF16), came, mib=4).T
 
     grads = call(

time: 79 us -> 70.2 us (0.89)
  waiting for transfers between devices: 30.4 us -> 22.8 us
  starting transfers between devices: 31.7 us -> 34.6 us
  local copies, waits for them, and re-layouts: 4.01 us -> 1.12 us
  Pallas kernels: 11.9 us -> 10.7 us
    ppermute x6 -> x3, waiting for transfers between devices: 9.55 us -> 0.01 us  [in_half(): lax.ppermute(value, 'seq', [(i, 4 * (i // 4) + (i % 4 + step) % 4) for i...]
    ppermute x20 -> x23, starting transfers between devices: 27.5 us -> 32.9 us  [send(): return lax.ppermute(value, ('seq', 'section'), pairs)]
    unnamed x8 -> x6, local copies, waits for them, and re-layouts: 4.01 us -> 1.12 us
    ppermute x6 -> x3, starting transfers between devices: 4.12 us -> 1.7 us  [in_half(): lax.ppermute(value, 'seq', [(i, 4 * (i // 4) + (i % 4 + step) % 4) for i...]
    ppermute x20 -> x23, waiting for transfers between devices: 20.8 us -> 22.7 us  [send(): return lax.ppermute(value, ('seq', 'section'), pairs)]
    pallas_call x11 -> x15, Pallas kernels: 11.9 us -> 10.7 us  [call(): pl.pallas_call(kernel, out_shape=shapes, in_specs=[pl.BlockSpec(memory_sp...]
  transfers between devices with their start and end apart: 26 -> 26, of which waited for: 10 -> 11; matrix products, arithmetic and copies ran while one was open for 0% -> 0% of each run, Pallas kernels for 7% -> 9%
where the time goes in v3:
time: 70.2 us; the launch traced here: 70 us
  starting transfers between devices  34.6 us (49%)
  waiting for transfers between devices  22.8 us (32%)
  Pallas kernels  10.7 us (15%)
  local copies, waits for them, and re-layouts  1.12 us (2%)
  between operations  0.8 us (1%)
    ppermute x23, starting transfers between devices, send(): return lax.ppermute(value, ('seq', 'section'), pairs)  32.9 us
    ppermute x23, waiting for transfers between devices, send(): return lax.ppermute(value, ('seq', 'section'), pairs)  22.7 us
    pallas_call x15, Pallas kernels, call(): pl.pallas_call(kernel, out_shape=shapes, in_specs=[pl.BlockSpec(memory_sp...  10.7 us
    ppermute x3, starting transfers between devices, in_half(): lax.ppermute(value, 'seq', [(i, 4 * (i // 4) + (i % 4 + step) % 4) for i...  1.7 us
  transfers between devices with their start and end apart: 26, of which 11 were waited for; matrix products, arithmetic and copies ran while one was open for 0% of the time, Pallas kernels for 9%

profile of v3, /device:TPU:1, one launch (start us, length us, event | category | flops | bytes accessed | tf_op | source)
XLA Modules:
  0.0 70.0 jit_solution(14873383215024562607)
XLA Ops:
  0.6 2.2 %dz.1 = (bf16[256,384]{1,0:T(8,128)(2,1)}, bf16[432,384]{1,0:T(8,128)(2,1)}) custom-call(bf16[256,384]{1,0:T(8,128)(2,1)} %pre_hbm.1, bf16[128,384]{1,0:T(8,128)(2,1)} %emb_hbm.1, bf16[880,384]{1,0:T(8,128)(2,1)} %filters_ref), custom_call_target="tpu_custom_call" | custom-call | bytes 1024 | tf_op jit(solution)/shard_map/dz/pallas_call | solution.py:288
  2.9 2.1 %collective-permute-start.1 = (bf16[432,384]{1,0:T(8,128)(2,1)}, bf16[432,384]{1,0:T(8,128)(2,1)S(1)}, u32[]{:S(2)}, u32[]{:S(2)}) collective-permute-start(bf16[432,384]{1,0:T(8,128)(2,1)} %get-tuple-element.53), channel_id=1, source_target_pairs={{0,4},{1,5},{2,6},{3,7},{4,0},{5,1},{6,2},{7,3},{8,12},{9,13},{10,... | collective-permute-start | bytes 995336 | tf_op jit(solution)/shard_map/ppermute | solution.py:94
  5.0 1.3 %collective-permute-start.4 = (bf16[256,384]{1,0:T(8,128)(2,1)}, bf16[256,384]{1,0:T(8,128)(2,1)S(1)}, u32[]{:S(2)}, u32[]{:S(2)}) collective-permute-start(bf16[256,384]{1,0:T(8,128)(2,1)} %get-tuple-element.52.refs_0_), channel_id=1, source_target_pairs={{0,8},{1,9},{2,10},{3,11},{4,12},{5,13},{6,14},{7,15},{8,0},{9,1},... | collective-permute-start | bytes 589832 | tf_op jit(solution)/shard_map/ppermute | solution.py:94
  6.3 2.3 %collective-permute-start = (bf16[256,384]{1,0:T(8,128)(2,1)}, bf16[256,384]{1,0:T(8,128)(2,1)S(1)}, u32[]{:S(2)}, u32[]{:S(2)}) collective-permute-start(bf16[256,384]{1,0:T(8,128)(2,1)} %get-tuple-element.52.refs_0_), channel_id=1, source_target_pairs={{0,16},{1,17},{2,18},{3,19},{4,20},{5,21},{6,22},{7,23},{8,24},{9,... | collective-permute-start | bytes 589832 | tf_op jit(solution)/shard_map/ppermute | solution.py:94
  11.7 1.9 %collective-permute-done.4.refs_2_ = bf16[256,384]{1,0:T(8,128)(2,1)S(1)} collective-permute-done((bf16[256,384]{1,0:T(8,128)(2,1)}, bf16[256,384]{1,0:T(8,128)(2,1)S(1)}, u32[]{:S(2)}, u32[]{:S(2)}) %collective-permute-start.4) | collective-permute-done | bytes 196640 | tf_op jit(solution)/shard_map/ppermute | solution.py:94
  14.2 5.9 %collective-permute-done.2.refs_3_ = bf16[176,256]{1,0:T(8,128)(2,1)S(1)} collective-permute-done((bf16[176,256]{1,0:T(8,128)(2,1)S(1)}, bf16[176,256]{1,0:T(8,128)(2,1)S(1)}, u32[]{:S(2)}, u32[]{:S(2)}) %collective-permute-start.2) | collective-permute-done | bytes 90144 | tf_op jit(solution)/shard_map/ppermute | solution.py:94
  20.2 1.3 %collective-permute-start.7 = (bf16[256,384]{1,0:T(8,128)(2,1)S(1)}, bf16[256,384]{1,0:T(8,128)(2,1)S(1)}, u32[]{:S(2)}, u32[]{:S(2)}) collective-permute-start(bf16[256,384]{1,0:T(8,128)(2,1)S(1)} %collective-permute-done.refs_4_), channel_id=1, source_target_pairs={{0,4},{1,5},{2,6},{3,7},{4,0},{5,1},{6,2},{7,3},{8,12},{9,13},{10,... | collective-permute-start | bytes 589832 | tf_op jit(solution)/shard_map/ppermute | solution.py:94
  21.5 4.0 %collective-permute-start.8 = (bf16[176,256]{1,0:T(8,128)(2,1)S(1)}, bf16[176,256]{1,0:T(8,128)(2,1)S(1)}, u32[]{:S(2)}, u32[]{:S(2)}) collective-permute-start(bf16[176,256]{1,0:T(8,128)(2,1)S(1)} %get-tuple-element.58), channel_id=1, source_target_pairs={{0,16},{1,24},{2,18},{3,26},{4,20},{5,28},{6,22},{7,30},{8,17},{9,... | collective-permute-start | bytes 270344 | tf_op jit(solution)/shard_map/ppermute | solution.py:94
  25.5 2.5 %collective-permute-start.9 = (bf16[176,256]{1,0:T(8,128)(2,1)S(1)}, bf16[176,256]{1,0:T(8,128)(2,1)S(1)}, u32[]{:S(2)}, u32[]{:S(2)}) collective-permute-start(bf16[176,256]{1,0:T(8,128)(2,1)S(1)} %get-tuple-element.58), channel_id=1, source_target_pairs={{0,0},{1,8},{2,2},{3,10},{4,4},{5,12},{6,6},{7,14},{8,1},{9,9},{10... | collective-permute-start | bytes 270344 | tf_op jit(solution)/shard_map/ppermute | solution.py:94
  28.1 3.1 %collective-permute-done.8.refs_2_ = bf16[176,256]{1,0:T(8,128)(2,1)S(1)} collective-permute-done((bf16[176,256]{1,0:T(8,128)(2,1)S(1)}, bf16[176,256]{1,0:T(8,128)(2,1)S(1)}, u32[]{:S(2)}, u32[]{:S(2)}) %collective-permute-start.8) | collective-permute-done | bytes 90144 | tf_op jit(solution)/shard_map/ppermute | solution.py:94
  32.3 1.3 %collective-permute-start.11 = (bf16[4,176,256]{2,1,0:T(8,128)(2,1)S(1)}, bf16[4,176,256]{2,1,0:T(8,128)(2,1)S(1)}, u32[]{:S(2)}, u32[]{:S(2)}) collective-permute-start(bf16[4,176,256]{2,1,0:T(8,128)(2,1)S(1)} %join.1.s00), channel_id=1, source_target_pairs={{0,2},{1,3},{2,0},{3,1},{4,6},{5,7},{6,4},{7,5},{8,10},{9,11},{10,... | collective-permute-start | bytes 1081352 | tf_op jit(solution)/shard_map/ppermute | solution.py:94
  34.6 2.5 %collective-permute-start.14 = (bf16[176,384]{1,0:T(8,128)(2,1)S(1)}, bf16[176,384]{1,0:T(8,128)(2,1)S(1)}, u32[]{:S(2)}, u32[]{:S(2)}) collective-permute-start(bf16[176,384]{1,0:T(8,128)(2,1)S(1)} %get-tuple-element.74), channel_id=1, source_target_pairs={{0,12},{1,13},{2,14},{3,15},{4,8},{5,9},{6,10},{7,11},{8,4},{9,5},... | collective-permute-start | bytes 405512 | tf_op jit(solution)/shard_map/ppermute | solution.py:94
  37.2 2.2 %collective-permute-done.13.refs_1_ = bf16[176,384]{1,0:T(8,128)(2,1)S(1)} collective-permute-done((bf16[176,384]{1,0:T(8,128)(2,1)S(1)}, bf16[176,384]{1,0:T(8,128)(2,1)S(1)}, u32[]{:S(2)}, u32[]{:S(2)}) %collective-permute-start.13) | collective-permute-done | bytes 135200 | tf_op jit(solution)/shard_map/ppermute | solution.py:94
  39.5 4.0 %collective-permute-done.14.refs_3_ = bf16[176,384]{1,0:T(8,128)(2,1)S(1)} collective-permute-done((bf16[176,384]{1,0:T(8,128)(2,1)S(1)}, bf16[176,384]{1,0:T(8,128)(2,1)S(1)}, u32[]{:S(2)}, u32[]{:S(2)}) %collective-permute-start.14) | collective-permute-done | bytes 135200 | tf_op jit(solution)/shard_map/ppermute | solution.py:94
  43.4 1.3 %away.1 = (bf16[2080,384]{1,0:T(8,128)(2,1)S(1)}, bf16[880,384]{1,0:T(8,128)(2,1)S(1)}, bf16[2,2,2,176,256]{4,3,2,1,0:T(8,128)(2,1)S(1)}) custom-call(bf16[2080,384]{1,0:T(8,128)(2,1)S(1)} %gather.1.most_ref, bf16[256,384]{1,0:T(8,128)(2,1)S(1)} %collective-permute-done.10.dz_last, ...), custom_call_target="tpu_custom_call", output_to_operand_aliasing={{0}: (0, {})} | custom-call | bytes 1024 | tf_op jit(solution)/shard_map/away/pallas_call | solution.py:288
  44.8 1.2 %collective-permute-start.15 = (bf16[2,2,2,176,256]{4,3,2,1,0:T(8,128)(2,1)S(1)}, bf16[2,2,2,176,256]{4,3,2,1,0:T(8,128)(2,1)S(1)}, u32[]{:S(2)}, u32[]{:S(2)}) collective-permute-start(bf16[2,2,2,176,256]{4,3,2,1,0:T(8,128)(2,1)S(1)} %get-tuple-element.83), channel_id=1, source_target_pairs={{0,1},{1,0},{2,3},{3,2},{4,5},{5,4},{6,7},{7,6},{8,9},{9,8},{10,11... | collective-permute-start | bytes 2162696 | tf_op jit(solution)/shard_map/ppermute | solution.py:94
  48.3 1.3 %collective-permute-start.19 = (bf16[2,176,256]{2,1,0:T(8,128)(2,1)S(1)}, bf16[2,176,256]{2,1,0:T(8,128)(2,1)S(1)}, u32[]{:S(2)}, u32[]{:S(2)}) collective-permute-start(bf16[2,176,256]{2,1,0:T(8,128)(2,1)S(1)} %get-tuple-element.92), channel_id=1, source_target_pairs={{0,2},{1,3},{2,0},{3,1},{4,6},{5,7},{6,4},{7,5},{8,10},{9,11},{10,... | collective-permute-start | bytes 540680 | tf_op jit(solution)/shard_map/ppermute | solution.py:94
  50.7 2.1 %filter.1 = (f32[176,384]{1,0:T(8,128)S(1)}, bf16[176,384]{1,0:T(8,128)(2,1)S(1)}, bf16[176,384]{1,0:T(8,128)(2,1)S(1)}, bf16[176,384]{1,0:T(8,128)(2,1)S(1)}, f32[176,384]{1,0:T(8,128)S(1)}) custom-call(bf16[5,176,2048]{2,1,0:T(8,128)(2,1)S(1)} %left.1.left_ref, bf16[2080,384]{1,0:T(8,128)(2,1)S(1)} %get-tuple-element.81.dz_ref), custom_call_target="tpu_custom_call" | custom-call | bytes 1024 | tf_op jit(solution)/shard_map/filter/pallas_call | solution.py:288
  54.6 2.9 %collective-permute-start.17 = (bf16[176,256]{1,0:T(8,128)(2,1)S(1)}, bf16[176,256]{1,0:T(8,128)(2,1)S(1)}, u32[]{:S(2)}, u32[]{:S(2)}) collective-permute-start(bf16[176,256]{1,0:T(8,128)(2,1)S(1)} %get-tuple-element.87), channel_id=1, source_target_pairs={{0,16},{1,24},{2,18},{3,26},{4,20},{5,28},{6,22},{7,30},{8,17},{9,... | collective-permute-start | bytes 270344 | tf_op jit(solution)/shard_map/ppermute | solution.py:94
  57.6 2.7 %collective-permute-start.18 = (bf16[176,256]{1,0:T(8,128)(2,1)S(1)}, bf16[176,256]{1,0:T(8,128)(2,1)S(1)}, u32[]{:S(2)}, u32[]{:S(2)}) collective-permute-start(bf16[176,256]{1,0:T(8,128)(2,1)S(1)} %get-tuple-element.88), channel_id=1, source_target_pairs={{0,20},{1,28},{2,22},{3,30},{4,16},{5,24},{6,18},{7,26},{8,21},{9,... | collective-permute-start | bytes 270344 | tf_op jit(solution)/shard_map/ppermute | solution.py:94
  60.4 1.9 %collective-permute-start.20 = (bf16[176,256]{1,0:T(8,128)(2,1)S(1)}, bf16[176,256]{1,0:T(8,128)(2,1)S(1)}, u32[]{:S(2)}, u32[]{:S(2)}) collective-permute-start(bf16[176,256]{1,0:T(8,128)(2,1)S(1)} %get-tuple-element.93), channel_id=1, source_target_pairs={{0,0},{1,8},{2,2},{3,10},{4,4},{5,12},{6,6},{7,14},{8,1},{9,9},{10... | collective-permute-start | bytes 270344 | tf_op jit(solution)/shard_map/ppermute | solution.py:94
  62.3 2.0 %collective-permute-start.21 = (bf16[176,256]{1,0:T(8,128)(2,1)S(1)}, bf16[176,256]{1,0:T(8,128)(2,1)S(1)}, u32[]{:S(2)}, u32[]{:S(2)}) collective-permute-start(bf16[176,256]{1,0:T(8,128)(2,1)S(1)} %get-tuple-element.94), channel_id=1, source_target_pairs={{0,4},{1,12},{2,6},{3,14},{4,0},{5,8},{6,2},{7,10},{8,5},{9,13},{1... | collective-permute-start | bytes 270344 | tf_op jit(solution)/shard_map/ppermute | solution.py:94
  66.3 1.5 %collective-permute-done.20.refs_2_ = bf16[176,256]{1,0:T(8,128)(2,1)S(1)} collective-permute-done((bf16[176,256]{1,0:T(8,128)(2,1)S(1)}, bf16[176,256]{1,0:T(8,128)(2,1)S(1)}, u32[]{:S(2)}, u32[]{:S(2)}) %collective-permute-start.20) | collective-permute-done | bytes 90144 | tf_op jit(solution)/shard_map/ppermute | solution.py:94
  67.8 1.5 %collective-permute-done.21.refs_3_ = bf16[176,256]{1,0:T(8,128)(2,1)S(1)} collective-permute-done((bf16[176,256]{1,0:T(8,128)(2,1)S(1)}, bf16[176,256]{1,0:T(8,128)(2,1)S(1)}, u32[]{:S(2)}, u32[]{:S(2)}) %collective-permute-start.21) | collective-permute-done | bytes 90144 | tf_op jit(solution)/shard_map/ppermute | solution.py:94
  (49 shorter events, 14.1 us)
Async XLA Ops:
  2.9 17.3 %collective-permute-start.1 = (bf16[432,384]{1,0:T(8,128)(2,1)}, bf16[432,384]{1,0:T(8,128)(2,1)S(1)}, u32[]{:S(2)}, u32[]{:S(2)}) collective-permute-start(bf16[432,384]{1,0:T(8,128)(2,1)} %get-tuple-element.53), channel_id=1, source_target_pairs={{0,4},{1,5},{2,6},{3,7},{4,0},{5,1},{6,2},{7,3},{8,12},{9,13},{10,... | collective-permute-start | bytes 995336 | tf_op jit(solution)/shard_map/ppermute | solution.py:94
  5.0 8.7 %collective-permute-start.4 = (bf16[256,384]{1,0:T(8,128)(2,1)}, bf16[256,384]{1,0:T(8,128)(2,1)S(1)}, u32[]{:S(2)}, u32[]{:S(2)}) collective-permute-start(bf16[256,384]{1,0:T(8,128)(2,1)} %get-tuple-element.52.refs_0_), channel_id=1, source_target_pairs={{0,8},{1,9},{2,10},{3,11},{4,12},{5,13},{6,14},{7,15},{8,0},{9,1},... | collective-permute-start | bytes 589832 | tf_op jit(solution)/shard_map/ppermute | solution.py:94
  6.3 13.9 %collective-permute-start = (bf16[256,384]{1,0:T(8,128)(2,1)}, bf16[256,384]{1,0:T(8,128)(2,1)S(1)}, u32[]{:S(2)}, u32[]{:S(2)}) collective-permute-start(bf16[256,384]{1,0:T(8,128)(2,1)} %get-tuple-element.52.refs_0_), channel_id=1, source_target_pairs={{0,16},{1,17},{2,18},{3,19},{4,20},{5,21},{6,22},{7,23},{8,24},{9,... | collective-permute-start | bytes 589832 | tf_op jit(solution)/shard_map/ppermute | solution.py:94
  10.1 10.0 %collective-permute-start.2 = (bf16[176,256]{1,0:T(8,128)(2,1)S(1)}, bf16[176,256]{1,0:T(8,128)(2,1)S(1)}, u32[]{:S(2)}, u32[]{:S(2)}) collective-permute-start(bf16[176,256]{1,0:T(8,128)(2,1)S(1)} %get-tuple-element.54), channel_id=1, source_target_pairs={{0,20},{1,28},{2,22},{3,30},{4,16},{5,24},{6,18},{7,26},{8,21},{9,... | collective-permute-start | bytes 270344 | tf_op jit(solution)/shard_map/ppermute | solution.py:94
  11.0 9.1 %collective-permute-start.3 = (bf16[176,256]{1,0:T(8,128)(2,1)S(1)}, bf16[176,256]{1,0:T(8,128)(2,1)S(1)}, u32[]{:S(2)}, u32[]{:S(2)}) collective-permute-start(bf16[176,256]{1,0:T(8,128)(2,1)S(1)} %get-tuple-element.54), channel_id=1, source_target_pairs={{0,4},{1,12},{2,6},{3,14},{4,0},{5,8},{6,2},{7,10},{8,5},{9,13},{1... | collective-permute-start | bytes 270344 | tf_op jit(solution)/shard_map/ppermute | solution.py:94
  13.6 14.5 %collective-permute-start.6 = (bf16[256,384]{1,0:T(8,128)(2,1)S(1)}, bf16[256,384]{1,0:T(8,128)(2,1)S(1)}, u32[]{:S(2)}, u32[]{:S(2)}) collective-permute-start(bf16[256,384]{1,0:T(8,128)(2,1)S(1)} %collective-permute-done.4.refs_2_), channel_id=1, source_target_pairs={{0,4},{1,5},{2,6},{3,7},{4,0},{5,1},{6,2},{7,3},{8,12},{9,13},{10,... | collective-permute-start | bytes 589832 | tf_op jit(solution)/shard_map/ppermute | solution.py:94
  20.2 12.2 %collective-permute-start.5 = (bf16[256,384]{1,0:T(8,128)(2,1)S(1)}, bf16[256,384]{1,0:T(8,128)(2,1)S(1)}, u32[]{:S(2)}, u32[]{:S(2)}) collective-permute-start(bf16[256,384]{1,0:T(8,128)(2,1)S(1)} %collective-permute-done.refs_4_), channel_id=1, source_target_pairs={{0,8},{1,9},{2,10},{3,11},{4,12},{5,13},{6,14},{7,15},{8,0},{9,1},... | collective-permute-start | bytes 589832 | tf_op jit(solution)/shard_map/ppermute | solution.py:94
  20.2 12.1 %collective-permute-start.7 = (bf16[256,384]{1,0:T(8,128)(2,1)S(1)}, bf16[256,384]{1,0:T(8,128)(2,1)S(1)}, u32[]{:S(2)}, u32[]{:S(2)}) collective-permute-start(bf16[256,384]{1,0:T(8,128)(2,1)S(1)} %collective-permute-done.refs_4_), channel_id=1, source_target_pairs={{0,4},{1,5},{2,6},{3,7},{4,0},{5,1},{6,2},{7,3},{8,12},{9,13},{10,... | collective-permute-start | bytes 589832 | tf_op jit(solution)/shard_map/ppermute | solution.py:94
  21.5 9.6 %collective-permute-start.8 = (bf16[176,256]{1,0:T(8,128)(2,1)S(1)}, bf16[176,256]{1,0:T(8,128)(2,1)S(1)}, u32[]{:S(2)}, u32[]{:S(2)}) collective-permute-start(bf16[176,256]{1,0:T(8,128)(2,1)S(1)} %get-tuple-element.58), channel_id=1, source_target_pairs={{0,16},{1,24},{2,18},{3,26},{4,20},{5,28},{6,22},{7,30},{8,17},{9,... | collective-permute-start | bytes 270344 | tf_op jit(solution)/shard_map/ppermute | solution.py:94
  25.5 6.8 %collective-permute-start.9 = (bf16[176,256]{1,0:T(8,128)(2,1)S(1)}, bf16[176,256]{1,0:T(8,128)(2,1)S(1)}, u32[]{:S(2)}, u32[]{:S(2)}) collective-permute-start(bf16[176,256]{1,0:T(8,128)(2,1)S(1)} %get-tuple-element.58), channel_id=1, source_target_pairs={{0,0},{1,8},{2,2},{3,10},{4,4},{5,12},{6,6},{7,14},{8,1},{9,9},{10... | collective-permute-start | bytes 270344 | tf_op jit(solution)/shard_map/ppermute | solution.py:94
  32.3 11.1 %collective-permute-start.11 = (bf16[4,176,256]{2,1,0:T(8,128)(2,1)S(1)}, bf16[4,176,256]{2,1,0:T(8,128)(2,1)S(1)}, u32[]{:S(2)}, u32[]{:S(2)}) collective-permute-start(bf16[4,176,256]{2,1,0:T(8,128)(2,1)S(1)} %join.1.s00), channel_id=1, source_target_pairs={{0,2},{1,3},{2,0},{3,1},{4,6},{5,7},{6,4},{7,5},{8,10},{9,11},{10,... | collective-permute-start | bytes 1081352 | tf_op jit(solution)/shard_map/ppermute | solution.py:94
  33.6 9.8 %collective-permute-start.12 = (bf16[4,176,256]{2,1,0:T(8,128)(2,1)S(1)}, bf16[4,176,256]{2,1,0:T(8,128)(2,1)S(1)}, u32[]{:S(2)}, u32[]{:S(2)}) collective-permute-start(bf16[4,176,256]{2,1,0:T(8,128)(2,1)S(1)} %join.1.s00), channel_id=1, source_target_pairs={{0,1},{1,0},{2,3},{3,2},{4,5},{5,4},{6,7},{7,6},{8,9},{9,8},{10,11... | collective-permute-start | bytes 1081352 | tf_op jit(solution)/shard_map/ppermute | solution.py:94
  34.4 9.0 %collective-permute-start.10 = (bf16[256,384]{1,0:T(8,128)(2,1)S(1)}, bf16[256,384]{1,0:T(8,128)(2,1)S(1)}, u32[]{:S(2)}, u32[]{:S(2)}) collective-permute-start(bf16[256,384]{1,0:T(8,128)(2,1)S(1)} %collective-permute-done.5.refs_6_), channel_id=1, source_target_pairs={{0,4},{1,5},{2,6},{3,7},{4,0},{5,1},{6,2},{7,3},{8,12},{9,13},{10,... | collective-permute-start | bytes 589832 | tf_op jit(solution)/shard_map/ppermute | solution.py:94
  34.4 5.1 %collective-permute-start.13 = (bf16[176,384]{1,0:T(8,128)(2,1)S(1)}, bf16[176,384]{1,0:T(8,128)(2,1)S(1)}, u32[]{:S(2)}, u32[]{:S(2)}) collective-permute-start(bf16[176,384]{1,0:T(8,128)(2,1)S(1)} %get-tuple-element.72), channel_id=1, source_target_pairs={{0,8},{1,9},{2,10},{3,11},{4,12},{5,13},{6,14},{7,15},{8,0},{9,1},... | collective-permute-start | bytes 405512 | tf_op jit(solution)/shard_map/ppermute | solution.py:94
  34.6 8.8 %collective-permute-start.14 = (bf16[176,384]{1,0:T(8,128)(2,1)S(1)}, bf16[176,384]{1,0:T(8,128)(2,1)S(1)}, u32[]{:S(2)}, u32[]{:S(2)}) collective-permute-start(bf16[176,384]{1,0:T(8,128)(2,1)S(1)} %get-tuple-element.74), channel_id=1, source_target_pairs={{0,12},{1,13},{2,14},{3,15},{4,8},{5,9},{6,10},{7,11},{8,4},{9,5},... | collective-permute-start | bytes 405512 | tf_op jit(solution)/shard_map/ppermute | solution.py:94
  47.9 6.7 %collective-permute-start.16 = (bf16[2,176,256]{2,1,0:T(8,128)(2,1)S(1)}, bf16[2,176,256]{2,1,0:T(8,128)(2,1)S(1)}, u32[]{:S(2)}, u32[]{:S(2)}) collective-permute-start(bf16[2,176,256]{2,1,0:T(8,128)(2,1)S(1)} %get-tuple-element.86), channel_id=1, source_target_pairs={{0,2},{1,3},{2,0},{3,1},{4,6},{5,7},{6,4},{7,5},{8,10},{9,11},{10,... | collective-permute-start | bytes 540680 | tf_op jit(solution)/shard_map/ppermute | solution.py:94
  48.3 9.3 %collective-permute-start.19 = (bf16[2,176,256]{2,1,0:T(8,128)(2,1)S(1)}, bf16[2,176,256]{2,1,0:T(8,128)(2,1)S(1)}, u32[]{:S(2)}, u32[]{:S(2)}) collective-permute-start(bf16[2,176,256]{2,1,0:T(8,128)(2,1)S(1)} %get-tuple-element.92), channel_id=1, source_target_pairs={{0,2},{1,3},{2,0},{3,1},{4,6},{5,7},{6,4},{7,5},{8,10},{9,11},{10,... | collective-permute-start | bytes 540680 | tf_op jit(solution)/shard_map/ppermute | solution.py:94
  52.8 7.5 %collective-permute-start.23 = (bf16[176,384]{1,0:T(8,128)(2,1)S(1)}, bf16[176,384]{1,0:T(8,128)(2,1)S(1)}, u32[]{:S(2)}, u32[]{:S(2)}) collective-permute-start(bf16[176,384]{1,0:T(8,128)(2,1)S(1)} %get-tuple-element.98), channel_id=1, source_target_pairs={{0,12},{4,0},{8,4},{12,8},{16,28},{20,16},{24,20},{28,24},{1,13},{... | collective-permute-start | bytes 405512 | tf_op jit(solution)/shard_map/ppermute | solution.py:98
  52.9 9.4 %collective-permute-start.24 = (bf16[176,384]{1,0:T(8,128)(2,1)S(1)}, bf16[176,384]{1,0:T(8,128)(2,1)S(1)}, u32[]{:S(2)}, u32[]{:S(2)}) collective-permute-start(bf16[176,384]{1,0:T(8,128)(2,1)S(1)} %get-tuple-element.99), channel_id=1, source_target_pairs={{0,8},{4,12},{8,0},{12,4},{16,24},{20,28},{24,16},{28,20},{1,9},{5... | collective-permute-start | bytes 405512 | tf_op jit(solution)/shard_map/ppermute | solution.py:98
  54.1 10.3 %collective-permute-start.25 = (bf16[176,384]{1,0:T(8,128)(2,1)S(1)}, bf16[176,384]{1,0:T(8,128)(2,1)S(1)}, u32[]{:S(2)}, u32[]{:S(2)}) collective-permute-start(bf16[176,384]{1,0:T(8,128)(2,1)S(1)} %get-tuple-element.100), channel_id=1, source_target_pairs={{0,4},{4,8},{8,12},{12,0},{16,20},{20,24},{24,28},{28,16},{1,5},{5... | collective-permute-start | bytes 405512 | tf_op jit(solution)/shard_map/ppermute | solution.py:98
  54.6 10.9 %collective-permute-start.17 = (bf16[176,256]{1,0:T(8,128)(2,1)S(1)}, bf16[176,256]{1,0:T(8,128)(2,1)S(1)}, u32[]{:S(2)}, u32[]{:S(2)}) collective-permute-start(bf16[176,256]{1,0:T(8,128)(2,1)S(1)} %get-tuple-element.87), channel_id=1, source_target_pairs={{0,16},{1,24},{2,18},{3,26},{4,20},{5,28},{6,22},{7,30},{8,17},{9,... | collective-permute-start | bytes 270344 | tf_op jit(solution)/shard_map/ppermute | solution.py:94
  57.6 8.8 %collective-permute-start.18 = (bf16[176,256]{1,0:T(8,128)(2,1)S(1)}, bf16[176,256]{1,0:T(8,128)(2,1)S(1)}, u32[]{:S(2)}, u32[]{:S(2)}) collective-permute-start(bf16[176,256]{1,0:T(8,128)(2,1)S(1)} %get-tuple-element.88), channel_id=1, source_target_pairs={{0,20},{1,28},{2,22},{3,30},{4,16},{5,24},{6,18},{7,26},{8,21},{9,... | collective-permute-start | bytes 270344 | tf_op jit(solution)/shard_map/ppermute | solution.py:94
  60.4 7.4 %collective-permute-start.20 = (bf16[176,256]{1,0:T(8,128)(2,1)S(1)}, bf16[176,256]{1,0:T(8,128)(2,1)S(1)}, u32[]{:S(2)}, u32[]{:S(2)}) collective-permute-start(bf16[176,256]{1,0:T(8,128)(2,1)S(1)} %get-tuple-element.93), channel_id=1, source_target_pairs={{0,0},{1,8},{2,2},{3,10},{4,4},{5,12},{6,6},{7,14},{8,1},{9,9},{10... | collective-permute-start | bytes 270344 | tf_op jit(solution)/shard_map/ppermute | solution.py:94
  62.3 7.0 %collective-permute-start.21 = (bf16[176,256]{1,0:T(8,128)(2,1)S(1)}, bf16[176,256]{1,0:T(8,128)(2,1)S(1)}, u32[]{:S(2)}, u32[]{:S(2)}) collective-permute-start(bf16[176,256]{1,0:T(8,128)(2,1)S(1)} %get-tuple-element.94), channel_id=1, source_target_pairs={{0,4},{1,12},{2,6},{3,14},{4,0},{5,8},{6,2},{7,10},{8,5},{9,13},{1... | collective-permute-start | bytes 270344 | tf_op jit(solution)/shard_map/ppermute | solution.py:94
  (5 other events, 62.5 us)

commit v4 on v3

--- a/solution.py
+++ b/solution.py
@@ -324,20 +324,21 @@
     )
     own0, own1 = call(functools.partial(cut_kernel, unit), "cut", (pos, pos), (acts,), mib=8)
     dz_h, dz_z, dz_y = send(dz, SWAP_H), send(dz, SWAP_Z), send(along, SWAP_Y)
-    t11, t01 = send(own1, turn(1, 1)), send(own1, turn(0, 1))
-
+    w0, w2, w4, wd = call(functools.partial(units_kernel, unit), "units", (weight,) * 4, (filters,), mib=4)
+    t01, t00 = send(own1, turn(0, 1)), send(own0, turn(0, 0))
     dz_zy = send(dz_z, SWAP_Y)
-    dz_h, dz_y, t11, t01, own0, filters = tie((dz_h, dz_y, t11, t01, own0, filters))
+    near_got = call(join_kernel, "join_near", shape((2, unit, rows), BF16), (t00, t01), mib=4)
+    far_got = send(near_got, SWAP_H)
+    dz_h, dz_y, wd, w2 = tie((dz_h, dz_y, wd, w2))
     dz_hz, dz_hy = send(dz_h, SWAP_Z), send(dz_h, SWAP_Y)
-    t10, t00 = send(own0, turn(1, 0)), send(own0, turn(0, 0))
-    units = call(functools.partial(units_kernel, unit), "units", (weight,) * 4, (filters,), mib=4)
-
-    dz_hz, dz_zy, dz_hy, t10, t00, *units = tie((dz_hz, dz_zy, dz_hy, t10, t00, *units))
-    got = call(join_kernel, "join", shape((4, unit, rows), BF16), (t00, t01, t10, t11), mib=4)
+    wd = send(wd, SWAP_ZY)
+
+    dz_hz, dz_zy, dz_hy, wd, w2, far_got = tie((dz_hz, dz_zy, dz_hy, wd, w2, far_got))
+    got = call(join_kernel, "join", shape((2, 2, unit, rows), BF16), (near_got, far_got), mib=4)
+    got = got.reshape(4, unit, rows)
     other = send(got, SWAP_X)
     dz_hzy = send(dz_hz, SWAP_Y)
-    w0, w2, w4, wd = units
-    w2, wd = send(w2, SWAP_Z), send(wd, SWAP_ZY)
+    w2 = send(w2, SWAP_Z)
     far = send(got, SWAP_C)
 
     weights = (w0, w2, w4, wd, dz_y)

time: 70.2 us -> 67.6 us (0.963)
  starting transfers between devices: 34.6 us -> 32.5 us
  waiting for transfers between devices: 22.8 us -> 22 us
    ppermute x23 -> x22, starting transfers between devices: 32.9 us -> 29.9 us  [send(): return lax.ppermute(value, ('seq', 'section'), pairs)]
    ppermute x3, starting transfers between devices: 1.7 us -> 2.62 us  [in_half(): lax.ppermute(value, 'seq', [(i, 4 * (i // 4) + (i % 4 + step) % 4) for i...]
    ppermute x23 -> x22, waiting for transfers between devices: 22.7 us -> 22 us  [send(): return lax.ppermute(value, ('seq', 'section'), pairs)]
    pallas_call x15 -> x16, Pallas kernels: 10.7 us -> 10.7 us  [call(): pl.pallas_call(kernel, out_shape=shapes, in_specs=[pl.BlockSpec(memory_sp...]
  transfers between devices with their start and end apart: 26 -> 25, of which waited for: 11 -> 11; matrix products, arithmetic and copies ran while one was open for 0% -> 0% of each run, Pallas kernels for 9% -> 10%
where the time goes in v4:
time: 67.6 us; the launch traced here: 67 us
  starting transfers between devices  32.5 us (48%)
  waiting for transfers between devices  22 us (33%)
  Pallas kernels  10.7 us (16%)
  local copies, waits for them, and re-layouts  1.12 us (2%)
  between operations  0.78 us (1%)
    ppermute x22, starting transfers between devices, send(): return lax.ppermute(value, ('seq', 'section'), pairs)  29.9 us
    ppermute x22, waiting for transfers between devices, send(): return lax.ppermute(value, ('seq', 'section'), pairs)  22 us
    pallas_call x16, Pallas kernels, call(): pl.pallas_call(kernel, out_shape=shapes, in_specs=[pl.BlockSpec(memory_sp...  10.7 us
    ppermute x3, starting transfers between devices, in_half(): lax.ppermute(value, 'seq', [(i, 4 * (i // 4) + (i % 4 + step) % 4) for i...  2.62 us
  transfers between devices with their start and end apart: 25, of which 11 were waited for; matrix products, arithmetic and copies ran while one was open for 0% of the time, Pallas kernels for 10%

profile of v4, /device:TPU:1, one launch (start us, length us, event | category | flops | bytes accessed | tf_op | source)
XLA Modules:
  0.0 67.0 jit_solution(5485635383929478296)
XLA Ops:
  0.6 2.2 %dz.1 = (bf16[256,384]{1,0:T(8,128)(2,1)}, bf16[432,384]{1,0:T(8,128)(2,1)}) custom-call(bf16[256,384]{1,0:T(8,128)(2,1)} %pre_hbm.1, bf16[128,384]{1,0:T(8,128)(2,1)} %emb_hbm.1, bf16[880,384]{1,0:T(8,128)(2,1)} %filters_ref.1), custom_call_target="tpu_custom_call" | custom-call | bytes 1024 | tf_op jit(solution)/shard_map/dz/pallas_call | solution.py:288
  2.9 2.1 %collective-permute-start.1 = (bf16[432,384]{1,0:T(8,128)(2,1)}, bf16[432,384]{1,0:T(8,128)(2,1)S(1)}, u32[]{:S(2)}, u32[]{:S(2)}) collective-permute-start(bf16[432,384]{1,0:T(8,128)(2,1)} %get-tuple-element.48), channel_id=1, source_target_pairs={{0,4},{1,5},{2,6},{3,7},{4,0},{5,1},{6,2},{7,3},{8,12},{9,13},{10,... | collective-permute-start | bytes 995336 | tf_op jit(solution)/shard_map/ppermute | solution.py:94
  5.0 1.3 %collective-permute-start.2 = (bf16[256,384]{1,0:T(8,128)(2,1)}, bf16[256,384]{1,0:T(8,128)(2,1)S(1)}, u32[]{:S(2)}, u32[]{:S(2)}) collective-permute-start(bf16[256,384]{1,0:T(8,128)(2,1)} %get-tuple-element.47.refs_0_), channel_id=1, source_target_pairs={{0,8},{1,9},{2,10},{3,11},{4,12},{5,13},{6,14},{7,15},{8,0},{9,1},... | collective-permute-start | bytes 589832 | tf_op jit(solution)/shard_map/ppermute | solution.py:94
  6.3 2.3 %collective-permute-start = (bf16[256,384]{1,0:T(8,128)(2,1)}, bf16[256,384]{1,0:T(8,128)(2,1)S(1)}, u32[]{:S(2)}, u32[]{:S(2)}) collective-permute-start(bf16[256,384]{1,0:T(8,128)(2,1)} %get-tuple-element.47.refs_0_), channel_id=1, source_target_pairs={{0,16},{1,17},{2,18},{3,19},{4,20},{5,21},{6,22},{7,23},{8,24},{9,... | collective-permute-start | bytes 589832 | tf_op jit(solution)/shard_map/ppermute | solution.py:94
  10.1 3.4 %collective-permute-start.7 = (bf16[176,256]{1,0:T(8,128)(2,1)S(1)}, bf16[176,256]{1,0:T(8,128)(2,1)S(1)}, u32[]{:S(2)}, u32[]{:S(2)}) collective-permute-start(bf16[176,256]{1,0:T(8,128)(2,1)S(1)} %get-tuple-element.55), channel_id=1, source_target_pairs={{0,0},{1,8},{2,2},{3,10},{4,4},{5,12},{6,6},{7,14},{8,1},{9,9},{10... | collective-permute-start | bytes 270344 | tf_op jit(solution)/shard_map/ppermute | solution.py:94
  13.9 1.3 %collective-permute-start.4 = (bf16[256,384]{1,0:T(8,128)(2,1)S(1)}, bf16[256,384]{1,0:T(8,128)(2,1)S(1)}, u32[]{:S(2)}, u32[]{:S(2)}) collective-permute-start(bf16[256,384]{1,0:T(8,128)(2,1)S(1)} %collective-permute-done.2.refs_2_), channel_id=1, source_target_pairs={{0,4},{1,5},{2,6},{3,7},{4,0},{5,1},{6,2},{7,3},{8,12},{9,13},{10,... | collective-permute-start | bytes 589832 | tf_op jit(solution)/shard_map/ppermute | solution.py:94
  15.2 2.1 %collective-permute-start.3 = (bf16[256,384]{1,0:T(8,128)(2,1)S(1)}, bf16[256,384]{1,0:T(8,128)(2,1)S(1)}, u32[]{:S(2)}, u32[]{:S(2)}) collective-permute-start(bf16[256,384]{1,0:T(8,128)(2,1)S(1)} %collective-permute-done.refs_4_), channel_id=1, source_target_pairs={{0,8},{1,9},{2,10},{3,11},{4,12},{5,13},{6,14},{7,15},{8,0},{9,1},... | collective-permute-start | bytes 589832 | tf_op jit(solution)/shard_map/ppermute | solution.py:94
  17.5 1.5 %collective-permute-done.8.refs_1_ = bf16[176,256]{1,0:T(8,128)(2,1)S(1)} collective-permute-done((bf16[176,256]{1,0:T(8,128)(2,1)S(1)}, bf16[176,256]{1,0:T(8,128)(2,1)S(1)}, u32[]{:S(2)}, u32[]{:S(2)}) %collective-permute-start.8) | collective-permute-done | bytes 90144 | tf_op jit(solution)/shard_map/ppermute | solution.py:94
  18.9 2.0 %collective-permute-start.9 = (bf16[2,176,256]{2,1,0:T(8,128)(2,1)S(1)}, bf16[2,176,256]{2,1,0:T(8,128)(2,1)S(1)}, u32[]{:S(2)}, u32[]{:S(2)}) collective-permute-start(bf16[2,176,256]{2,1,0:T(8,128)(2,1)S(1)} %join_near.1.refs_0_), channel_id=1, source_target_pairs={{0,16},{1,17},{2,18},{3,19},{4,20},{5,21},{6,22},{7,23},{8,24},{9,... | collective-permute-start | bytes 540680 | tf_op jit(solution)/shard_map/ppermute | solution.py:94
  20.9 6.3 %collective-permute-done.9.refs_1_ = bf16[2,176,256]{2,1,0:T(8,128)(2,1)S(1)} collective-permute-done((bf16[2,176,256]{2,1,0:T(8,128)(2,1)S(1)}, bf16[2,176,256]{2,1,0:T(8,128)(2,1)S(1)}, u32[]{:S(2)}, u32[]{:S(2)}) %collective-permute-start.9) | collective-permute-done | bytes 180256 | tf_op jit(solution)/shard_map/ppermute | solution.py:94
  27.2 3.4 %collective-permute-done.6.refs_3_ = bf16[176,384]{1,0:T(8,128)(2,1)S(1)} collective-permute-done((bf16[176,384]{1,0:T(8,128)(2,1)S(1)}, bf16[176,384]{1,0:T(8,128)(2,1)S(1)}, u32[]{:S(2)}, u32[]{:S(2)}) %collective-permute-start.6) | collective-permute-done | bytes 135200 | tf_op jit(solution)/shard_map/ppermute | solution.py:94
  30.7 1.3 %collective-permute-start.11 = (bf16[4,176,256]{2,1,0:T(8,128)(2,1)S(1)}, bf16[4,176,256]{2,1,0:T(8,128)(2,1)S(1)}, u32[]{:S(2)}, u32[]{:S(2)}) collective-permute-start(bf16[4,176,256]{2,1,0:T(8,128)(2,1)S(1)} %bitcast.2), channel_id=1, source_target_pairs={{0,2},{1,3},{2,0},{3,1},{4,6},{5,7},{6,4},{7,5},{8,10},{9,11},{10,... | collective-permute-start | bytes 1081352 | tf_op jit(solution)/shard_map/ppermute | solution.py:94
  34.5 4.6 %collective-permute-done.13.refs_1_ = bf16[176,384]{1,0:T(8,128)(2,1)S(1)} collective-permute-done((bf16[176,384]{1,0:T(8,128)(2,1)S(1)}, bf16[176,384]{1,0:T(8,128)(2,1)S(1)}, u32[]{:S(2)}, u32[]{:S(2)}) %collective-permute-start.13) | collective-permute-done | bytes 135200 | tf_op jit(solution)/shard_map/ppermute | solution.py:94
  39.8 1.3 %away.1 = (bf16[2080,384]{1,0:T(8,128)(2,1)S(1)}, bf16[880,384]{1,0:T(8,128)(2,1)S(1)}, bf16[2,2,2,176,256]{4,3,2,1,0:T(8,128)(2,1)S(1)}) custom-call(bf16[2080,384]{1,0:T(8,128)(2,1)S(1)} %gather.1.most_ref, bf16[256,384]{1,0:T(8,128)(2,1)S(1)} %collective-permute-done.10.dz_last, ...), custom_call_target="tpu_custom_call", output_to_operand_aliasing={{0}: (0, {})} | custom-call | bytes 1024 | tf_op jit(solution)/shard_map/away/pallas_call | solution.py:288
  41.1 1.8 %collective-permute-start.14 = (bf16[2,2,2,176,256]{4,3,2,1,0:T(8,128)(2,1)S(1)}, bf16[2,2,2,176,256]{4,3,2,1,0:T(8,128)(2,1)S(1)}, u32[]{:S(2)}, u32[]{:S(2)}) collective-permute-start(bf16[2,2,2,176,256]{4,3,2,1,0:T(8,128)(2,1)S(1)} %get-tuple-element.73), channel_id=1, source_target_pairs={{0,1},{1,0},{2,3},{3,2},{4,5},{5,4},{6,7},{7,6},{8,9},{9,8},{10,11... | collective-permute-start | bytes 2162696 | tf_op jit(solution)/shard_map/ppermute | solution.py:94
  43.0 1.2 %keep.1.keep_ref = f32[2,2,2,176,256]{4,3,2,1,0:T(8,128)S(1)} custom-call(bf16[2080,384]{1,0:T(8,128)(2,1)S(1)} %get-tuple-element.71.dz_ref, bf16[880,384]{1,0:T(8,128)(2,1)S(1)} %get-tuple-element.72.weights), custom_call_target="tpu_custom_call" | custom-call | bytes 1024 | tf_op jit(solution)/shard_map/keep/pallas_call | solution.py:288
  44.8 1.3 %collective-permute-start.15 = (bf16[2,176,256]{2,1,0:T(8,128)(2,1)S(1)}, bf16[2,176,256]{2,1,0:T(8,128)(2,1)S(1)}, u32[]{:S(2)}, u32[]{:S(2)}) collective-permute-start(bf16[2,176,256]{2,1,0:T(8,128)(2,1)S(1)} %get-tuple-element.76), channel_id=1, source_target_pairs={{0,2},{1,3},{2,0},{3,1},{4,6},{5,7},{6,4},{7,5},{8,10},{9,11},{10,... | collective-permute-start | bytes 540680 | tf_op jit(solution)/shard_map/ppermute | solution.py:94
  47.6 2.1 %filter.1 = (f32[176,384]{1,0:T(8,128)S(1)}, bf16[176,384]{1,0:T(8,128)(2,1)S(1)}, bf16[176,384]{1,0:T(8,128)(2,1)S(1)}, bf16[176,384]{1,0:T(8,128)(2,1)S(1)}, f32[176,384]{1,0:T(8,128)S(1)}) custom-call(bf16[5,176,2048]{2,1,0:T(8,128)(2,1)S(1)} %left.1.left_ref, bf16[2080,384]{1,0:T(8,128)(2,1)S(1)} %get-tuple-element.71.dz_ref), custom_call_target="tpu_custom_call" | custom-call | bytes 1024 | tf_op jit(solution)/shard_map/filter/pallas_call | solution.py:288
  49.8 2.6 %collective-permute-start.23 = (bf16[176,384]{1,0:T(8,128)(2,1)S(1)}, bf16[176,384]{1,0:T(8,128)(2,1)S(1)}, u32[]{:S(2)}, u32[]{:S(2)}) collective-permute-start(bf16[176,384]{1,0:T(8,128)(2,1)S(1)} %get-tuple-element.89), channel_id=1, source_target_pairs={{0,8},{4,12},{8,0},{12,4},{16,24},{20,28},{24,16},{28,20},{1,9},{5... | collective-permute-start | bytes 405512 | tf_op jit(solution)/shard_map/ppermute | solution.py:98
  52.4 1.6 %collective-permute-start.16 = (bf16[176,256]{1,0:T(8,128)(2,1)S(1)}, bf16[176,256]{1,0:T(8,128)(2,1)S(1)}, u32[]{:S(2)}, u32[]{:S(2)}) collective-permute-start(bf16[176,256]{1,0:T(8,128)(2,1)S(1)} %get-tuple-element.77), channel_id=1, source_target_pairs={{0,16},{1,24},{2,18},{3,26},{4,20},{5,28},{6,22},{7,30},{8,17},{9,... | collective-permute-start | bytes 270344 | tf_op jit(solution)/shard_map/ppermute | solution.py:94
  54.5 2.4 %collective-permute-start.17 = (bf16[176,256]{1,0:T(8,128)(2,1)S(1)}, bf16[176,256]{1,0:T(8,128)(2,1)S(1)}, u32[]{:S(2)}, u32[]{:S(2)}) collective-permute-start(bf16[176,256]{1,0:T(8,128)(2,1)S(1)} %get-tuple-element.78), channel_id=1, source_target_pairs={{0,20},{1,28},{2,22},{3,30},{4,16},{5,24},{6,18},{7,26},{8,21},{9,... | collective-permute-start | bytes 270344 | tf_op jit(solution)/shard_map/ppermute | solution.py:94
  57.0 3.2 %collective-permute-start.19 = (bf16[176,256]{1,0:T(8,128)(2,1)S(1)}, bf16[176,256]{1,0:T(8,128)(2,1)S(1)}, u32[]{:S(2)}, u32[]{:S(2)}) collective-permute-start(bf16[176,256]{1,0:T(8,128)(2,1)S(1)} %get-tuple-element.83), channel_id=1, source_target_pairs={{0,0},{1,8},{2,2},{3,10},{4,4},{5,12},{6,6},{7,14},{8,1},{9,9},{10... | collective-permute-start | bytes 270344 | tf_op jit(solution)/shard_map/ppermute | solution.py:94
  62.5 2.2 %collective-permute-done.19.refs_2_ = bf16[176,256]{1,0:T(8,128)(2,1)S(1)} collective-permute-done((bf16[176,256]{1,0:T(8,128)(2,1)S(1)}, bf16[176,256]{1,0:T(8,128)(2,1)S(1)}, u32[]{:S(2)}, u32[]{:S(2)}) %collective-permute-start.19) | collective-permute-done | bytes 90144 | tf_op jit(solution)/shard_map/ppermute | solution.py:94
  64.7 1.6 %collective-permute-done.20.refs_3_ = bf16[176,256]{1,0:T(8,128)(2,1)S(1)} collective-permute-done((bf16[176,256]{1,0:T(8,128)(2,1)S(1)}, bf16[176,256]{1,0:T(8,128)(2,1)S(1)}, u32[]{:S(2)}, u32[]{:S(2)}) %collective-permute-start.20) | collective-permute-done | bytes 90144 | tf_op jit(solution)/shard_map/ppermute | solution.py:94
  (48 shorter events, 11.3 us)
Async XLA Ops:
  2.9 12.3 %collective-permute-start.1 = (bf16[432,384]{1,0:T(8,128)(2,1)}, bf16[432,384]{1,0:T(8,128)(2,1)S(1)}, u32[]{:S(2)}, u32[]{:S(2)}) collective-permute-start(bf16[432,384]{1,0:T(8,128)(2,1)} %get-tuple-element.48), channel_id=1, source_target_pairs={{0,4},{1,5},{2,6},{3,7},{4,0},{5,1},{6,2},{7,3},{8,12},{9,13},{10,... | collective-permute-start | bytes 995336 | tf_op jit(solution)/shard_map/ppermute | solution.py:94
  5.0 8.9 %collective-permute-start.2 = (bf16[256,384]{1,0:T(8,128)(2,1)}, bf16[256,384]{1,0:T(8,128)(2,1)S(1)}, u32[]{:S(2)}, u32[]{:S(2)}) collective-permute-start(bf16[256,384]{1,0:T(8,128)(2,1)} %get-tuple-element.47.refs_0_), channel_id=1, source_target_pairs={{0,8},{1,9},{2,10},{3,11},{4,12},{5,13},{6,14},{7,15},{8,0},{9,1},... | collective-permute-start | bytes 589832 | tf_op jit(solution)/shard_map/ppermute | solution.py:94
  6.3 8.9 %collective-permute-start = (bf16[256,384]{1,0:T(8,128)(2,1)}, bf16[256,384]{1,0:T(8,128)(2,1)S(1)}, u32[]{:S(2)}, u32[]{:S(2)}) collective-permute-start(bf16[256,384]{1,0:T(8,128)(2,1)} %get-tuple-element.47.refs_0_), channel_id=1, source_target_pairs={{0,16},{1,17},{2,18},{3,19},{4,20},{5,21},{6,22},{7,23},{8,24},{9,... | collective-permute-start | bytes 589832 | tf_op jit(solution)/shard_map/ppermute | solution.py:94
  10.1 7.3 %collective-permute-start.7 = (bf16[176,256]{1,0:T(8,128)(2,1)S(1)}, bf16[176,256]{1,0:T(8,128)(2,1)S(1)}, u32[]{:S(2)}, u32[]{:S(2)}) collective-permute-start(bf16[176,256]{1,0:T(8,128)(2,1)S(1)} %get-tuple-element.55), channel_id=1, source_target_pairs={{0,0},{1,8},{2,2},{3,10},{4,4},{5,12},{6,6},{7,14},{8,1},{9,9},{10... | collective-permute-start | bytes 270344 | tf_op jit(solution)/shard_map/ppermute | solution.py:94
  13.5 5.4 %collective-permute-start.8 = (bf16[176,256]{1,0:T(8,128)(2,1)S(1)}, bf16[176,256]{1,0:T(8,128)(2,1)S(1)}, u32[]{:S(2)}, u32[]{:S(2)}) collective-permute-start(bf16[176,256]{1,0:T(8,128)(2,1)S(1)} %get-tuple-element.56), channel_id=1, source_target_pairs={{0,4},{1,12},{2,6},{3,14},{4,0},{5,8},{6,2},{7,10},{8,5},{9,13},{1... | collective-permute-start | bytes 270344 | tf_op jit(solution)/shard_map/ppermute | solution.py:94
  13.9 13.3 %collective-permute-start.4 = (bf16[256,384]{1,0:T(8,128)(2,1)S(1)}, bf16[256,384]{1,0:T(8,128)(2,1)S(1)}, u32[]{:S(2)}, u32[]{:S(2)}) collective-permute-start(bf16[256,384]{1,0:T(8,128)(2,1)S(1)} %collective-permute-done.2.refs_2_), channel_id=1, source_target_pairs={{0,4},{1,5},{2,6},{3,7},{4,0},{5,1},{6,2},{7,3},{8,12},{9,13},{10,... | collective-permute-start | bytes 589832 | tf_op jit(solution)/shard_map/ppermute | solution.py:94
  15.2 15.5 %collective-permute-start.3 = (bf16[256,384]{1,0:T(8,128)(2,1)S(1)}, bf16[256,384]{1,0:T(8,128)(2,1)S(1)}, u32[]{:S(2)}, u32[]{:S(2)}) collective-permute-start(bf16[256,384]{1,0:T(8,128)(2,1)S(1)} %collective-permute-done.refs_4_), channel_id=1, source_target_pairs={{0,8},{1,9},{2,10},{3,11},{4,12},{5,13},{6,14},{7,15},{8,0},{9,1},... | collective-permute-start | bytes 589832 | tf_op jit(solution)/shard_map/ppermute | solution.py:94
  17.2 13.4 %collective-permute-start.5 = (bf16[256,384]{1,0:T(8,128)(2,1)S(1)}, bf16[256,384]{1,0:T(8,128)(2,1)S(1)}, u32[]{:S(2)}, u32[]{:S(2)}) collective-permute-start(bf16[256,384]{1,0:T(8,128)(2,1)S(1)} %collective-permute-done.refs_4_), channel_id=1, source_target_pairs={{0,4},{1,5},{2,6},{3,7},{4,0},{5,1},{6,2},{7,3},{8,12},{9,13},{10,... | collective-permute-start | bytes 589832 | tf_op jit(solution)/shard_map/ppermute | solution.py:94
  18.9 8.2 %collective-permute-start.9 = (bf16[2,176,256]{2,1,0:T(8,128)(2,1)S(1)}, bf16[2,176,256]{2,1,0:T(8,128)(2,1)S(1)}, u32[]{:S(2)}, u32[]{:S(2)}) collective-permute-start(bf16[2,176,256]{2,1,0:T(8,128)(2,1)S(1)} %join_near.1.refs_0_), channel_id=1, source_target_pairs={{0,16},{1,17},{2,18},{3,19},{4,20},{5,21},{6,22},{7,23},{8,24},{9,... | collective-permute-start | bytes 540680 | tf_op jit(solution)/shard_map/ppermute | solution.py:94
  20.9 9.7 %collective-permute-start.6 = (bf16[176,384]{1,0:T(8,128)(2,1)S(1)}, bf16[176,384]{1,0:T(8,128)(2,1)S(1)}, u32[]{:S(2)}, u32[]{:S(2)}) collective-permute-start(bf16[176,384]{1,0:T(8,128)(2,1)S(1)} %get-tuple-element.53), channel_id=1, source_target_pairs={{0,12},{1,13},{2,14},{3,15},{4,8},{5,9},{6,10},{7,11},{8,4},{9,5},... | collective-permute-start | bytes 405512 | tf_op jit(solution)/shard_map/ppermute | solution.py:94
  30.7 9.2 %collective-permute-start.11 = (bf16[4,176,256]{2,1,0:T(8,128)(2,1)S(1)}, bf16[4,176,256]{2,1,0:T(8,128)(2,1)S(1)}, u32[]{:S(2)}, u32[]{:S(2)}) collective-permute-start(bf16[4,176,256]{2,1,0:T(8,128)(2,1)S(1)} %bitcast.2), channel_id=1, source_target_pairs={{0,2},{1,3},{2,0},{3,1},{4,6},{5,7},{6,4},{7,5},{8,10},{9,11},{10,... | collective-permute-start | bytes 1081352 | tf_op jit(solution)/shard_map/ppermute | solution.py:94
  31.9 7.9 %collective-permute-start.12 = (bf16[4,176,256]{2,1,0:T(8,128)(2,1)S(1)}, bf16[4,176,256]{2,1,0:T(8,128)(2,1)S(1)}, u32[]{:S(2)}, u32[]{:S(2)}) collective-permute-start(bf16[4,176,256]{2,1,0:T(8,128)(2,1)S(1)} %bitcast.3), channel_id=1, source_target_pairs={{0,1},{1,0},{2,3},{3,2},{4,5},{5,4},{6,7},{7,6},{8,9},{9,8},{10,11... | collective-permute-start | bytes 1081352 | tf_op jit(solution)/shard_map/ppermute | solution.py:94
  33.1 6.5 %collective-permute-start.10 = (bf16[256,384]{1,0:T(8,128)(2,1)S(1)}, bf16[256,384]{1,0:T(8,128)(2,1)S(1)}, u32[]{:S(2)}, u32[]{:S(2)}) collective-permute-start(bf16[256,384]{1,0:T(8,128)(2,1)S(1)} %collective-permute-done.3.refs_6_), channel_id=1, source_target_pairs={{0,4},{1,5},{2,6},{3,7},{4,0},{5,1},{6,2},{7,3},{8,12},{9,13},{10,... | collective-permute-start | bytes 589832 | tf_op jit(solution)/shard_map/ppermute | solution.py:94
  34.2 4.9 %collective-permute-start.13 = (bf16[176,384]{1,0:T(8,128)(2,1)S(1)}, bf16[176,384]{1,0:T(8,128)(2,1)S(1)}, u32[]{:S(2)}, u32[]{:S(2)}) collective-permute-start(bf16[176,384]{1,0:T(8,128)(2,1)S(1)} %get-tuple-element.62), channel_id=1, source_target_pairs={{0,8},{1,9},{2,10},{3,11},{4,12},{5,13},{6,14},{7,15},{8,0},{9,1},... | collective-permute-start | bytes 405512 | tf_op jit(solution)/shard_map/ppermute | solution.py:94
  41.1 3.6 %collective-permute-start.14 = (bf16[2,2,2,176,256]{4,3,2,1,0:T(8,128)(2,1)S(1)}, bf16[2,2,2,176,256]{4,3,2,1,0:T(8,128)(2,1)S(1)}, u32[]{:S(2)}, u32[]{:S(2)}) collective-permute-start(bf16[2,2,2,176,256]{4,3,2,1,0:T(8,128)(2,1)S(1)} %get-tuple-element.73), channel_id=1, source_target_pairs={{0,1},{1,0},{2,3},{3,2},{4,5},{5,4},{6,7},{7,6},{8,9},{9,8},{10,11... | collective-permute-start | bytes 2162696 | tf_op jit(solution)/shard_map/ppermute | solution.py:94
  44.8 7.6 %collective-permute-start.15 = (bf16[2,176,256]{2,1,0:T(8,128)(2,1)S(1)}, bf16[2,176,256]{2,1,0:T(8,128)(2,1)S(1)}, u32[]{:S(2)}, u32[]{:S(2)}) collective-permute-start(bf16[2,176,256]{2,1,0:T(8,128)(2,1)S(1)} %get-tuple-element.76), channel_id=1, source_target_pairs={{0,2},{1,3},{2,0},{3,1},{4,6},{5,7},{6,4},{7,5},{8,10},{9,11},{10,... | collective-permute-start | bytes 540680 | tf_op jit(solution)/shard_map/ppermute | solution.py:94
  46.2 8.3 %collective-permute-start.18 = (bf16[2,176,256]{2,1,0:T(8,128)(2,1)S(1)}, bf16[2,176,256]{2,1,0:T(8,128)(2,1)S(1)}, u32[]{:S(2)}, u32[]{:S(2)}) collective-permute-start(bf16[2,176,256]{2,1,0:T(8,128)(2,1)S(1)} %get-tuple-element.82), channel_id=1, source_target_pairs={{0,2},{1,3},{2,0},{3,1},{4,6},{5,7},{6,4},{7,5},{8,10},{9,11},{10,... | collective-permute-start | bytes 540680 | tf_op jit(solution)/shard_map/ppermute | solution.py:94
  49.8 7.2 %collective-permute-start.22 = (bf16[176,384]{1,0:T(8,128)(2,1)S(1)}, bf16[176,384]{1,0:T(8,128)(2,1)S(1)}, u32[]{:S(2)}, u32[]{:S(2)}) collective-permute-start(bf16[176,384]{1,0:T(8,128)(2,1)S(1)} %get-tuple-element.88), channel_id=1, source_target_pairs={{0,12},{4,0},{8,4},{12,8},{16,28},{20,16},{24,20},{28,24},{1,13},{... | collective-permute-start | bytes 405512 | tf_op jit(solution)/shard_map/ppermute | solution.py:98
  49.8 10.4 %collective-permute-start.23 = (bf16[176,384]{1,0:T(8,128)(2,1)S(1)}, bf16[176,384]{1,0:T(8,128)(2,1)S(1)}, u32[]{:S(2)}, u32[]{:S(2)}) collective-permute-start(bf16[176,384]{1,0:T(8,128)(2,1)S(1)} %get-tuple-element.89), channel_id=1, source_target_pairs={{0,8},{4,12},{8,0},{12,4},{16,24},{20,28},{24,16},{28,20},{1,9},{5... | collective-permute-start | bytes 405512 | tf_op jit(solution)/shard_map/ppermute | solution.py:98
  52.4 8.4 %collective-permute-start.24 = (bf16[176,384]{1,0:T(8,128)(2,1)S(1)}, bf16[176,384]{1,0:T(8,128)(2,1)S(1)}, u32[]{:S(2)}, u32[]{:S(2)}) collective-permute-start(bf16[176,384]{1,0:T(8,128)(2,1)S(1)} %get-tuple-element.90), channel_id=1, source_target_pairs={{0,4},{4,8},{8,12},{12,0},{16,20},{20,24},{24,28},{28,16},{1,5},{5... | collective-permute-start | bytes 405512 | tf_op jit(solution)/shard_map/ppermute | solution.py:98
  52.4 9.5 %collective-permute-start.16 = (bf16[176,256]{1,0:T(8,128)(2,1)S(1)}, bf16[176,256]{1,0:T(8,128)(2,1)S(1)}, u32[]{:S(2)}, u32[]{:S(2)}) collective-permute-start(bf16[176,256]{1,0:T(8,128)(2,1)S(1)} %get-tuple-element.77), channel_id=1, source_target_pairs={{0,16},{1,24},{2,18},{3,26},{4,20},{5,28},{6,22},{7,30},{8,17},{9,... | collective-permute-start | bytes 270344 | tf_op jit(solution)/shard_map/ppermute | solution.py:94
  54.5 8.0 %collective-permute-start.17 = (bf16[176,256]{1,0:T(8,128)(2,1)S(1)}, bf16[176,256]{1,0:T(8,128)(2,1)S(1)}, u32[]{:S(2)}, u32[]{:S(2)}) collective-permute-start(bf16[176,256]{1,0:T(8,128)(2,1)S(1)} %get-tuple-element.78), channel_id=1, source_target_pairs={{0,20},{1,28},{2,22},{3,30},{4,16},{5,24},{6,18},{7,26},{8,21},{9,... | collective-permute-start | bytes 270344 | tf_op jit(solution)/shard_map/ppermute | solution.py:94
  57.0 7.7 %collective-permute-start.19 = (bf16[176,256]{1,0:T(8,128)(2,1)S(1)}, bf16[176,256]{1,0:T(8,128)(2,1)S(1)}, u32[]{:S(2)}, u32[]{:S(2)}) collective-permute-start(bf16[176,256]{1,0:T(8,128)(2,1)S(1)} %get-tuple-element.83), channel_id=1, source_target_pairs={{0,0},{1,8},{2,2},{3,10},{4,4},{5,12},{6,6},{7,14},{8,1},{9,9},{10... | collective-permute-start | bytes 270344 | tf_op jit(solution)/shard_map/ppermute | solution.py:94
  60.3 6.1 %collective-permute-start.20 = (bf16[176,256]{1,0:T(8,128)(2,1)S(1)}, bf16[176,256]{1,0:T(8,128)(2,1)S(1)}, u32[]{:S(2)}, u32[]{:S(2)}) collective-permute-start(bf16[176,256]{1,0:T(8,128)(2,1)S(1)} %get-tuple-element.84), channel_id=1, source_target_pairs={{0,4},{1,12},{2,6},{3,14},{4,0},{5,8},{6,2},{7,10},{8,5},{9,13},{1... | collective-permute-start | bytes 270344 | tf_op jit(solution)/shard_map/ppermute | solution.py:94
  (4 other events, 42.5 us)

commit v5 on v4

--- a/solution.py
+++ b/solution.py
@@ -101,7 +101,6 @@
 SWAP_H = lambda h, zl, y, x, c: (1 - h, zl, y, x, c)
 SWAP_Z = lambda h, zl, y, x, c: (h, 1 - zl, y, x, c)
 SWAP_Y = lambda h, zl, y, x, c: (h, zl, 1 - y, x, c)
-SWAP_ZY = lambda h, zl, y, x, c: (h, 1 - zl, 1 - y, x, c)
 SWAP_X = lambda h, zl, y, x, c: (h, zl, y, 1 - x, c)
 SWAP_C = lambda h, zl, y, x, c: (h, zl, y, x, 1 - c)
 
@@ -111,13 +110,17 @@
 
 
 def dz_kernel(pre_hbm, emb_hbm, filters_hbm, out_ref, along_ref, pre_ref, emb_ref, weight_ref, arrived):
-    rows, unit = pre_ref.shape[0], weight_ref.shape[0]
-    first = pl.multiple_of((1 + 2 * coords()[2]) * unit, 16)
+    rows, unit = pre_ref.shape[0], weight_ref.shape[1]
+    y = coords()[2]
     copies = [
         pltpu.make_async_copy(emb_hbm, emb_ref, arrived.at[0]),
         pltpu.make_async_copy(pre_hbm, pre_ref, arrived.at[1]),
-        pltpu.make_async_copy(filters_hbm.at[pl.ds(first, unit), :], weight_ref, arrived.at[2]),
     ]
+    for n, m in enumerate((1 + 2 * y, 3 - 2 * y)):
+        first = pl.multiple_of(m * unit, 16)
+        copies.append(
+            pltpu.make_async_copy(filters_hbm.at[pl.ds(first, unit), :], weight_ref.at[n], arrived.at[2 + n])
+        )
     for copy in copies:
         copy.start()
     half = emb_ref.shape[0]
@@ -130,14 +133,15 @@
     value = (up * gelu_slope(pre_ref[...].astype(F32))).astype(BF16)
     out_ref[...] = value
     along_ref[:rows] = value
-    along_ref[rows:] = weight_ref[...]
-
-
-def units_kernel(unit, filters_ref, first_ref, middle_ref, last_ref, across_ref):
-    for m, ref in ((0, first_ref), (2, middle_ref), (4, last_ref)):
-        ref[...] = filters_ref[m * unit : (m + 1) * unit, :]
-    first = pl.multiple_of((3 - 2 * coords()[2]) * unit, 16)
-    across_ref[...] = filters_ref[pl.ds(first, unit), :]
+    for n in range(2):
+        along_ref[rows + n * unit : rows + (n + 1) * unit] = weight_ref[n]
+
+
+def units_kernel(unit, filters_ref, came_ref, first_ref, last_ref, along_ref):
+    first_ref[...] = filters_ref[:unit, :]
+    last_ref[...] = filters_ref[4 * unit :, :]
+    along_ref[:unit] = filters_ref[2 * unit : 3 * unit, :]
+    along_ref[unit:] = came_ref[came_ref.shape[0] - unit :, :]
 
 
 def cut_kernel(unit, acts_ref, *out_refs):
@@ -159,6 +163,12 @@
 def join_kernel(*refs):
     for n, ref in enumerate(refs[:-1]):
         refs[-1][n] = ref[...]
+
+
+def pair_kernel(first_ref, last_ref, out_ref):
+    half = first_ref.shape[0]
+    out_ref[:half] = first_ref[...]
+    out_ref[half:] = last_ref[...]
 
 
 EDGE = 16
@@ -212,13 +222,19 @@
 
 
 def away_kernel(rows, unit, most_ref, dz_last, *refs):
-    w_refs, (dz_ref, weights, out_ref) = refs[:5], refs[5:]
+    first, last, along_z, along_y, dz_ref, weights, out_ref = refs
     _, zl, y, _, _ = coords()
     place_dz(rows, dz_ref, 7)[...] = dz_last[...]
-    for m, ref in zip((0, 2, 4, 1 + 2 * y, 3 - 2 * y), w_refs):
+    units = (
+        (0, first, 0),
+        (4, last, 0),
+        (2, along_z, 0),
+        (1 + 2 * y, along_z, unit),
+        (3 - 2 * y, along_y, rows),
+    )
+    for m, ref, start in units:
         slot = lax.rem(2 * zl + y + 5 - m, 5)
-        first = ref.shape[0] - unit
-        weights[pl.ds(pl.multiple_of(slot * unit, EDGE), unit), :] = ref[first:]
+        weights[pl.ds(pl.multiple_of(slot * unit, EDGE), unit), :] = ref[start : start + unit]
     input_terms(rows, unit, dz_ref, weights, out_ref, 1)
 
 
@@ -245,14 +261,13 @@
         out_ref[pl.ds(first, unit), :] = (refs[b][...].astype(F32) + refs[2 + b][...].astype(F32)).astype(BF16)
 
 
-def left_kernel(rows, unit, s00, s10, s01, s11, out_ref, lines):
+def left_kernel(rows, unit, own_ref, came_ref, out_ref, lines):
     h, _, y, x, c = coords()
-    for xr, cr, ref in ((0, 0, s00), (1, 0, s10), (0, 1, s01), (1, 1, s11)):
-        which = x ^ xr ^ h
-        for a in range(2):
-            for b in range(2):
-                block = 4 * (h ^ a) + 2 * (c ^ cr) + (y ^ b)
-                lines[which, :, pl.ds(pl.multiple_of(block * rows, rows), rows)] = ref[2 * a + b].astype(F32)
+    for cr, ref in enumerate((own_ref, came_ref)):
+        for n in range(8):
+            which = x ^ (n // 4) ^ h
+            block = 4 * (h ^ (n // 2 % 2)) + 2 * (c ^ cr) + (y ^ (n % 2))
+            lines[which, :, pl.ds(pl.multiple_of(block * rows, rows), rows)] = ref[n].astype(F32)
     total = 8 * rows
     place = lax.broadcasted_iota(jnp.int32, (unit, total), 1)
     for half in range(2):
@@ -311,44 +326,48 @@
     dz, along = call(
         dz_kernel,
         "dz",
-        (block, shape((rows + unit, wide), BF16)),
+        (block, shape((rows + 2 * unit, wide), BF16)),
         (pre_act, emb_grad, filters),
         scratch=[
             pltpu.VMEM(pre_act.shape, BF16),
             pltpu.VMEM(emb_grad.shape, BF16),
-            pltpu.VMEM((unit, wide), BF16),
-            pltpu.SemaphoreType.DMA((3,)),
+            pltpu.VMEM((2, unit, wide), BF16),
+            pltpu.SemaphoreType.DMA((4,)),
         ],
         mib=60,
         anywhere=True,
     )
     own0, own1 = call(functools.partial(cut_kernel, unit), "cut", (pos, pos), (acts,), mib=8)
     dz_h, dz_z, dz_y = send(dz, SWAP_H), send(dz, SWAP_Z), send(along, SWAP_Y)
-    w0, w2, w4, wd = call(functools.partial(units_kernel, unit), "units", (weight,) * 4, (filters,), mib=4)
     t01, t00 = send(own1, turn(0, 1)), send(own0, turn(0, 0))
     dz_zy = send(dz_z, SWAP_Y)
     near_got = call(join_kernel, "join_near", shape((2, unit, rows), BF16), (t00, t01), mib=4)
     far_got = send(near_got, SWAP_H)
-    dz_h, dz_y, wd, w2 = tie((dz_h, dz_y, wd, w2))
+    dz_h, dz_y, filters = tie((dz_h, dz_y, filters))
     dz_hz, dz_hy = send(dz_h, SWAP_Z), send(dz_h, SWAP_Y)
-    wd = send(wd, SWAP_ZY)
-
-    dz_hz, dz_zy, dz_hy, wd, w2, far_got = tie((dz_hz, dz_zy, dz_hy, wd, w2, far_got))
+
+    w0, w4, along = call(
+        functools.partial(units_kernel, unit),
+        "units",
+        (weight, weight, shape((2 * unit, wide), BF16)),
+        (filters, dz_y),
+        mib=4,
+    )
+    dz_hz, dz_zy, dz_hy, along, far_got = tie((dz_hz, dz_zy, dz_hy, along, far_got))
     got = call(join_kernel, "join", shape((2, 2, unit, rows), BF16), (near_got, far_got), mib=4)
     got = got.reshape(4, unit, rows)
     other = send(got, SWAP_X)
     dz_hzy = send(dz_hz, SWAP_Y)
-    w2 = send(w2, SWAP_Z)
-    far = send(got, SWAP_C)
-
-    weights = (w0, w2, w4, wd, dz_y)
-    dz_hzy, other, far, *weights = tie((dz_hzy, other, far, *weights))
-    far_other = send(other, SWAP_C)
+    along = send(along, SWAP_Z)
+
+    weights = (w0, w4, along, dz_y)
+    dz_hzy, other, *weights = tie((dz_hzy, other, *weights))
+    both = call(pair_kernel, "pair", shape((8, unit, rows), BF16), (got, other), mib=8)
     left = call(
         functools.partial(left_kernel, rows, unit),
         "left",
         shape((5, unit, total), BF16),
-        (got, other, far, far_other),
+        (both, send(both, SWAP_C)),
         scratch=[pltpu.VMEM((2, unit, total), F32)],
     )
     padded = shape((total + 2 * EDGE, wide), BF16)

time: 67.6 us -> 66.4 us (0.982)
  waiting for transfers between devices: 22 us -> 14.3 us
  starting transfers between devices: 32.5 us -> 39.1 us
    ppermute x22 -> x20, waiting for transfers between devices: 22 us -> 14.3 us  [send(): return lax.ppermute(value, ('seq', 'section'), pairs)]
    ppermute x22 -> x20, starting transfers between devices: 29.9 us -> 36.5 us  [send(): return lax.ppermute(value, ('seq', 'section'), pairs)]
    pallas_call x16 -> x17, Pallas kernels: 10.7 us -> 10.8 us  [call(): pl.pallas_call(kernel, out_shape=shapes, in_specs=[pl.BlockSpec(memory_sp...]
  transfers between devices with their start and end apart: 25 -> 23, of which waited for: 11 -> 9; matrix products, arithmetic and copies ran while one was open for 0% -> 0% of each run, Pallas kernels for 10% -> 10%
where the time goes in v5:
time: 66.4 us; the launch traced here: 66.1 us
  starting transfers between devices  39.1 us (59%)
  waiting for transfers between devices  14.3 us (22%)
  Pallas kernels  10.8 us (16%)
  local copies, waits for them, and re-layouts  1.12 us (2%)
  between operations  0.78 us (1%)
    ppermute x20, starting transfers between devices, send(): return lax.ppermute(value, ('seq', 'section'), pairs)  36.5 us
    ppermute x20, waiting for transfers between devices, send(): return lax.ppermute(value, ('seq', 'section'), pairs)  14.3 us
    pallas_call x17, Pallas kernels, call(): pl.pallas_call(kernel, out_shape=shapes, in_specs=[pl.BlockSpec(memory_sp...  10.8 us
    ppermute x3, starting transfers between devices, in_half(): lax.ppermute(value, 'seq', [(i, 4 * (i // 4) + (i % 4 + step) % 4) for i...  2.55 us
  transfers between devices with their start and end apart: 23, of which 9 were waited for; matrix products, arithmetic and copies ran while one was open for 0% of the time, Pallas kernels for 10%

profile of v5, /device:TPU:1, one launch (start us, length us, event | category | flops | bytes accessed | tf_op | source)
XLA Modules:
  0.0 66.1 jit_solution(7600817533562516804)
XLA Ops:
  0.6 2.3 %dz.1 = (bf16[256,384]{1,0:T(8,128)(2,1)}, bf16[608,384]{1,0:T(8,128)(2,1)}) custom-call(bf16[256,384]{1,0:T(8,128)(2,1)} %pre_hbm.1, bf16[128,384]{1,0:T(8,128)(2,1)} %emb_hbm.1, bf16[880,384]{1,0:T(8,128)(2,1)} %filters_ref), custom_call_target="tpu_custom_call" | custom-call | bytes 1024 | tf_op jit(solution)/shard_map/dz/pallas_call | solution.py:303
  3.0 2.1 %collective-permute-start.1 = (bf16[608,384]{1,0:T(8,128)(2,1)}, bf16[608,384]{1,0:T(8,128)(2,1)S(1)}, u32[]{:S(2)}, u32[]{:S(2)}) collective-permute-start(bf16[608,384]{1,0:T(8,128)(2,1)} %get-tuple-element.43), channel_id=1, source_target_pairs={{0,4},{1,5},{2,6},{3,7},{4,0},{5,1},{6,2},{7,3},{8,12},{9,13},{10,... | collective-permute-start | bytes 1400840 | tf_op jit(solution)/shard_map/ppermute | solution.py:94
  5.1 1.3 %collective-permute-start.2 = (bf16[256,384]{1,0:T(8,128)(2,1)}, bf16[256,384]{1,0:T(8,128)(2,1)S(1)}, u32[]{:S(2)}, u32[]{:S(2)}) collective-permute-start(bf16[256,384]{1,0:T(8,128)(2,1)} %get-tuple-element.42.refs_0_), channel_id=1, source_target_pairs={{0,8},{1,9},{2,10},{3,11},{4,12},{5,13},{6,14},{7,15},{8,0},{9,1},... | collective-permute-start | bytes 589832 | tf_op jit(solution)/shard_map/ppermute | solution.py:94
  6.4 2.3 %collective-permute-start = (bf16[256,384]{1,0:T(8,128)(2,1)}, bf16[256,384]{1,0:T(8,128)(2,1)S(1)}, u32[]{:S(2)}, u32[]{:S(2)}) collective-permute-start(bf16[256,384]{1,0:T(8,128)(2,1)} %get-tuple-element.42.refs_0_), channel_id=1, source_target_pairs={{0,16},{1,17},{2,18},{3,19},{4,20},{5,21},{6,22},{7,23},{8,24},{9,... | collective-permute-start | bytes 589832 | tf_op jit(solution)/shard_map/ppermute | solution.py:94
  10.2 3.4 %collective-permute-start.6 = (bf16[176,256]{1,0:T(8,128)(2,1)S(1)}, bf16[176,256]{1,0:T(8,128)(2,1)S(1)}, u32[]{:S(2)}, u32[]{:S(2)}) collective-permute-start(bf16[176,256]{1,0:T(8,128)(2,1)S(1)} %get-tuple-element.48), channel_id=1, source_target_pairs={{0,0},{1,8},{2,2},{3,10},{4,4},{5,12},{6,6},{7,14},{8,1},{9,9},{10... | collective-permute-start | bytes 270344 | tf_op jit(solution)/shard_map/ppermute | solution.py:94
  13.9 1.2 %collective-permute-start.4 = (bf16[256,384]{1,0:T(8,128)(2,1)S(1)}, bf16[256,384]{1,0:T(8,128)(2,1)S(1)}, u32[]{:S(2)}, u32[]{:S(2)}) collective-permute-start(bf16[256,384]{1,0:T(8,128)(2,1)S(1)} %collective-permute-done.2.refs_2_), channel_id=1, source_target_pairs={{0,4},{1,5},{2,6},{3,7},{4,0},{5,1},{6,2},{7,3},{8,12},{9,13},{10,... | collective-permute-start | bytes 589832 | tf_op jit(solution)/shard_map/ppermute | solution.py:94
  16.9 1.3 %collective-permute-start.3 = (bf16[256,384]{1,0:T(8,128)(2,1)S(1)}, bf16[256,384]{1,0:T(8,128)(2,1)S(1)}, u32[]{:S(2)}, u32[]{:S(2)}) collective-permute-start(bf16[256,384]{1,0:T(8,128)(2,1)S(1)} %collective-permute-done.refs_4_), channel_id=1, source_target_pairs={{0,8},{1,9},{2,10},{3,11},{4,12},{5,13},{6,14},{7,15},{8,0},{9,1},... | collective-permute-start | bytes 589832 | tf_op jit(solution)/shard_map/ppermute | solution.py:94
  18.7 1.8 %collective-permute-start.8 = (bf16[2,176,256]{2,1,0:T(8,128)(2,1)S(1)}, bf16[2,176,256]{2,1,0:T(8,128)(2,1)S(1)}, u32[]{:S(2)}, u32[]{:S(2)}) collective-permute-start(bf16[2,176,256]{2,1,0:T(8,128)(2,1)S(1)} %join_near.1.refs_0_), channel_id=1, source_target_pairs={{0,16},{1,17},{2,18},{3,19},{4,20},{5,21},{6,22},{7,23},{8,24},{9,... | collective-permute-start | bytes 540680 | tf_op jit(solution)/shard_map/ppermute | solution.py:94
  20.6 5.4 %collective-permute-done.8.refs_1_ = bf16[2,176,256]{2,1,0:T(8,128)(2,1)S(1)} collective-permute-done((bf16[2,176,256]{2,1,0:T(8,128)(2,1)S(1)}, bf16[2,176,256]{2,1,0:T(8,128)(2,1)S(1)}, u32[]{:S(2)}, u32[]{:S(2)}) %collective-permute-start.8) | collective-permute-done | bytes 180256 | tf_op jit(solution)/shard_map/ppermute | solution.py:94
  26.1 1.4 %collective-permute-start.10 = (bf16[4,176,256]{2,1,0:T(8,128)(2,1)S(1)}, bf16[4,176,256]{2,1,0:T(8,128)(2,1)S(1)}, u32[]{:S(2)}, u32[]{:S(2)}) collective-permute-start(bf16[4,176,256]{2,1,0:T(8,128)(2,1)S(1)} %bitcast.2), channel_id=1, source_target_pairs={{0,2},{1,3},{2,0},{3,1},{4,6},{5,7},{6,4},{7,5},{8,10},{9,11},{10,... | collective-permute-start | bytes 1081352 | tf_op jit(solution)/shard_map/ppermute | solution.py:94
  27.5 2.1 %collective-permute-start.11 = (bf16[352,384]{1,0:T(8,128)(2,1)S(1)}, bf16[352,384]{1,0:T(8,128)(2,1)S(1)}, u32[]{:S(2)}, u32[]{:S(2)}) collective-permute-start(bf16[352,384]{1,0:T(8,128)(2,1)S(1)} %get-tuple-element.56), channel_id=1, source_target_pairs={{0,8},{1,9},{2,10},{3,11},{4,12},{5,13},{6,14},{7,15},{8,0},{9,1},... | collective-permute-start | bytes 811016 | tf_op jit(solution)/shard_map/ppermute | solution.py:94
  29.6 2.2 %collective-permute-start.9 = (bf16[256,384]{1,0:T(8,128)(2,1)S(1)}, bf16[256,384]{1,0:T(8,128)(2,1)S(1)}, u32[]{:S(2)}, u32[]{:S(2)}) collective-permute-start(bf16[256,384]{1,0:T(8,128)(2,1)S(1)} %collective-permute-done.3.refs_6_), channel_id=1, source_target_pairs={{0,4},{1,5},{2,6},{3,7},{4,0},{5,1},{6,2},{7,3},{8,12},{9,13},{10,... | collective-permute-start | bytes 589832 | tf_op jit(solution)/shard_map/ppermute | solution.py:94
  32.0 3.2 %collective-permute-done.9.dz_last = bf16[256,384]{1,0:T(8,128)(2,1)S(1)} collective-permute-done((bf16[256,384]{1,0:T(8,128)(2,1)S(1)}, bf16[256,384]{1,0:T(8,128)(2,1)S(1)}, u32[]{:S(2)}, u32[]{:S(2)}) %collective-permute-start.9) | collective-permute-done | bytes 196640 | tf_op jit(solution)/shard_map/ppermute | solution.py:94
  35.2 1.3 %away.1 = (bf16[2080,384]{1,0:T(8,128)(2,1)S(1)}, bf16[880,384]{1,0:T(8,128)(2,1)S(1)}, bf16[2,2,2,176,256]{4,3,2,1,0:T(8,128)(2,1)S(1)}) custom-call(bf16[2080,384]{1,0:T(8,128)(2,1)S(1)} %gather.1.most_ref, bf16[256,384]{1,0:T(8,128)(2,1)S(1)} %collective-permute-done.9.dz_last, ...), custom_call_target="tpu_custom_call", output_to_operand_aliasing={{0}: (0, {})} | custom-call | bytes 1024 | tf_op jit(solution)/shard_map/away/pallas_call | solution.py:303
  36.4 3.9 %collective-permute-start.12 = (bf16[2,2,2,176,256]{4,3,2,1,0:T(8,128)(2,1)S(1)}, bf16[2,2,2,176,256]{4,3,2,1,0:T(8,128)(2,1)S(1)}, u32[]{:S(2)}, u32[]{:S(2)}) collective-permute-start(bf16[2,2,2,176,256]{4,3,2,1,0:T(8,128)(2,1)S(1)} %get-tuple-element.64), channel_id=1, source_target_pairs={{0,1},{1,0},{2,3},{3,2},{4,5},{5,4},{6,7},{7,6},{8,9},{9,8},{10,11... | collective-permute-start | bytes 2162696 | tf_op jit(solution)/shard_map/ppermute | solution.py:94
  40.5 1.2 %keep.1.keep_ref = f32[2,2,2,176,256]{4,3,2,1,0:T(8,128)S(1)} custom-call(bf16[2080,384]{1,0:T(8,128)(2,1)S(1)} %get-tuple-element.62.dz_ref, bf16[880,384]{1,0:T(8,128)(2,1)S(1)} %get-tuple-element.63.weights), custom_call_target="tpu_custom_call" | custom-call | bytes 1024 | tf_op jit(solution)/shard_map/keep/pallas_call | solution.py:303
  45.1 2.1 %filter.1 = (f32[176,384]{1,0:T(8,128)S(1)}, bf16[176,384]{1,0:T(8,128)(2,1)S(1)}, bf16[176,384]{1,0:T(8,128)(2,1)S(1)}, bf16[176,384]{1,0:T(8,128)(2,1)S(1)}, f32[176,384]{1,0:T(8,128)S(1)}) custom-call(bf16[5,176,2048]{2,1,0:T(8,128)(2,1)S(1)} %left.1.left_ref, bf16[2080,384]{1,0:T(8,128)(2,1)S(1)} %get-tuple-element.62.dz_ref), custom_call_target="tpu_custom_call" | custom-call | bytes 1024 | tf_op jit(solution)/shard_map/filter/pallas_call | solution.py:303
  47.2 2.2 %collective-permute-start.20 = (bf16[176,384]{1,0:T(8,128)(2,1)S(1)}, bf16[176,384]{1,0:T(8,128)(2,1)S(1)}, u32[]{:S(2)}, u32[]{:S(2)}) collective-permute-start(bf16[176,384]{1,0:T(8,128)(2,1)S(1)} %get-tuple-element.78), channel_id=1, source_target_pairs={{0,12},{4,0},{8,4},{12,8},{16,28},{20,16},{24,20},{28,24},{1,13},{... | collective-permute-start | bytes 405512 | tf_op jit(solution)/shard_map/ppermute | solution.py:98
  49.8 5.4 %collective-permute-start.14 = (bf16[176,256]{1,0:T(8,128)(2,1)S(1)}, bf16[176,256]{1,0:T(8,128)(2,1)S(1)}, u32[]{:S(2)}, u32[]{:S(2)}) collective-permute-start(bf16[176,256]{1,0:T(8,128)(2,1)S(1)} %get-tuple-element.68), channel_id=1, source_target_pairs={{0,16},{1,24},{2,18},{3,26},{4,20},{5,28},{6,22},{7,30},{8,17},{9,... | collective-permute-start | bytes 270344 | tf_op jit(solution)/shard_map/ppermute | solution.py:94
  55.2 2.8 %collective-permute-start.15 = (bf16[176,256]{1,0:T(8,128)(2,1)S(1)}, bf16[176,256]{1,0:T(8,128)(2,1)S(1)}, u32[]{:S(2)}, u32[]{:S(2)}) collective-permute-start(bf16[176,256]{1,0:T(8,128)(2,1)S(1)} %get-tuple-element.69), channel_id=1, source_target_pairs={{0,20},{1,28},{2,22},{3,30},{4,16},{5,24},{6,18},{7,26},{8,21},{9,... | collective-permute-start | bytes 270344 | tf_op jit(solution)/shard_map/ppermute | solution.py:94
  58.1 1.9 %collective-permute-start.17 = (bf16[176,256]{1,0:T(8,128)(2,1)S(1)}, bf16[176,256]{1,0:T(8,128)(2,1)S(1)}, u32[]{:S(2)}, u32[]{:S(2)}) collective-permute-start(bf16[176,256]{1,0:T(8,128)(2,1)S(1)} %get-tuple-element.74), channel_id=1, source_target_pairs={{0,0},{1,8},{2,2},{3,10},{4,4},{5,12},{6,6},{7,14},{8,1},{9,9},{10... | collective-permute-start | bytes 270344 | tf_op jit(solution)/shard_map/ppermute | solution.py:94
  60.2 1.2 %home.1 = f32[880,384]{1,0:T(8,128)} custom-call(f32[176,384]{1,0:T(8,128)S(1)} %get-tuple-element.77.first_ref, bf16[176,384]{1,0:T(8,128)(2,1)S(1)} %collective-permute-done.20.s1_ref, bf16[176,384]{1,0:T(8,128)(2,1)S(1)} %collective-permute-done.21.s2_ref, bf16[176,384]{1,0:T(8,128)(2,1)S(1)} %collective-permute-done.22.s3_ref, ...), custom_call_target="tpu_custom_call" | custom-call | bytes 1024 | tf_op jit(solution)/shard_map/home/pallas_call | solution.py:303
  61.5 1.6 %collective-permute-done.15.refs_1_ = bf16[176,256]{1,0:T(8,128)(2,1)S(1)} collective-permute-done((bf16[176,256]{1,0:T(8,128)(2,1)S(1)}, bf16[176,256]{1,0:T(8,128)(2,1)S(1)}, u32[]{:S(2)}, u32[]{:S(2)}) %collective-permute-start.15) | collective-permute-done | bytes 90144 | tf_op jit(solution)/shard_map/ppermute | solution.py:94
  64.2 1.2 %collective-permute-done.18.refs_3_ = bf16[176,256]{1,0:T(8,128)(2,1)S(1)} collective-permute-done((bf16[176,256]{1,0:T(8,128)(2,1)S(1)}, bf16[176,256]{1,0:T(8,128)(2,1)S(1)}, u32[]{:S(2)}, u32[]{:S(2)}) %collective-permute-start.18) | collective-permute-done | bytes 90144 | tf_op jit(solution)/shard_map/ppermute | solution.py:94
  (45 shorter events, 10.4 us)
Async XLA Ops:
  3.0 12.8 %collective-permute-start.1 = (bf16[608,384]{1,0:T(8,128)(2,1)}, bf16[608,384]{1,0:T(8,128)(2,1)S(1)}, u32[]{:S(2)}, u32[]{:S(2)}) collective-permute-start(bf16[608,384]{1,0:T(8,128)(2,1)} %get-tuple-element.43), channel_id=1, source_target_pairs={{0,4},{1,5},{2,6},{3,7},{4,0},{5,1},{6,2},{7,3},{8,12},{9,13},{10,... | collective-permute-start | bytes 1400840 | tf_op jit(solution)/shard_map/ppermute | solution.py:94
  5.1 8.8 %collective-permute-start.2 = (bf16[256,384]{1,0:T(8,128)(2,1)}, bf16[256,384]{1,0:T(8,128)(2,1)S(1)}, u32[]{:S(2)}, u32[]{:S(2)}) collective-permute-start(bf16[256,384]{1,0:T(8,128)(2,1)} %get-tuple-element.42.refs_0_), channel_id=1, source_target_pairs={{0,8},{1,9},{2,10},{3,11},{4,12},{5,13},{6,14},{7,15},{8,0},{9,1},... | collective-permute-start | bytes 589832 | tf_op jit(solution)/shard_map/ppermute | solution.py:94
  6.4 8.8 %collective-permute-start = (bf16[256,384]{1,0:T(8,128)(2,1)}, bf16[256,384]{1,0:T(8,128)(2,1)S(1)}, u32[]{:S(2)}, u32[]{:S(2)}) collective-permute-start(bf16[256,384]{1,0:T(8,128)(2,1)} %get-tuple-element.42.refs_0_), channel_id=1, source_target_pairs={{0,16},{1,17},{2,18},{3,19},{4,20},{5,21},{6,22},{7,23},{8,24},{9,... | collective-permute-start | bytes 589832 | tf_op jit(solution)/shard_map/ppermute | solution.py:94
  9.8 22.0 %copy-start.2 = (bf16[256,384]{1,0:T(8,128)(2,1)S(1)}, bf16[256,384]{1,0:T(8,128)(2,1)}, u32[]{:S(2)}) copy-start(bf16[256,384]{1,0:T(8,128)(2,1)} %get-tuple-element.42.refs_0_) | copy-start | bytes 589828
  10.2 7.9 %collective-permute-start.6 = (bf16[176,256]{1,0:T(8,128)(2,1)S(1)}, bf16[176,256]{1,0:T(8,128)(2,1)S(1)}, u32[]{:S(2)}, u32[]{:S(2)}) collective-permute-start(bf16[176,256]{1,0:T(8,128)(2,1)S(1)} %get-tuple-element.48), channel_id=1, source_target_pairs={{0,0},{1,8},{2,2},{3,10},{4,4},{5,12},{6,6},{7,14},{8,1},{9,9},{10... | collective-permute-start | bytes 270344 | tf_op jit(solution)/shard_map/ppermute | solution.py:94
  13.6 5.1 %collective-permute-start.7 = (bf16[176,256]{1,0:T(8,128)(2,1)S(1)}, bf16[176,256]{1,0:T(8,128)(2,1)S(1)}, u32[]{:S(2)}, u32[]{:S(2)}) collective-permute-start(bf16[176,256]{1,0:T(8,128)(2,1)S(1)} %get-tuple-element.49), channel_id=1, source_target_pairs={{0,4},{1,12},{2,6},{3,14},{4,0},{5,8},{6,2},{7,10},{8,5},{9,13},{1... | collective-permute-start | bytes 270344 | tf_op jit(solution)/shard_map/ppermute | solution.py:94
  13.9 12.2 %collective-permute-start.4 = (bf16[256,384]{1,0:T(8,128)(2,1)S(1)}, bf16[256,384]{1,0:T(8,128)(2,1)S(1)}, u32[]{:S(2)}, u32[]{:S(2)}) collective-permute-start(bf16[256,384]{1,0:T(8,128)(2,1)S(1)} %collective-permute-done.2.refs_2_), channel_id=1, source_target_pairs={{0,4},{1,5},{2,6},{3,7},{4,0},{5,1},{6,2},{7,3},{8,12},{9,13},{10,... | collective-permute-start | bytes 589832 | tf_op jit(solution)/shard_map/ppermute | solution.py:94
  15.7 10.3 %collective-permute-start.5 = (bf16[256,384]{1,0:T(8,128)(2,1)S(1)}, bf16[256,384]{1,0:T(8,128)(2,1)S(1)}, u32[]{:S(2)}, u32[]{:S(2)}) collective-permute-start(bf16[256,384]{1,0:T(8,128)(2,1)S(1)} %collective-permute-done.refs_4_), channel_id=1, source_target_pairs={{0,4},{1,5},{2,6},{3,7},{4,0},{5,1},{6,2},{7,3},{8,12},{9,13},{10,... | collective-permute-start | bytes 589832 | tf_op jit(solution)/shard_map/ppermute | solution.py:94
  16.9 9.2 %collective-permute-start.3 = (bf16[256,384]{1,0:T(8,128)(2,1)S(1)}, bf16[256,384]{1,0:T(8,128)(2,1)S(1)}, u32[]{:S(2)}, u32[]{:S(2)}) collective-permute-start(bf16[256,384]{1,0:T(8,128)(2,1)S(1)} %collective-permute-done.refs_4_), channel_id=1, source_target_pairs={{0,8},{1,9},{2,10},{3,11},{4,12},{5,13},{6,14},{7,15},{8,0},{9,1},... | collective-permute-start | bytes 589832 | tf_op jit(solution)/shard_map/ppermute | solution.py:94
  18.7 7.3 %collective-permute-start.8 = (bf16[2,176,256]{2,1,0:T(8,128)(2,1)S(1)}, bf16[2,176,256]{2,1,0:T(8,128)(2,1)S(1)}, u32[]{:S(2)}, u32[]{:S(2)}) collective-permute-start(bf16[2,176,256]{2,1,0:T(8,128)(2,1)S(1)} %join_near.1.refs_0_), channel_id=1, source_target_pairs={{0,16},{1,17},{2,18},{3,19},{4,20},{5,21},{6,22},{7,23},{8,24},{9,... | collective-permute-start | bytes 540680 | tf_op jit(solution)/shard_map/ppermute | solution.py:94
  26.1 9.0 %collective-permute-start.10 = (bf16[4,176,256]{2,1,0:T(8,128)(2,1)S(1)}, bf16[4,176,256]{2,1,0:T(8,128)(2,1)S(1)}, u32[]{:S(2)}, u32[]{:S(2)}) collective-permute-start(bf16[4,176,256]{2,1,0:T(8,128)(2,1)S(1)} %bitcast.2), channel_id=1, source_target_pairs={{0,2},{1,3},{2,0},{3,1},{4,6},{5,7},{6,4},{7,5},{8,10},{9,11},{10,... | collective-permute-start | bytes 1081352 | tf_op jit(solution)/shard_map/ppermute | solution.py:94
  27.5 7.7 %collective-permute-start.11 = (bf16[352,384]{1,0:T(8,128)(2,1)S(1)}, bf16[352,384]{1,0:T(8,128)(2,1)S(1)}, u32[]{:S(2)}, u32[]{:S(2)}) collective-permute-start(bf16[352,384]{1,0:T(8,128)(2,1)S(1)} %get-tuple-element.56), channel_id=1, source_target_pairs={{0,8},{1,9},{2,10},{3,11},{4,12},{5,13},{6,14},{7,15},{8,0},{9,1},... | collective-permute-start | bytes 811016 | tf_op jit(solution)/shard_map/ppermute | solution.py:94
  29.6 5.6 %collective-permute-start.9 = (bf16[256,384]{1,0:T(8,128)(2,1)S(1)}, bf16[256,384]{1,0:T(8,128)(2,1)S(1)}, u32[]{:S(2)}, u32[]{:S(2)}) collective-permute-start(bf16[256,384]{1,0:T(8,128)(2,1)S(1)} %collective-permute-done.3.refs_6_), channel_id=1, source_target_pairs={{0,4},{1,5},{2,6},{3,7},{4,0},{5,1},{6,2},{7,3},{8,12},{9,13},{10,... | collective-permute-start | bytes 589832 | tf_op jit(solution)/shard_map/ppermute | solution.py:94
  36.4 5.7 %collective-permute-start.12 = (bf16[2,2,2,176,256]{4,3,2,1,0:T(8,128)(2,1)S(1)}, bf16[2,2,2,176,256]{4,3,2,1,0:T(8,128)(2,1)S(1)}, u32[]{:S(2)}, u32[]{:S(2)}) collective-permute-start(bf16[2,2,2,176,256]{4,3,2,1,0:T(8,128)(2,1)S(1)} %get-tuple-element.64), channel_id=1, source_target_pairs={{0,1},{1,0},{2,3},{3,2},{4,5},{5,4},{6,7},{7,6},{8,9},{9,8},{10,11... | collective-permute-start | bytes 2162696 | tf_op jit(solution)/shard_map/ppermute | solution.py:94
  40.4 3.5 %collective-permute-start.19 = (bf16[8,176,256]{2,1,0:T(8,128)(2,1)S(1)}, bf16[8,176,256]{2,1,0:T(8,128)(2,1)S(1)}, u32[]{:S(2)}, u32[]{:S(2)}) collective-permute-start(bf16[8,176,256]{2,1,0:T(8,128)(2,1)S(1)} %pair.1.own_ref), channel_id=1, source_target_pairs={{0,1},{1,0},{2,3},{3,2},{4,5},{5,4},{6,7},{7,6},{8,9},{9,8},{10,11... | collective-permute-start | bytes 2162696 | tf_op jit(solution)/shard_map/ppermute | solution.py:94
  42.2 7.5 %collective-permute-start.13 = (bf16[2,176,256]{2,1,0:T(8,128)(2,1)S(1)}, bf16[2,176,256]{2,1,0:T(8,128)(2,1)S(1)}, u32[]{:S(2)}, u32[]{:S(2)}) collective-permute-start(bf16[2,176,256]{2,1,0:T(8,128)(2,1)S(1)} %get-tuple-element.67), channel_id=1, source_target_pairs={{0,2},{1,3},{2,0},{3,1},{4,6},{5,7},{6,4},{7,5},{8,10},{9,11},{10,... | collective-permute-start | bytes 540680 | tf_op jit(solution)/shard_map/ppermute | solution.py:94
  43.0 12.1 %collective-permute-start.16 = (bf16[2,176,256]{2,1,0:T(8,128)(2,1)S(1)}, bf16[2,176,256]{2,1,0:T(8,128)(2,1)S(1)}, u32[]{:S(2)}, u32[]{:S(2)}) collective-permute-start(bf16[2,176,256]{2,1,0:T(8,128)(2,1)S(1)} %get-tuple-element.73), channel_id=1, source_target_pairs={{0,2},{1,3},{2,0},{3,1},{4,6},{5,7},{6,4},{7,5},{8,10},{9,11},{10,... | collective-permute-start | bytes 540680 | tf_op jit(solution)/shard_map/ppermute | solution.py:94
  47.2 10.9 %collective-permute-start.20 = (bf16[176,384]{1,0:T(8,128)(2,1)S(1)}, bf16[176,384]{1,0:T(8,128)(2,1)S(1)}, u32[]{:S(2)}, u32[]{:S(2)}) collective-permute-start(bf16[176,384]{1,0:T(8,128)(2,1)S(1)} %get-tuple-element.78), channel_id=1, source_target_pairs={{0,12},{4,0},{8,4},{12,8},{16,28},{20,16},{24,20},{28,24},{1,13},{... | collective-permute-start | bytes 405512 | tf_op jit(solution)/shard_map/ppermute | solution.py:98
  49.4 10.6 %collective-permute-start.21 = (bf16[176,384]{1,0:T(8,128)(2,1)S(1)}, bf16[176,384]{1,0:T(8,128)(2,1)S(1)}, u32[]{:S(2)}, u32[]{:S(2)}) collective-permute-start(bf16[176,384]{1,0:T(8,128)(2,1)S(1)} %get-tuple-element.79), channel_id=1, source_target_pairs={{0,8},{4,12},{8,0},{12,4},{16,24},{20,28},{24,16},{28,20},{1,9},{5... | collective-permute-start | bytes 405512 | tf_op jit(solution)/shard_map/ppermute | solution.py:98
  49.4 10.8 %collective-permute-start.22 = (bf16[176,384]{1,0:T(8,128)(2,1)S(1)}, bf16[176,384]{1,0:T(8,128)(2,1)S(1)}, u32[]{:S(2)}, u32[]{:S(2)}) collective-permute-start(bf16[176,384]{1,0:T(8,128)(2,1)S(1)} %get-tuple-element.80), channel_id=1, source_target_pairs={{0,4},{4,8},{8,12},{12,0},{16,20},{20,24},{24,28},{28,16},{1,5},{5... | collective-permute-start | bytes 405512 | tf_op jit(solution)/shard_map/ppermute | solution.py:98
  49.8 11.7 %collective-permute-start.14 = (bf16[176,256]{1,0:T(8,128)(2,1)S(1)}, bf16[176,256]{1,0:T(8,128)(2,1)S(1)}, u32[]{:S(2)}, u32[]{:S(2)}) collective-permute-start(bf16[176,256]{1,0:T(8,128)(2,1)S(1)} %get-tuple-element.68), channel_id=1, source_target_pairs={{0,16},{1,24},{2,18},{3,26},{4,20},{5,28},{6,22},{7,30},{8,17},{9,... | collective-permute-start | bytes 270344 | tf_op jit(solution)/shard_map/ppermute | solution.py:94
  55.2 7.9 %collective-permute-start.15 = (bf16[176,256]{1,0:T(8,128)(2,1)S(1)}, bf16[176,256]{1,0:T(8,128)(2,1)S(1)}, u32[]{:S(2)}, u32[]{:S(2)}) collective-permute-start(bf16[176,256]{1,0:T(8,128)(2,1)S(1)} %get-tuple-element.69), channel_id=1, source_target_pairs={{0,20},{1,28},{2,22},{3,30},{4,16},{5,24},{6,18},{7,26},{8,21},{9,... | collective-permute-start | bytes 270344 | tf_op jit(solution)/shard_map/ppermute | solution.py:94
  58.1 6.1 %collective-permute-start.17 = (bf16[176,256]{1,0:T(8,128)(2,1)S(1)}, bf16[176,256]{1,0:T(8,128)(2,1)S(1)}, u32[]{:S(2)}, u32[]{:S(2)}) collective-permute-start(bf16[176,256]{1,0:T(8,128)(2,1)S(1)} %get-tuple-element.74), channel_id=1, source_target_pairs={{0,0},{1,8},{2,2},{3,10},{4,4},{5,12},{6,6},{7,14},{8,1},{9,9},{10... | collective-permute-start | bytes 270344 | tf_op jit(solution)/shard_map/ppermute | solution.py:94
  60.0 5.4 %collective-permute-start.18 = (bf16[176,256]{1,0:T(8,128)(2,1)S(1)}, bf16[176,256]{1,0:T(8,128)(2,1)S(1)}, u32[]{:S(2)}, u32[]{:S(2)}) collective-permute-start(bf16[176,256]{1,0:T(8,128)(2,1)S(1)} %get-tuple-element.75), channel_id=1, source_target_pairs={{0,4},{1,12},{2,6},{3,14},{4,0},{5,8},{6,2},{7,10},{8,5},{9,13},{1... | collective-permute-start | bytes 270344 | tf_op jit(solution)/shard_map/ppermute | solution.py:94
  (2 other events, 21.1 us)

commit v6 on v5

--- a/solution.py
+++ b/solution.py
@@ -94,13 +94,10 @@
     return lax.ppermute(value, ("seq", "section"), pairs)
 
 
-def in_half(value, step):
-    return lax.ppermute(value, "seq", [(i, 4 * (i // 4) + (i % 4 + step) % 4) for i in range(8)])
-
-
 SWAP_H = lambda h, zl, y, x, c: (1 - h, zl, y, x, c)
 SWAP_Z = lambda h, zl, y, x, c: (h, 1 - zl, y, x, c)
 SWAP_Y = lambda h, zl, y, x, c: (h, zl, 1 - y, x, c)
+SWAP_ZY = lambda h, zl, y, x, c: (h, 1 - zl, 1 - y, x, c)
 SWAP_X = lambda h, zl, y, x, c: (h, zl, y, 1 - x, c)
 SWAP_C = lambda h, zl, y, x, c: (h, zl, y, x, 1 - c)
 
@@ -258,18 +255,18 @@
     y, out_ref = coords()[2], refs[4]
     for b in range(2):
         first = pl.multiple_of((y ^ b) * unit, 16)
-        out_ref[pl.ds(first, unit), :] = (refs[b][...].astype(F32) + refs[2 + b][...].astype(F32)).astype(BF16)
-
-
-def left_kernel(rows, unit, own_ref, came_ref, out_ref, lines):
-    h, _, y, x, c = coords()
+        out_ref[pl.ds(first, unit), :] = (refs[1 - b][...].astype(F32) + refs[3 - b][...].astype(F32)).astype(BF16)
+
+
+def filter_kernel(scale, rows, own_ref, came_ref, dz_ref, first_ref, s1_ref, s2_ref, s3_ref, last_ref, lines, grads):
+    h, zl, y, x, c = coords()
+    unit, total = first_ref.shape[0], 8 * rows
     for cr, ref in enumerate((own_ref, came_ref)):
         for n in range(8):
             which = x ^ (n // 4) ^ h
             block = 4 * (h ^ (n // 2 % 2)) + 2 * (c ^ cr) + (y ^ (n % 2))
             lines[which, :, pl.ds(pl.multiple_of(block * rows, rows), rows)] = ref[n].astype(F32)
-    total = 8 * rows
-    place = lax.broadcasted_iota(jnp.int32, (unit, total), 1)
+    lines[:, :, total:] = jnp.zeros((2, unit, lines.shape[2] - total), F32)
     for half in range(2):
 
         @pl.when(h == half)
@@ -277,23 +274,19 @@
             for v, (tap, which) in enumerate(TAPS[half]):
                 line = lines[which]
                 if tap != 2:
-                    line = pltpu.roll(line, (2 - tap) % total, 1)
-                    fits = (place + (tap - 2) >= 0) & (place + (tap - 2) < total)
-                    line = jnp.where(fits, line, 0.0)
-                out_ref[v] = line.astype(BF16)
-
-
-def filter_kernel(scale, left_ref, dz_ref, first_ref, s1_ref, s2_ref, s3_ref, last_ref):
-    _, zl, y, _, _ = coords()
-    for m, ref in enumerate((first_ref, s1_ref, s2_ref, s3_ref, last_ref)):
-        slot = lax.rem(2 * zl + y + 5 - m, 5)
-        grad = jnp.dot(left_ref[slot], dz_ref[EDGE:-EDGE, :], preferred_element_type=F32) * scale
-        ref[...] = grad.astype(ref.dtype)
-
-
-def home_kernel(unit, first_ref, s1_ref, s2_ref, s3_ref, last_ref, out_ref):
-    for m, ref in enumerate((first_ref, s1_ref, s2_ref, s3_ref, last_ref)):
-        out_ref[m * unit : (m + 1) * unit, :] = ref[...].astype(F32)
+                    line = pltpu.roll(line, (2 - tap) % lines.shape[2], 1)
+                left = line[:, :total].astype(BF16)
+                grads[v] = jnp.dot(left, dz_ref[EDGE:-EDGE, :], preferred_element_type=F32) * scale
+
+    units = (0, 3 - 2 * y, 2, 1 + 2 * y, 4)
+    for m, ref in zip(units, (first_ref, s1_ref, s2_ref, s3_ref, last_ref)):
+        ref[...] = grads[lax.rem(2 * zl + y + 5 - m, 5)].astype(ref.dtype)
+
+
+def home_kernel(unit, first_ref, zy_ref, z_ref, y_ref, last_ref, out_ref):
+    y = coords()[2]
+    for m, ref in ((0, first_ref), (1 + 2 * y, y_ref), (2, z_ref), (3 - 2 * y, zy_ref), (4, last_ref)):
+        out_ref[pl.ds(pl.multiple_of(m * unit, 16), unit), :] = ref[...].astype(F32)
 
 
 def call(kernel, name, shapes, args, scratch=(), flops=0, mib=16, anywhere=False, alias={}):
@@ -363,13 +356,7 @@
     weights = (w0, w4, along, dz_y)
     dz_hzy, other, *weights = tie((dz_hzy, other, *weights))
     both = call(pair_kernel, "pair", shape((8, unit, rows), BF16), (got, other), mib=8)
-    left = call(
-        functools.partial(left_kernel, rows, unit),
-        "left",
-        shape((5, unit, total), BF16),
-        (both, send(both, SWAP_C)),
-        scratch=[pltpu.VMEM((2, unit, total), F32)],
-    )
+    far_both = send(both, SWAP_C)
     padded = shape((total + 2 * EDGE, wide), BF16)
     most = call(
         functools.partial(gather_kernel, rows),
@@ -404,17 +391,19 @@
     near_blocks = call(owners_kernel, "near", (pos,) * 2, (keep_near, near), mib=8)
     far_blocks = [send(block, turn(1, b)) for b, block in enumerate(far_blocks)]
     near_blocks = [send(block, turn(0, b)) for b, block in enumerate(near_blocks)]
-    came = tuple(far_blocks + near_blocks)
+    came = tuple(far_blocks[::-1] + near_blocks[::-1])
     input_grad = call(functools.partial(last_kernel, unit), "last", shape((2 * unit, rows), BF16), came, mib=4).T
 
     grads = call(
-        functools.partial(filter_kernel, 1.0 / math.sqrt(total)),
+        functools.partial(filter_kernel, 1.0 / math.sqrt(total), rows),
         "filter",
         tuple(shape((unit, wide), F32 if m in (0, 4) else BF16) for m in range(5)),
-        (left, dz_all),
+        (both, far_both, dz_all),
+        scratch=[pltpu.VMEM((2, unit, total + 128), F32), pltpu.VMEM((5, unit, wide), F32)],
         flops=flops,
     )
-    grads = tuple(in_half(grad, -m) if m in (1, 2, 3) else grad for m, grad in enumerate(grads))
+    first, along_y, along_z, across, last = grads
+    grads = (first, send(across, SWAP_ZY), send(along_z, SWAP_Z), send(along_y, SWAP_Y), last)
     filter_grad = call(functools.partial(home_kernel, unit), "home", shape((5 * unit, wide), F32), grads, mib=8)
     return input_grad, filter_grad
 

time: 66.4 us -> 65.4 us (0.985)
  waiting for transfers between devices: 14.3 us -> 11.8 us
  starting transfers between devices: 39.1 us -> 41.3 us
    ppermute x20 -> x23, starting transfers between devices: 36.5 us -> 41.3 us  [send(): return lax.ppermute(value, ('seq', 'section'), pairs)]
    ppermute x3 -> x0, starting transfers between devices: 2.55 us -> none  [in_half(): lax.ppermute(value, 'seq', [(i, 4 * (i // 4) + (i % 4 + step) % 4) for i...]
    ppermute x20 -> x23, waiting for transfers between devices: 14.3 us -> 11.8 us  [send(): return lax.ppermute(value, ('seq', 'section'), pairs)]
    pallas_call x17 -> x16, Pallas kernels: 10.8 us -> 10.2 us  [call(): pl.pallas_call(kernel, out_shape=shapes, in_specs=[pl.BlockSpec(memory_sp...]
  transfers between devices with their start and end apart: 23 -> 23, of which waited for: 9 -> 7; matrix products, arithmetic and copies ran while one was open for 0% -> 0% of each run, Pallas kernels for 10% -> 9%
where the time goes in v6:
time: 65.4 us; the launch traced here: 65.2 us
  starting transfers between devices  41.3 us (63%)
  waiting for transfers between devices  11.8 us (18%)
  Pallas kernels  10.2 us (16%)
  local copies, waits for them, and re-layouts  1.12 us (2%)
  between operations  0.77 us (1%)
    ppermute x23, starting transfers between devices, send(): return lax.ppermute(value, ('seq', 'section'), pairs)  41.3 us
    ppermute x23, waiting for transfers between devices, send(): return lax.ppermute(value, ('seq', 'section'), pairs)  11.8 us
    pallas_call x16, Pallas kernels, call(): pl.pallas_call(kernel, out_shape=shapes, in_specs=[pl.BlockSpec(memory_sp...  10.2 us
  transfers between devices with their start and end apart: 23, of which 7 were waited for; matrix products, arithmetic and copies ran while one was open for 0% of the time, Pallas kernels for 9%

profile of v6, /device:TPU:1, one launch (start us, length us, event | category | flops | bytes accessed | tf_op | source)
XLA Modules:
  0.0 65.2 jit_solution(5823299368652236158)
XLA Ops:
  0.6 2.3 %dz.1 = (bf16[256,384]{1,0:T(8,128)(2,1)}, bf16[608,384]{1,0:T(8,128)(2,1)}) custom-call(bf16[256,384]{1,0:T(8,128)(2,1)} %pre_hbm.1, bf16[128,384]{1,0:T(8,128)(2,1)} %emb_hbm.1, bf16[880,384]{1,0:T(8,128)(2,1)} %filters_ref), custom_call_target="tpu_custom_call" | custom-call | bytes 1024 | tf_op jit(solution)/shard_map/dz/pallas_call | solution.py:296
  3.0 2.1 %collective-permute-start.1 = (bf16[608,384]{1,0:T(8,128)(2,1)}, bf16[608,384]{1,0:T(8,128)(2,1)S(1)}, u32[]{:S(2)}, u32[]{:S(2)}) collective-permute-start(bf16[608,384]{1,0:T(8,128)(2,1)} %get-tuple-element.43), channel_id=1, source_target_pairs={{0,4},{1,5},{2,6},{3,7},{4,0},{5,1},{6,2},{7,3},{8,12},{9,13},{10,... | collective-permute-start | bytes 1400840 | tf_op jit(solution)/shard_map/ppermute | solution.py:94
  5.1 1.3 %collective-permute-start.2 = (bf16[256,384]{1,0:T(8,128)(2,1)}, bf16[256,384]{1,0:T(8,128)(2,1)S(1)}, u32[]{:S(2)}, u32[]{:S(2)}) collective-permute-start(bf16[256,384]{1,0:T(8,128)(2,1)} %get-tuple-element.42.refs_0_), channel_id=1, source_target_pairs={{0,8},{1,9},{2,10},{3,11},{4,12},{5,13},{6,14},{7,15},{8,0},{9,1},... | collective-permute-start | bytes 589832 | tf_op jit(solution)/shard_map/ppermute | solution.py:94
  6.4 2.3 %collective-permute-start = (bf16[256,384]{1,0:T(8,128)(2,1)}, bf16[256,384]{1,0:T(8,128)(2,1)S(1)}, u32[]{:S(2)}, u32[]{:S(2)}) collective-permute-start(bf16[256,384]{1,0:T(8,128)(2,1)} %get-tuple-element.42.refs_0_), channel_id=1, source_target_pairs={{0,16},{1,17},{2,18},{3,19},{4,20},{5,21},{6,22},{7,23},{8,24},{9,... | collective-permute-start | bytes 589832 | tf_op jit(solution)/shard_map/ppermute | solution.py:94
  8.7 1.1 %copy-done.1 = bf16[256,1408]{1,0:T(8,128)(2,1)S(1)} copy-done((bf16[256,1408]{1,0:T(8,128)(2,1)S(1)}, bf16[256,1408]{1,0:T(8,128)(2,1)}, u32[]{:S(2)}) %copy-start.1) | copy-done | bytes 720920
  10.2 3.4 %collective-permute-start.6 = (bf16[176,256]{1,0:T(8,128)(2,1)S(1)}, bf16[176,256]{1,0:T(8,128)(2,1)S(1)}, u32[]{:S(2)}, u32[]{:S(2)}) collective-permute-start(bf16[176,256]{1,0:T(8,128)(2,1)S(1)} %get-tuple-element.48), channel_id=1, source_target_pairs={{0,0},{1,8},{2,2},{3,10},{4,4},{5,12},{6,6},{7,14},{8,1},{9,9},{10... | collective-permute-start | bytes 270344 | tf_op jit(solution)/shard_map/ppermute | solution.py:94
  13.9 1.2 %collective-permute-start.4 = (bf16[256,384]{1,0:T(8,128)(2,1)S(1)}, bf16[256,384]{1,0:T(8,128)(2,1)S(1)}, u32[]{:S(2)}, u32[]{:S(2)}) collective-permute-start(bf16[256,384]{1,0:T(8,128)(2,1)S(1)} %collective-permute-done.2.refs_2_), channel_id=1, source_target_pairs={{0,4},{1,5},{2,6},{3,7},{4,0},{5,1},{6,2},{7,3},{8,12},{9,13},{10,... | collective-permute-start | bytes 589832 | tf_op jit(solution)/shard_map/ppermute | solution.py:94
  15.7 1.1 %collective-permute-start.5 = (bf16[256,384]{1,0:T(8,128)(2,1)S(1)}, bf16[256,384]{1,0:T(8,128)(2,1)S(1)}, u32[]{:S(2)}, u32[]{:S(2)}) collective-permute-start(bf16[256,384]{1,0:T(8,128)(2,1)S(1)} %collective-permute-done.refs_4_), channel_id=1, source_target_pairs={{0,4},{1,5},{2,6},{3,7},{4,0},{5,1},{6,2},{7,3},{8,12},{9,13},{10,... | collective-permute-start | bytes 589832 | tf_op jit(solution)/shard_map/ppermute | solution.py:94
  16.9 1.3 %collective-permute-start.3 = (bf16[256,384]{1,0:T(8,128)(2,1)S(1)}, bf16[256,384]{1,0:T(8,128)(2,1)S(1)}, u32[]{:S(2)}, u32[]{:S(2)}) collective-permute-start(bf16[256,384]{1,0:T(8,128)(2,1)S(1)} %collective-permute-done.refs_4_), channel_id=1, source_target_pairs={{0,8},{1,9},{2,10},{3,11},{4,12},{5,13},{6,14},{7,15},{8,0},{9,1},... | collective-permute-start | bytes 589832 | tf_op jit(solution)/shard_map/ppermute | solution.py:94
  18.7 1.8 %collective-permute-start.8 = (bf16[2,176,256]{2,1,0:T(8,128)(2,1)S(1)}, bf16[2,176,256]{2,1,0:T(8,128)(2,1)S(1)}, u32[]{:S(2)}, u32[]{:S(2)}) collective-permute-start(bf16[2,176,256]{2,1,0:T(8,128)(2,1)S(1)} %join_near.1.refs_0_), channel_id=1, source_target_pairs={{0,16},{1,17},{2,18},{3,19},{4,20},{5,21},{6,22},{7,23},{8,24},{9,... | collective-permute-start | bytes 540680 | tf_op jit(solution)/shard_map/ppermute | solution.py:94
  20.6 5.4 %collective-permute-done.8.refs_1_ = bf16[2,176,256]{2,1,0:T(8,128)(2,1)S(1)} collective-permute-done((bf16[2,176,256]{2,1,0:T(8,128)(2,1)S(1)}, bf16[2,176,256]{2,1,0:T(8,128)(2,1)S(1)}, u32[]{:S(2)}, u32[]{:S(2)}) %collective-permute-start.8) | collective-permute-done | bytes 180256 | tf_op jit(solution)/shard_map/ppermute | solution.py:94
  26.1 1.4 %collective-permute-start.10 = (bf16[4,176,256]{2,1,0:T(8,128)(2,1)S(1)}, bf16[4,176,256]{2,1,0:T(8,128)(2,1)S(1)}, u32[]{:S(2)}, u32[]{:S(2)}) collective-permute-start(bf16[4,176,256]{2,1,0:T(8,128)(2,1)S(1)} %bitcast.2), channel_id=1, source_target_pairs={{0,2},{1,3},{2,0},{3,1},{4,6},{5,7},{6,4},{7,5},{8,10},{9,11},{10,... | collective-permute-start | bytes 1081352 | tf_op jit(solution)/shard_map/ppermute | solution.py:94
  27.5 2.1 %collective-permute-start.11 = (bf16[352,384]{1,0:T(8,128)(2,1)S(1)}, bf16[352,384]{1,0:T(8,128)(2,1)S(1)}, u32[]{:S(2)}, u32[]{:S(2)}) collective-permute-start(bf16[352,384]{1,0:T(8,128)(2,1)S(1)} %get-tuple-element.56), channel_id=1, source_target_pairs={{0,8},{1,9},{2,10},{3,11},{4,12},{5,13},{6,14},{7,15},{8,0},{9,1},... | collective-permute-start | bytes 811016 | tf_op jit(solution)/shard_map/ppermute | solution.py:94
  29.6 2.2 %collective-permute-start.9 = (bf16[256,384]{1,0:T(8,128)(2,1)S(1)}, bf16[256,384]{1,0:T(8,128)(2,1)S(1)}, u32[]{:S(2)}, u32[]{:S(2)}) collective-permute-start(bf16[256,384]{1,0:T(8,128)(2,1)S(1)} %collective-permute-done.3.refs_6_), channel_id=1, source_target_pairs={{0,4},{1,5},{2,6},{3,7},{4,0},{5,1},{6,2},{7,3},{8,12},{9,13},{10,... | collective-permute-start | bytes 589832 | tf_op jit(solution)/shard_map/ppermute | solution.py:94
  32.0 3.2 %collective-permute-done.9.dz_last = bf16[256,384]{1,0:T(8,128)(2,1)S(1)} collective-permute-done((bf16[256,384]{1,0:T(8,128)(2,1)S(1)}, bf16[256,384]{1,0:T(8,128)(2,1)S(1)}, u32[]{:S(2)}, u32[]{:S(2)}) %collective-permute-start.9) | collective-permute-done | bytes 196640 | tf_op jit(solution)/shard_map/ppermute | solution.py:94
  35.2 1.3 %away.1 = (bf16[2080,384]{1,0:T(8,128)(2,1)S(1)}, bf16[880,384]{1,0:T(8,128)(2,1)S(1)}, bf16[2,2,2,176,256]{4,3,2,1,0:T(8,128)(2,1)S(1)}) custom-call(bf16[2080,384]{1,0:T(8,128)(2,1)S(1)} %gather.1.most_ref, bf16[256,384]{1,0:T(8,128)(2,1)S(1)} %collective-permute-done.9.dz_last, ...), custom_call_target="tpu_custom_call", output_to_operand_aliasing={{0}: (0, {})} | custom-call | bytes 1024 | tf_op jit(solution)/shard_map/away/pallas_call | solution.py:296
  36.5 3.9 %collective-permute-start.12 = (bf16[2,2,2,176,256]{4,3,2,1,0:T(8,128)(2,1)S(1)}, bf16[2,2,2,176,256]{4,3,2,1,0:T(8,128)(2,1)S(1)}, u32[]{:S(2)}, u32[]{:S(2)}) collective-permute-start(bf16[2,2,2,176,256]{4,3,2,1,0:T(8,128)(2,1)S(1)} %get-tuple-element.64), channel_id=1, source_target_pairs={{0,1},{1,0},{2,3},{3,2},{4,5},{5,4},{6,7},{7,6},{8,9},{9,8},{10,11... | collective-permute-start | bytes 2162696 | tf_op jit(solution)/shard_map/ppermute | solution.py:94
  40.5 1.2 %keep.1.keep_ref = f32[2,2,2,176,256]{4,3,2,1,0:T(8,128)S(1)} custom-call(bf16[2080,384]{1,0:T(8,128)(2,1)S(1)} %get-tuple-element.62.dz_ref, bf16[880,384]{1,0:T(8,128)(2,1)S(1)} %get-tuple-element.63.weights), custom_call_target="tpu_custom_call" | custom-call | bytes 1024 | tf_op jit(solution)/shard_map/keep/pallas_call | solution.py:296
  43.9 2.6 %filter.1 = (f32[176,384]{1,0:T(8,128)S(1)}, bf16[176,384]{1,0:T(8,128)(2,1)S(1)}, bf16[176,384]{1,0:T(8,128)(2,1)S(1)}, bf16[176,384]{1,0:T(8,128)(2,1)S(1)}, f32[176,384]{1,0:T(8,128)S(1)}) custom-call(bf16[8,176,256]{2,1,0:T(8,128)(2,1)S(1)} %pair.1.own_ref, bf16[8,176,256]{2,1,0:T(8,128)(2,1)S(1)} %collective-permute-done.19.came_ref, ...), custom_call_target="tpu_custom_call" | custom-call | bytes 1024 | tf_op jit(solution)/shard_map/filter/pallas_call | solution.py:296
  46.5 2.2 %collective-permute-start.20 = (bf16[176,384]{1,0:T(8,128)(2,1)S(1)}, bf16[176,384]{1,0:T(8,128)(2,1)S(1)}, u32[]{:S(2)}, u32[]{:S(2)}) collective-permute-start(bf16[176,384]{1,0:T(8,128)(2,1)S(1)} %get-tuple-element.78), channel_id=1, source_target_pairs={{0,12},{1,13},{2,14},{3,15},{4,8},{5,9},{6,10},{7,11},{8,4},{9,5},... | collective-permute-start | bytes 405512 | tf_op jit(solution)/shard_map/ppermute | solution.py:94
  49.3 6.7 %collective-permute-start.14 = (bf16[176,256]{1,0:T(8,128)(2,1)S(1)}, bf16[176,256]{1,0:T(8,128)(2,1)S(1)}, u32[]{:S(2)}, u32[]{:S(2)}) collective-permute-start(bf16[176,256]{1,0:T(8,128)(2,1)S(1)} %get-tuple-element.68), channel_id=1, source_target_pairs={{0,20},{1,28},{2,22},{3,30},{4,16},{5,24},{6,18},{7,26},{8,21},{9,... | collective-permute-start | bytes 270344 | tf_op jit(solution)/shard_map/ppermute | solution.py:94
  57.0 4.8 %collective-permute-start.18 = (bf16[176,256]{1,0:T(8,128)(2,1)S(1)}, bf16[176,256]{1,0:T(8,128)(2,1)S(1)}, u32[]{:S(2)}, u32[]{:S(2)}) collective-permute-start(bf16[176,256]{1,0:T(8,128)(2,1)S(1)} %get-tuple-element.75), channel_id=1, source_target_pairs={{0,0},{1,8},{2,2},{3,10},{4,4},{5,12},{6,6},{7,14},{8,1},{9,9},{10... | collective-permute-start | bytes 270344 | tf_op jit(solution)/shard_map/ppermute | solution.py:94
  61.8 1.2 %home.1 = f32[880,384]{1,0:T(8,128)} custom-call(f32[176,384]{1,0:T(8,128)S(1)} %get-tuple-element.77.first_ref, bf16[176,384]{1,0:T(8,128)(2,1)S(1)} %collective-permute-done.20.zy_ref, bf16[176,384]{1,0:T(8,128)(2,1)S(1)} %collective-permute-done.21.z_ref, bf16[176,384]{1,0:T(8,128)(2,1)S(1)} %collective-permute-done.22.y_ref, ...), custom_call_target="tpu_custom_call" | custom-call | bytes 1024 | tf_op jit(solution)/shard_map/home/pallas_call | solution.py:296
  63.4 1.1 %collective-permute-done.18.refs_3_ = bf16[176,256]{1,0:T(8,128)(2,1)S(1)} collective-permute-done((bf16[176,256]{1,0:T(8,128)(2,1)S(1)}, bf16[176,256]{1,0:T(8,128)(2,1)S(1)}, u32[]{:S(2)}, u32[]{:S(2)}) %collective-permute-start.18) | collective-permute-done | bytes 90144 | tf_op jit(solution)/shard_map/ppermute | solution.py:94
  (44 shorter events, 7.1 us)
Async XLA Ops:
  3.0 12.8 %collective-permute-start.1 = (bf16[608,384]{1,0:T(8,128)(2,1)}, bf16[608,384]{1,0:T(8,128)(2,1)S(1)}, u32[]{:S(2)}, u32[]{:S(2)}) collective-permute-start(bf16[608,384]{1,0:T(8,128)(2,1)} %get-tuple-element.43), channel_id=1, source_target_pairs={{0,4},{1,5},{2,6},{3,7},{4,0},{5,1},{6,2},{7,3},{8,12},{9,13},{10,... | collective-permute-start | bytes 1400840 | tf_op jit(solution)/shard_map/ppermute | solution.py:94
  5.1 8.8 %collective-permute-start.2 = (bf16[256,384]{1,0:T(8,128)(2,1)}, bf16[256,384]{1,0:T(8,128)(2,1)S(1)}, u32[]{:S(2)}, u32[]{:S(2)}) collective-permute-start(bf16[256,384]{1,0:T(8,128)(2,1)} %get-tuple-element.42.refs_0_), channel_id=1, source_target_pairs={{0,8},{1,9},{2,10},{3,11},{4,12},{5,13},{6,14},{7,15},{8,0},{9,1},... | collective-permute-start | bytes 589832 | tf_op jit(solution)/shard_map/ppermute | solution.py:94
  6.4 8.8 %collective-permute-start = (bf16[256,384]{1,0:T(8,128)(2,1)}, bf16[256,384]{1,0:T(8,128)(2,1)S(1)}, u32[]{:S(2)}, u32[]{:S(2)}) collective-permute-start(bf16[256,384]{1,0:T(8,128)(2,1)} %get-tuple-element.42.refs_0_), channel_id=1, source_target_pairs={{0,16},{1,17},{2,18},{3,19},{4,20},{5,21},{6,22},{7,23},{8,24},{9,... | collective-permute-start | bytes 589832 | tf_op jit(solution)/shard_map/ppermute | solution.py:94
  9.8 22.0 %copy-start.2 = (bf16[256,384]{1,0:T(8,128)(2,1)S(1)}, bf16[256,384]{1,0:T(8,128)(2,1)}, u32[]{:S(2)}) copy-start(bf16[256,384]{1,0:T(8,128)(2,1)} %get-tuple-element.42.refs_0_) | copy-start | bytes 589828
  10.2 7.9 %collective-permute-start.6 = (bf16[176,256]{1,0:T(8,128)(2,1)S(1)}, bf16[176,256]{1,0:T(8,128)(2,1)S(1)}, u32[]{:S(2)}, u32[]{:S(2)}) collective-permute-start(bf16[176,256]{1,0:T(8,128)(2,1)S(1)} %get-tuple-element.48), channel_id=1, source_target_pairs={{0,0},{1,8},{2,2},{3,10},{4,4},{5,12},{6,6},{7,14},{8,1},{9,9},{10... | collective-permute-start | bytes 270344 | tf_op jit(solution)/shard_map/ppermute | solution.py:94
  13.6 5.1 %collective-permute-start.7 = (bf16[176,256]{1,0:T(8,128)(2,1)S(1)}, bf16[176,256]{1,0:T(8,128)(2,1)S(1)}, u32[]{:S(2)}, u32[]{:S(2)}) collective-permute-start(bf16[176,256]{1,0:T(8,128)(2,1)S(1)} %get-tuple-element.49), channel_id=1, source_target_pairs={{0,4},{1,12},{2,6},{3,14},{4,0},{5,8},{6,2},{7,10},{8,5},{9,13},{1... | collective-permute-start | bytes 270344 | tf_op jit(solution)/shard_map/ppermute | solution.py:94
  13.9 12.2 %collective-permute-start.4 = (bf16[256,384]{1,0:T(8,128)(2,1)S(1)}, bf16[256,384]{1,0:T(8,128)(2,1)S(1)}, u32[]{:S(2)}, u32[]{:S(2)}) collective-permute-start(bf16[256,384]{1,0:T(8,128)(2,1)S(1)} %collective-permute-done.2.refs_2_), channel_id=1, source_target_pairs={{0,4},{1,5},{2,6},{3,7},{4,0},{5,1},{6,2},{7,3},{8,12},{9,13},{10,... | collective-permute-start | bytes 589832 | tf_op jit(solution)/shard_map/ppermute | solution.py:94
  15.7 10.3 %collective-permute-start.5 = (bf16[256,384]{1,0:T(8,128)(2,1)S(1)}, bf16[256,384]{1,0:T(8,128)(2,1)S(1)}, u32[]{:S(2)}, u32[]{:S(2)}) collective-permute-start(bf16[256,384]{1,0:T(8,128)(2,1)S(1)} %collective-permute-done.refs_4_), channel_id=1, source_target_pairs={{0,4},{1,5},{2,6},{3,7},{4,0},{5,1},{6,2},{7,3},{8,12},{9,13},{10,... | collective-permute-start | bytes 589832 | tf_op jit(solution)/shard_map/ppermute | solution.py:94
  16.9 9.2 %collective-permute-start.3 = (bf16[256,384]{1,0:T(8,128)(2,1)S(1)}, bf16[256,384]{1,0:T(8,128)(2,1)S(1)}, u32[]{:S(2)}, u32[]{:S(2)}) collective-permute-start(bf16[256,384]{1,0:T(8,128)(2,1)S(1)} %collective-permute-done.refs_4_), channel_id=1, source_target_pairs={{0,8},{1,9},{2,10},{3,11},{4,12},{5,13},{6,14},{7,15},{8,0},{9,1},... | collective-permute-start | bytes 589832 | tf_op jit(solution)/shard_map/ppermute | solution.py:94
  18.7 7.3 %collective-permute-start.8 = (bf16[2,176,256]{2,1,0:T(8,128)(2,1)S(1)}, bf16[2,176,256]{2,1,0:T(8,128)(2,1)S(1)}, u32[]{:S(2)}, u32[]{:S(2)}) collective-permute-start(bf16[2,176,256]{2,1,0:T(8,128)(2,1)S(1)} %join_near.1.refs_0_), channel_id=1, source_target_pairs={{0,16},{1,17},{2,18},{3,19},{4,20},{5,21},{6,22},{7,23},{8,24},{9,... | collective-permute-start | bytes 540680 | tf_op jit(solution)/shard_map/ppermute | solution.py:94
  26.1 9.0 %collective-permute-start.10 = (bf16[4,176,256]{2,1,0:T(8,128)(2,1)S(1)}, bf16[4,176,256]{2,1,0:T(8,128)(2,1)S(1)}, u32[]{:S(2)}, u32[]{:S(2)}) collective-permute-start(bf16[4,176,256]{2,1,0:T(8,128)(2,1)S(1)} %bitcast.2), channel_id=1, source_target_pairs={{0,2},{1,3},{2,0},{3,1},{4,6},{5,7},{6,4},{7,5},{8,10},{9,11},{10,... | collective-permute-start | bytes 1081352 | tf_op jit(solution)/shard_map/ppermute | solution.py:94
  27.5 7.7 %collective-permute-start.11 = (bf16[352,384]{1,0:T(8,128)(2,1)S(1)}, bf16[352,384]{1,0:T(8,128)(2,1)S(1)}, u32[]{:S(2)}, u32[]{:S(2)}) collective-permute-start(bf16[352,384]{1,0:T(8,128)(2,1)S(1)} %get-tuple-element.56), channel_id=1, source_target_pairs={{0,8},{1,9},{2,10},{3,11},{4,12},{5,13},{6,14},{7,15},{8,0},{9,1},... | collective-permute-start | bytes 811016 | tf_op jit(solution)/shard_map/ppermute | solution.py:94
  29.6 5.6 %collective-permute-start.9 = (bf16[256,384]{1,0:T(8,128)(2,1)S(1)}, bf16[256,384]{1,0:T(8,128)(2,1)S(1)}, u32[]{:S(2)}, u32[]{:S(2)}) collective-permute-start(bf16[256,384]{1,0:T(8,128)(2,1)S(1)} %collective-permute-done.3.refs_6_), channel_id=1, source_target_pairs={{0,4},{1,5},{2,6},{3,7},{4,0},{5,1},{6,2},{7,3},{8,12},{9,13},{10,... | collective-permute-start | bytes 589832 | tf_op jit(solution)/shard_map/ppermute | solution.py:94
  36.5 5.7 %collective-permute-start.12 = (bf16[2,2,2,176,256]{4,3,2,1,0:T(8,128)(2,1)S(1)}, bf16[2,2,2,176,256]{4,3,2,1,0:T(8,128)(2,1)S(1)}, u32[]{:S(2)}, u32[]{:S(2)}) collective-permute-start(bf16[2,2,2,176,256]{4,3,2,1,0:T(8,128)(2,1)S(1)} %get-tuple-element.64), channel_id=1, source_target_pairs={{0,1},{1,0},{2,3},{3,2},{4,5},{5,4},{6,7},{7,6},{8,9},{9,8},{10,11... | collective-permute-start | bytes 2162696 | tf_op jit(solution)/shard_map/ppermute | solution.py:94
  40.4 3.5 %collective-permute-start.19 = (bf16[8,176,256]{2,1,0:T(8,128)(2,1)S(1)}, bf16[8,176,256]{2,1,0:T(8,128)(2,1)S(1)}, u32[]{:S(2)}, u32[]{:S(2)}) collective-permute-start(bf16[8,176,256]{2,1,0:T(8,128)(2,1)S(1)} %pair.1.own_ref), channel_id=1, source_target_pairs={{0,1},{1,0},{2,3},{3,2},{4,5},{5,4},{6,7},{7,6},{8,9},{9,8},{10,11... | collective-permute-start | bytes 2162696 | tf_op jit(solution)/shard_map/ppermute | solution.py:94
  42.2 7.0 %collective-permute-start.13 = (bf16[2,176,256]{2,1,0:T(8,128)(2,1)S(1)}, bf16[2,176,256]{2,1,0:T(8,128)(2,1)S(1)}, u32[]{:S(2)}, u32[]{:S(2)}) collective-permute-start(bf16[2,176,256]{2,1,0:T(8,128)(2,1)S(1)} %get-tuple-element.67), channel_id=1, source_target_pairs={{0,2},{1,3},{2,0},{3,1},{4,6},{5,7},{6,4},{7,5},{8,10},{9,11},{10,... | collective-permute-start | bytes 540680 | tf_op jit(solution)/shard_map/ppermute | solution.py:94
  43.0 12.9 %collective-permute-start.16 = (bf16[2,176,256]{2,1,0:T(8,128)(2,1)S(1)}, bf16[2,176,256]{2,1,0:T(8,128)(2,1)S(1)}, u32[]{:S(2)}, u32[]{:S(2)}) collective-permute-start(bf16[2,176,256]{2,1,0:T(8,128)(2,1)S(1)} %get-tuple-element.73), channel_id=1, source_target_pairs={{0,2},{1,3},{2,0},{3,1},{4,6},{5,7},{6,4},{7,5},{8,10},{9,11},{10,... | collective-permute-start | bytes 540680 | tf_op jit(solution)/shard_map/ppermute | solution.py:94
  46.5 9.5 %collective-permute-start.20 = (bf16[176,384]{1,0:T(8,128)(2,1)S(1)}, bf16[176,384]{1,0:T(8,128)(2,1)S(1)}, u32[]{:S(2)}, u32[]{:S(2)}) collective-permute-start(bf16[176,384]{1,0:T(8,128)(2,1)S(1)} %get-tuple-element.78), channel_id=1, source_target_pairs={{0,12},{1,13},{2,14},{3,15},{4,8},{5,9},{6,10},{7,11},{8,4},{9,5},... | collective-permute-start | bytes 405512 | tf_op jit(solution)/shard_map/ppermute | solution.py:94
  48.7 8.2 %collective-permute-start.21 = (bf16[176,384]{1,0:T(8,128)(2,1)S(1)}, bf16[176,384]{1,0:T(8,128)(2,1)S(1)}, u32[]{:S(2)}, u32[]{:S(2)}) collective-permute-start(bf16[176,384]{1,0:T(8,128)(2,1)S(1)} %get-tuple-element.79), channel_id=1, source_target_pairs={{0,8},{1,9},{2,10},{3,11},{4,12},{5,13},{6,14},{7,15},{8,0},{9,1},... | collective-permute-start | bytes 405512 | tf_op jit(solution)/shard_map/ppermute | solution.py:94
  48.7 13.1 %collective-permute-start.22 = (bf16[176,384]{1,0:T(8,128)(2,1)S(1)}, bf16[176,384]{1,0:T(8,128)(2,1)S(1)}, u32[]{:S(2)}, u32[]{:S(2)}) collective-permute-start(bf16[176,384]{1,0:T(8,128)(2,1)S(1)} %get-tuple-element.80), channel_id=1, source_target_pairs={{0,4},{1,5},{2,6},{3,7},{4,0},{5,1},{6,2},{7,3},{8,12},{9,13},{10,... | collective-permute-start | bytes 405512 | tf_op jit(solution)/shard_map/ppermute | solution.py:94
  49.3 13.7 %collective-permute-start.14 = (bf16[176,256]{1,0:T(8,128)(2,1)S(1)}, bf16[176,256]{1,0:T(8,128)(2,1)S(1)}, u32[]{:S(2)}, u32[]{:S(2)}) collective-permute-start(bf16[176,256]{1,0:T(8,128)(2,1)S(1)} %get-tuple-element.68), channel_id=1, source_target_pairs={{0,20},{1,28},{2,22},{3,30},{4,16},{5,24},{6,18},{7,26},{8,21},{9,... | collective-permute-start | bytes 270344 | tf_op jit(solution)/shard_map/ppermute | solution.py:94
  55.9 7.0 %collective-permute-start.15 = (bf16[176,256]{1,0:T(8,128)(2,1)S(1)}, bf16[176,256]{1,0:T(8,128)(2,1)S(1)}, u32[]{:S(2)}, u32[]{:S(2)}) collective-permute-start(bf16[176,256]{1,0:T(8,128)(2,1)S(1)} %get-tuple-element.69), channel_id=1, source_target_pairs={{0,16},{1,24},{2,18},{3,26},{4,20},{5,28},{6,22},{7,30},{8,17},{9,... | collective-permute-start | bytes 270344 | tf_op jit(solution)/shard_map/ppermute | solution.py:94
  56.0 7.4 %collective-permute-start.17 = (bf16[176,256]{1,0:T(8,128)(2,1)S(1)}, bf16[176,256]{1,0:T(8,128)(2,1)S(1)}, u32[]{:S(2)}, u32[]{:S(2)}) collective-permute-start(bf16[176,256]{1,0:T(8,128)(2,1)S(1)} %get-tuple-element.74), channel_id=1, source_target_pairs={{0,4},{1,12},{2,6},{3,14},{4,0},{5,8},{6,2},{7,10},{8,5},{9,13},{1... | collective-permute-start | bytes 270344 | tf_op jit(solution)/shard_map/ppermute | solution.py:94
  57.0 7.6 %collective-permute-start.18 = (bf16[176,256]{1,0:T(8,128)(2,1)S(1)}, bf16[176,256]{1,0:T(8,128)(2,1)S(1)}, u32[]{:S(2)}, u32[]{:S(2)}) collective-permute-start(bf16[176,256]{1,0:T(8,128)(2,1)S(1)} %get-tuple-element.75), channel_id=1, source_target_pairs={{0,0},{1,8},{2,2},{3,10},{4,4},{5,12},{6,6},{7,14},{8,1},{9,9},{10... | collective-permute-start | bytes 270344 | tf_op jit(solution)/shard_map/ppermute | solution.py:94
  (2 other events, 21.1 us)

commit v7 on v6

--- a/solution.py
+++ b/solution.py
@@ -124,12 +124,14 @@
     row = lax.broadcasted_iota(jnp.int32, (rows, half), 0)
     pair = lax.broadcasted_iota(jnp.int32, (rows, half), 1)
     twice = (row // 2 == pair).astype(BF16)
-    for copy in copies:
+    for copy in copies[:2]:
         copy.wait()
     up = jnp.dot(twice, emb_ref[...], preferred_element_type=F32) * 0.5
     value = (up * gelu_slope(pre_ref[...].astype(F32))).astype(BF16)
     out_ref[...] = value
     along_ref[:rows] = value
+    for copy in copies[2:]:
+        copy.wait()
     for n in range(2):
         along_ref[rows + n * unit : rows + (n + 1) * unit] = weight_ref[n]
 
@@ -141,15 +143,22 @@
     along_ref[unit:] = came_ref[came_ref.shape[0] - unit :, :]
 
 
-def cut_kernel(unit, acts_ref, *out_refs):
+def cut_kernel(unit, acts_hbm, *refs):
+    out_refs, (acts_ref, arrived) = refs[:2], refs[2:]
     _, _, y, x, c = coords()
     for j in range(4):
 
         @pl.when(2 * x + c == j)
         def _():
+            first = 2 * j * unit // 128 * 128
+            last = min(first + acts_ref.shape[1], acts_hbm.shape[1])
+            there = acts_ref.at[:, : last - first]
+            copy = pltpu.make_async_copy(acts_hbm.at[:, first:last], there, arrived)
+            copy.start()
+            copy.wait()
             for s in range(2):
-                first = (2 * j + s) * unit
-                value = acts_ref[:, first : first + unit].astype(F32).T.astype(BF16)
+                start = (2 * j + s) * unit - first
+                value = acts_ref[:, start : start + unit].astype(F32).T.astype(BF16)
                 for b, ref in enumerate(out_refs):
 
                     @pl.when(y ^ b == s)
@@ -330,7 +339,7 @@
         mib=60,
         anywhere=True,
     )
-    own0, own1 = call(functools.partial(cut_kernel, unit), "cut", (pos, pos), (acts,), mib=8)
+    own0, own1 = call(functools.partial(cut_kernel, unit), "cut", (pos, pos), (acts,), [pltpu.VMEM((rows, 512), BF16), pltpu.SemaphoreType.DMA], mib=60, anywhere=True)
     dz_h, dz_z, dz_y = send(dz, SWAP_H), send(dz, SWAP_Z), send(along, SWAP_Y)
     t01, t00 = send(own1, turn(0, 1)), send(own0, turn(0, 0))
     dz_zy = send(dz_z, SWAP_Y)

time: 65.4 us -> 65.3 us (level)
  starting transfers between devices: 41.3 us -> 39.3 us
  Pallas kernels: 10.2 us -> 11.7 us
  waiting for transfers between devices: 11.8 us -> 13.3 us
  local copies, waits for them, and re-layouts: 1.12 us -> 0.01 us
    ppermute x23, starting transfers between devices: 41.3 us -> 39.3 us  [send(): return lax.ppermute(value, ('seq', 'section'), pairs)]
    ppermute x23, waiting for transfers between devices: 11.8 us -> 13.3 us  [send(): return lax.ppermute(value, ('seq', 'section'), pairs)]
    pallas_call x16, Pallas kernels: 10.2 us -> 11.7 us  [call(): pl.pallas_call(kernel, out_shape=shapes, in_specs=[pl.BlockSpec(memory_sp...]
    unnamed x6 -> x4, local copies, waits for them, and re-layouts: 1.12 us -> 0.01 us
  transfers between devices with their start and end apart: 23 -> 23, of which waited for: 7 -> 7; matrix products, arithmetic and copies ran while one was open for 0% -> 0% of each run, Pallas kernels for 9% -> 11%
where the time goes in v7:
time: 65.3 us; the launch traced here: 65.1 us
  starting transfers between devices  39.3 us (60%)
  waiting for transfers between devices  13.3 us (20%)
  Pallas kernels  11.7 us (18%)
  between operations  0.78 us (1%)
    ppermute x23, starting transfers between devices, send(): return lax.ppermute(value, ('seq', 'section'), pairs)  39.3 us
    ppermute x23, waiting for transfers between devices, send(): return lax.ppermute(value, ('seq', 'section'), pairs)  13.3 us
    pallas_call x16, Pallas kernels, call(): pl.pallas_call(kernel, out_shape=shapes, in_specs=[pl.BlockSpec(memory_sp...  11.7 us
  transfers between devices with their start and end apart: 23, of which 7 were waited for; matrix products, arithmetic and copies ran while one was open for 0% of the time, Pallas kernels for 11%

profile of v7, /device:TPU:1, one launch (start us, length us, event | category | flops | bytes accessed | tf_op | source)
XLA Modules:
  0.0 65.1 jit_solution(14031800889461758907)
XLA Ops:
  0.6 2.2 %dz.1 = (bf16[256,384]{1,0:T(8,128)(2,1)}, bf16[608,384]{1,0:T(8,128)(2,1)}) custom-call(bf16[256,384]{1,0:T(8,128)(2,1)} %pre_hbm.1, bf16[128,384]{1,0:T(8,128)(2,1)} %emb_hbm.1, bf16[880,384]{1,0:T(8,128)(2,1)} %filters_ref), custom_call_target="tpu_custom_call" | custom-call | bytes 1024 | tf_op jit(solution)/shard_map/dz/pallas_call | solution.py:305
  2.8 2.1 %collective-permute-start.1 = (bf16[608,384]{1,0:T(8,128)(2,1)}, bf16[608,384]{1,0:T(8,128)(2,1)S(1)}, u32[]{:S(2)}, u32[]{:S(2)}) collective-permute-start(bf16[608,384]{1,0:T(8,128)(2,1)} %get-tuple-element.43), channel_id=1, source_target_pairs={{0,4},{1,5},{2,6},{3,7},{4,0},{5,1},{6,2},{7,3},{8,12},{9,13},{10,... | collective-permute-start | bytes 1400840 | tf_op jit(solution)/shard_map/ppermute | solution.py:94
  5.0 1.3 %collective-permute-start.2 = (bf16[256,384]{1,0:T(8,128)(2,1)}, bf16[256,384]{1,0:T(8,128)(2,1)S(1)}, u32[]{:S(2)}, u32[]{:S(2)}) collective-permute-start(bf16[256,384]{1,0:T(8,128)(2,1)} %get-tuple-element.42.refs_0_), channel_id=1, source_target_pairs={{0,8},{1,9},{2,10},{3,11},{4,12},{5,13},{6,14},{7,15},{8,0},{9,1},... | collective-permute-start | bytes 589832 | tf_op jit(solution)/shard_map/ppermute | solution.py:94
  6.3 2.3 %collective-permute-start = (bf16[256,384]{1,0:T(8,128)(2,1)}, bf16[256,384]{1,0:T(8,128)(2,1)S(1)}, u32[]{:S(2)}, u32[]{:S(2)}) collective-permute-start(bf16[256,384]{1,0:T(8,128)(2,1)} %get-tuple-element.42.refs_0_), channel_id=1, source_target_pairs={{0,16},{1,17},{2,18},{3,19},{4,20},{5,21},{6,22},{7,23},{8,24},{9,... | collective-permute-start | bytes 589832 | tf_op jit(solution)/shard_map/ppermute | solution.py:94
  8.6 2.0 %cut.1 = (bf16[176,256]{1,0:T(8,128)(2,1)}, bf16[176,256]{1,0:T(8,128)(2,1)}) custom-call(bf16[256,1408]{1,0:T(8,128)(2,1)} %acts_hbm.1), custom_call_target="tpu_custom_call" | custom-call | bytes 1024 | tf_op jit(solution)/shard_map/cut/pallas_call | solution.py:305
  10.6 3.4 %collective-permute-start.6 = (bf16[176,256]{1,0:T(8,128)(2,1)}, bf16[176,256]{1,0:T(8,128)(2,1)S(1)}, u32[]{:S(2)}, u32[]{:S(2)}) collective-permute-start(bf16[176,256]{1,0:T(8,128)(2,1)} %get-tuple-element.48), channel_id=1, source_target_pairs={{0,0},{1,8},{2,2},{3,10},{4,4},{5,12},{6,6},{7,14},{8,1},{9,9},{10... | collective-permute-start | bytes 270344 | tf_op jit(solution)/shard_map/ppermute | solution.py:94
  14.3 1.2 %collective-permute-start.4 = (bf16[256,384]{1,0:T(8,128)(2,1)S(1)}, bf16[256,384]{1,0:T(8,128)(2,1)S(1)}, u32[]{:S(2)}, u32[]{:S(2)}) collective-permute-start(bf16[256,384]{1,0:T(8,128)(2,1)S(1)} %collective-permute-done.2.refs_2_), channel_id=1, source_target_pairs={{0,4},{1,5},{2,6},{3,7},{4,0},{5,1},{6,2},{7,3},{8,12},{9,13},{10,... | collective-permute-start | bytes 589832 | tf_op jit(solution)/shard_map/ppermute | solution.py:94
  15.6 1.1 %collective-permute-start.5 = (bf16[256,384]{1,0:T(8,128)(2,1)S(1)}, bf16[256,384]{1,0:T(8,128)(2,1)S(1)}, u32[]{:S(2)}, u32[]{:S(2)}) collective-permute-start(bf16[256,384]{1,0:T(8,128)(2,1)S(1)} %collective-permute-done.refs_4_), channel_id=1, source_target_pairs={{0,4},{1,5},{2,6},{3,7},{4,0},{5,1},{6,2},{7,3},{8,12},{9,13},{10,... | collective-permute-start | bytes 589832 | tf_op jit(solution)/shard_map/ppermute | solution.py:94
  16.7 1.3 %collective-permute-start.3 = (bf16[256,384]{1,0:T(8,128)(2,1)S(1)}, bf16[256,384]{1,0:T(8,128)(2,1)S(1)}, u32[]{:S(2)}, u32[]{:S(2)}) collective-permute-start(bf16[256,384]{1,0:T(8,128)(2,1)S(1)} %collective-permute-done.refs_4_), channel_id=1, source_target_pairs={{0,8},{1,9},{2,10},{3,11},{4,12},{5,13},{6,14},{7,15},{8,0},{9,1},... | collective-permute-start | bytes 589832 | tf_op jit(solution)/shard_map/ppermute | solution.py:94
  18.0 1.2 %collective-permute-done.7.refs_1_ = bf16[176,256]{1,0:T(8,128)(2,1)S(1)} collective-permute-done((bf16[176,256]{1,0:T(8,128)(2,1)}, bf16[176,256]{1,0:T(8,128)(2,1)S(1)}, u32[]{:S(2)}, u32[]{:S(2)}) %collective-permute-start.7) | collective-permute-done | bytes 90144 | tf_op jit(solution)/shard_map/ppermute | solution.py:94
  19.3 1.1 %collective-permute-start.8 = (bf16[2,176,256]{2,1,0:T(8,128)(2,1)S(1)}, bf16[2,176,256]{2,1,0:T(8,128)(2,1)S(1)}, u32[]{:S(2)}, u32[]{:S(2)}) collective-permute-start(bf16[2,176,256]{2,1,0:T(8,128)(2,1)S(1)} %join_near.1.refs_0_), channel_id=1, source_target_pairs={{0,16},{1,17},{2,18},{3,19},{4,20},{5,21},{6,22},{7,23},{8,24},{9,... | collective-permute-start | bytes 540680 | tf_op jit(solution)/shard_map/ppermute | solution.py:94
  20.5 6.8 %collective-permute-done.8.refs_1_ = bf16[2,176,256]{2,1,0:T(8,128)(2,1)S(1)} collective-permute-done((bf16[2,176,256]{2,1,0:T(8,128)(2,1)S(1)}, bf16[2,176,256]{2,1,0:T(8,128)(2,1)S(1)}, u32[]{:S(2)}, u32[]{:S(2)}) %collective-permute-start.8) | collective-permute-done | bytes 180256 | tf_op jit(solution)/shard_map/ppermute | solution.py:94
  27.3 1.3 %collective-permute-start.10 = (bf16[4,176,256]{2,1,0:T(8,128)(2,1)S(1)}, bf16[4,176,256]{2,1,0:T(8,128)(2,1)S(1)}, u32[]{:S(2)}, u32[]{:S(2)}) collective-permute-start(bf16[4,176,256]{2,1,0:T(8,128)(2,1)S(1)} %bitcast.2), channel_id=1, source_target_pairs={{0,2},{1,3},{2,0},{3,1},{4,6},{5,7},{6,4},{7,5},{8,10},{9,11},{10,... | collective-permute-start | bytes 1081352 | tf_op jit(solution)/shard_map/ppermute | solution.py:94
  29.4 2.2 %collective-permute-start.9 = (bf16[256,384]{1,0:T(8,128)(2,1)S(1)}, bf16[256,384]{1,0:T(8,128)(2,1)S(1)}, u32[]{:S(2)}, u32[]{:S(2)}) collective-permute-start(bf16[256,384]{1,0:T(8,128)(2,1)S(1)} %collective-permute-done.3.refs_6_), channel_id=1, source_target_pairs={{0,4},{1,5},{2,6},{3,7},{4,0},{5,1},{6,2},{7,3},{8,12},{9,13},{10,... | collective-permute-start | bytes 589832 | tf_op jit(solution)/shard_map/ppermute | solution.py:94
  31.8 3.2 %collective-permute-done.9.dz_last = bf16[256,384]{1,0:T(8,128)(2,1)S(1)} collective-permute-done((bf16[256,384]{1,0:T(8,128)(2,1)S(1)}, bf16[256,384]{1,0:T(8,128)(2,1)S(1)}, u32[]{:S(2)}, u32[]{:S(2)}) %collective-permute-start.9) | collective-permute-done | bytes 196640 | tf_op jit(solution)/shard_map/ppermute | solution.py:94
  35.0 1.3 %away.1 = (bf16[2080,384]{1,0:T(8,128)(2,1)S(1)}, bf16[880,384]{1,0:T(8,128)(2,1)S(1)}, bf16[2,2,2,176,256]{4,3,2,1,0:T(8,128)(2,1)S(1)}) custom-call(bf16[2080,384]{1,0:T(8,128)(2,1)S(1)} %gather.1.most_ref, bf16[256,384]{1,0:T(8,128)(2,1)S(1)} %collective-permute-done.9.dz_last, ...), custom_call_target="tpu_custom_call", output_to_operand_aliasing={{0}: (0, {})} | custom-call | bytes 1024 | tf_op jit(solution)/shard_map/away/pallas_call | solution.py:305
  36.3 4.3 %collective-permute-start.12 = (bf16[2,2,2,176,256]{4,3,2,1,0:T(8,128)(2,1)S(1)}, bf16[2,2,2,176,256]{4,3,2,1,0:T(8,128)(2,1)S(1)}, u32[]{:S(2)}, u32[]{:S(2)}) collective-permute-start(bf16[2,2,2,176,256]{4,3,2,1,0:T(8,128)(2,1)S(1)} %get-tuple-element.64), channel_id=1, source_target_pairs={{0,1},{1,0},{2,3},{3,2},{4,5},{5,4},{6,7},{7,6},{8,9},{9,8},{10,11... | collective-permute-start | bytes 2162696 | tf_op jit(solution)/shard_map/ppermute | solution.py:94
  40.8 1.2 %keep.1.keep_ref = f32[2,2,2,176,256]{4,3,2,1,0:T(8,128)S(1)} custom-call(bf16[2080,384]{1,0:T(8,128)(2,1)S(1)} %get-tuple-element.62.dz_ref, bf16[880,384]{1,0:T(8,128)(2,1)S(1)} %get-tuple-element.63.weights), custom_call_target="tpu_custom_call" | custom-call | bytes 1024 | tf_op jit(solution)/shard_map/keep/pallas_call | solution.py:305
  44.2 2.6 %filter.1 = (f32[176,384]{1,0:T(8,128)S(1)}, bf16[176,384]{1,0:T(8,128)(2,1)S(1)}, bf16[176,384]{1,0:T(8,128)(2,1)S(1)}, bf16[176,384]{1,0:T(8,128)(2,1)S(1)}, f32[176,384]{1,0:T(8,128)S(1)}) custom-call(bf16[8,176,256]{2,1,0:T(8,128)(2,1)S(1)} %pair.1.own_ref, bf16[8,176,256]{2,1,0:T(8,128)(2,1)S(1)} %collective-permute-done.19.came_ref, ...), custom_call_target="tpu_custom_call" | custom-call | bytes 1024 | tf_op jit(solution)/shard_map/filter/pallas_call | solution.py:305
  46.8 1.8 %collective-permute-start.20 = (bf16[176,384]{1,0:T(8,128)(2,1)S(1)}, bf16[176,384]{1,0:T(8,128)(2,1)S(1)}, u32[]{:S(2)}, u32[]{:S(2)}) collective-permute-start(bf16[176,384]{1,0:T(8,128)(2,1)S(1)} %get-tuple-element.78), channel_id=1, source_target_pairs={{0,12},{1,13},{2,14},{3,15},{4,8},{5,9},{6,10},{7,11},{8,4},{9,5},... | collective-permute-start | bytes 405512 | tf_op jit(solution)/shard_map/ppermute | solution.py:94
  49.6 6.2 %collective-permute-start.14 = (bf16[176,256]{1,0:T(8,128)(2,1)S(1)}, bf16[176,256]{1,0:T(8,128)(2,1)S(1)}, u32[]{:S(2)}, u32[]{:S(2)}) collective-permute-start(bf16[176,256]{1,0:T(8,128)(2,1)S(1)} %get-tuple-element.68), channel_id=1, source_target_pairs={{0,20},{1,28},{2,22},{3,30},{4,16},{5,24},{6,18},{7,26},{8,21},{9,... | collective-permute-start | bytes 270344 | tf_op jit(solution)/shard_map/ppermute | solution.py:94
  56.8 4.8 %collective-permute-start.18 = (bf16[176,256]{1,0:T(8,128)(2,1)S(1)}, bf16[176,256]{1,0:T(8,128)(2,1)S(1)}, u32[]{:S(2)}, u32[]{:S(2)}) collective-permute-start(bf16[176,256]{1,0:T(8,128)(2,1)S(1)} %get-tuple-element.75), channel_id=1, source_target_pairs={{0,0},{1,8},{2,2},{3,10},{4,4},{5,12},{6,6},{7,14},{8,1},{9,9},{10... | collective-permute-start | bytes 270344 | tf_op jit(solution)/shard_map/ppermute | solution.py:94
  61.7 1.2 %home.1 = f32[880,384]{1,0:T(8,128)} custom-call(f32[176,384]{1,0:T(8,128)S(1)} %get-tuple-element.77.first_ref, bf16[176,384]{1,0:T(8,128)(2,1)S(1)} %collective-permute-done.20.zy_ref, bf16[176,384]{1,0:T(8,128)(2,1)S(1)} %collective-permute-done.21.z_ref, bf16[176,384]{1,0:T(8,128)(2,1)S(1)} %collective-permute-done.22.y_ref, ...), custom_call_target="tpu_custom_call" | custom-call | bytes 1024 | tf_op jit(solution)/shard_map/home/pallas_call | solution.py:305
  63.3 1.1 %collective-permute-done.18.refs_3_ = bf16[176,256]{1,0:T(8,128)(2,1)S(1)} collective-permute-done((bf16[176,256]{1,0:T(8,128)(2,1)S(1)}, bf16[176,256]{1,0:T(8,128)(2,1)S(1)}, u32[]{:S(2)}, u32[]{:S(2)}) %collective-permute-start.18) | collective-permute-done | bytes 90144 | tf_op jit(solution)/shard_map/ppermute | solution.py:94
  (42 shorter events, 6.9 us)
Async XLA Ops:
  2.8 28.8 %copy-start.1 = (bf16[256,384]{1,0:T(8,128)(2,1)S(1)}, bf16[256,384]{1,0:T(8,128)(2,1)}, u32[]{:S(2)}) copy-start(bf16[256,384]{1,0:T(8,128)(2,1)} %get-tuple-element.42.refs_0_) | copy-start | bytes 589828
  2.8 12.8 %collective-permute-start.1 = (bf16[608,384]{1,0:T(8,128)(2,1)}, bf16[608,384]{1,0:T(8,128)(2,1)S(1)}, u32[]{:S(2)}, u32[]{:S(2)}) collective-permute-start(bf16[608,384]{1,0:T(8,128)(2,1)} %get-tuple-element.43), channel_id=1, source_target_pairs={{0,4},{1,5},{2,6},{3,7},{4,0},{5,1},{6,2},{7,3},{8,12},{9,13},{10,... | collective-permute-start | bytes 1400840 | tf_op jit(solution)/shard_map/ppermute | solution.py:94
  5.0 9.3 %collective-permute-start.2 = (bf16[256,384]{1,0:T(8,128)(2,1)}, bf16[256,384]{1,0:T(8,128)(2,1)S(1)}, u32[]{:S(2)}, u32[]{:S(2)}) collective-permute-start(bf16[256,384]{1,0:T(8,128)(2,1)} %get-tuple-element.42.refs_0_), channel_id=1, source_target_pairs={{0,8},{1,9},{2,10},{3,11},{4,12},{5,13},{6,14},{7,15},{8,0},{9,1},... | collective-permute-start | bytes 589832 | tf_op jit(solution)/shard_map/ppermute | solution.py:94
  6.3 9.3 %collective-permute-start = (bf16[256,384]{1,0:T(8,128)(2,1)}, bf16[256,384]{1,0:T(8,128)(2,1)S(1)}, u32[]{:S(2)}, u32[]{:S(2)}) collective-permute-start(bf16[256,384]{1,0:T(8,128)(2,1)} %get-tuple-element.42.refs_0_), channel_id=1, source_target_pairs={{0,16},{1,17},{2,18},{3,19},{4,20},{5,21},{6,22},{7,23},{8,24},{9,... | collective-permute-start | bytes 589832 | tf_op jit(solution)/shard_map/ppermute | solution.py:94
  10.6 7.4 %collective-permute-start.6 = (bf16[176,256]{1,0:T(8,128)(2,1)}, bf16[176,256]{1,0:T(8,128)(2,1)S(1)}, u32[]{:S(2)}, u32[]{:S(2)}) collective-permute-start(bf16[176,256]{1,0:T(8,128)(2,1)} %get-tuple-element.48), channel_id=1, source_target_pairs={{0,0},{1,8},{2,2},{3,10},{4,4},{5,12},{6,6},{7,14},{8,1},{9,9},{10... | collective-permute-start | bytes 270344 | tf_op jit(solution)/shard_map/ppermute | solution.py:94
  14.0 5.3 %collective-permute-start.7 = (bf16[176,256]{1,0:T(8,128)(2,1)}, bf16[176,256]{1,0:T(8,128)(2,1)S(1)}, u32[]{:S(2)}, u32[]{:S(2)}) collective-permute-start(bf16[176,256]{1,0:T(8,128)(2,1)} %get-tuple-element.49), channel_id=1, source_target_pairs={{0,4},{1,12},{2,6},{3,14},{4,0},{5,8},{6,2},{7,10},{8,5},{9,13},{1... | collective-permute-start | bytes 270344 | tf_op jit(solution)/shard_map/ppermute | solution.py:94
  14.3 13.0 %collective-permute-start.4 = (bf16[256,384]{1,0:T(8,128)(2,1)S(1)}, bf16[256,384]{1,0:T(8,128)(2,1)S(1)}, u32[]{:S(2)}, u32[]{:S(2)}) collective-permute-start(bf16[256,384]{1,0:T(8,128)(2,1)S(1)} %collective-permute-done.2.refs_2_), channel_id=1, source_target_pairs={{0,4},{1,5},{2,6},{3,7},{4,0},{5,1},{6,2},{7,3},{8,12},{9,13},{10,... | collective-permute-start | bytes 589832 | tf_op jit(solution)/shard_map/ppermute | solution.py:94
  15.6 11.7 %collective-permute-start.5 = (bf16[256,384]{1,0:T(8,128)(2,1)S(1)}, bf16[256,384]{1,0:T(8,128)(2,1)S(1)}, u32[]{:S(2)}, u32[]{:S(2)}) collective-permute-start(bf16[256,384]{1,0:T(8,128)(2,1)S(1)} %collective-permute-done.refs_4_), channel_id=1, source_target_pairs={{0,4},{1,5},{2,6},{3,7},{4,0},{5,1},{6,2},{7,3},{8,12},{9,13},{10,... | collective-permute-start | bytes 589832 | tf_op jit(solution)/shard_map/ppermute | solution.py:94
  16.7 10.5 %collective-permute-start.3 = (bf16[256,384]{1,0:T(8,128)(2,1)S(1)}, bf16[256,384]{1,0:T(8,128)(2,1)S(1)}, u32[]{:S(2)}, u32[]{:S(2)}) collective-permute-start(bf16[256,384]{1,0:T(8,128)(2,1)S(1)} %collective-permute-done.refs_4_), channel_id=1, source_target_pairs={{0,8},{1,9},{2,10},{3,11},{4,12},{5,13},{6,14},{7,15},{8,0},{9,1},... | collective-permute-start | bytes 589832 | tf_op jit(solution)/shard_map/ppermute | solution.py:94
  19.3 7.9 %collective-permute-start.8 = (bf16[2,176,256]{2,1,0:T(8,128)(2,1)S(1)}, bf16[2,176,256]{2,1,0:T(8,128)(2,1)S(1)}, u32[]{:S(2)}, u32[]{:S(2)}) collective-permute-start(bf16[2,176,256]{2,1,0:T(8,128)(2,1)S(1)} %join_near.1.refs_0_), channel_id=1, source_target_pairs={{0,16},{1,17},{2,18},{3,19},{4,20},{5,21},{6,22},{7,23},{8,24},{9,... | collective-permute-start | bytes 540680 | tf_op jit(solution)/shard_map/ppermute | solution.py:94
  27.3 7.7 %collective-permute-start.10 = (bf16[4,176,256]{2,1,0:T(8,128)(2,1)S(1)}, bf16[4,176,256]{2,1,0:T(8,128)(2,1)S(1)}, u32[]{:S(2)}, u32[]{:S(2)}) collective-permute-start(bf16[4,176,256]{2,1,0:T(8,128)(2,1)S(1)} %bitcast.2), channel_id=1, source_target_pairs={{0,2},{1,3},{2,0},{3,1},{4,6},{5,7},{6,4},{7,5},{8,10},{9,11},{10,... | collective-permute-start | bytes 1081352 | tf_op jit(solution)/shard_map/ppermute | solution.py:94
  28.6 6.4 %collective-permute-start.11 = (bf16[352,384]{1,0:T(8,128)(2,1)S(1)}, bf16[352,384]{1,0:T(8,128)(2,1)S(1)}, u32[]{:S(2)}, u32[]{:S(2)}) collective-permute-start(bf16[352,384]{1,0:T(8,128)(2,1)S(1)} %get-tuple-element.56), channel_id=1, source_target_pairs={{0,8},{1,9},{2,10},{3,11},{4,12},{5,13},{6,14},{7,15},{8,0},{9,1},... | collective-permute-start | bytes 811016 | tf_op jit(solution)/shard_map/ppermute | solution.py:94
  29.4 5.6 %collective-permute-start.9 = (bf16[256,384]{1,0:T(8,128)(2,1)S(1)}, bf16[256,384]{1,0:T(8,128)(2,1)S(1)}, u32[]{:S(2)}, u32[]{:S(2)}) collective-permute-start(bf16[256,384]{1,0:T(8,128)(2,1)S(1)} %collective-permute-done.3.refs_6_), channel_id=1, source_target_pairs={{0,4},{1,5},{2,6},{3,7},{4,0},{5,1},{6,2},{7,3},{8,12},{9,13},{10,... | collective-permute-start | bytes 589832 | tf_op jit(solution)/shard_map/ppermute | solution.py:94
  36.3 6.1 %collective-permute-start.12 = (bf16[2,2,2,176,256]{4,3,2,1,0:T(8,128)(2,1)S(1)}, bf16[2,2,2,176,256]{4,3,2,1,0:T(8,128)(2,1)S(1)}, u32[]{:S(2)}, u32[]{:S(2)}) collective-permute-start(bf16[2,2,2,176,256]{4,3,2,1,0:T(8,128)(2,1)S(1)} %get-tuple-element.64), channel_id=1, source_target_pairs={{0,1},{1,0},{2,3},{3,2},{4,5},{5,4},{6,7},{7,6},{8,9},{9,8},{10,11... | collective-permute-start | bytes 2162696 | tf_op jit(solution)/shard_map/ppermute | solution.py:94
  40.7 3.5 %collective-permute-start.19 = (bf16[8,176,256]{2,1,0:T(8,128)(2,1)S(1)}, bf16[8,176,256]{2,1,0:T(8,128)(2,1)S(1)}, u32[]{:S(2)}, u32[]{:S(2)}) collective-permute-start(bf16[8,176,256]{2,1,0:T(8,128)(2,1)S(1)} %pair.1.own_ref), channel_id=1, source_target_pairs={{0,1},{1,0},{2,3},{3,2},{4,5},{5,4},{6,7},{7,6},{8,9},{9,8},{10,11... | collective-permute-start | bytes 2162696 | tf_op jit(solution)/shard_map/ppermute | solution.py:94
  42.5 7.0 %collective-permute-start.13 = (bf16[2,176,256]{2,1,0:T(8,128)(2,1)S(1)}, bf16[2,176,256]{2,1,0:T(8,128)(2,1)S(1)}, u32[]{:S(2)}, u32[]{:S(2)}) collective-permute-start(bf16[2,176,256]{2,1,0:T(8,128)(2,1)S(1)} %get-tuple-element.67), channel_id=1, source_target_pairs={{0,2},{1,3},{2,0},{3,1},{4,6},{5,7},{6,4},{7,5},{8,10},{9,11},{10,... | collective-permute-start | bytes 540680 | tf_op jit(solution)/shard_map/ppermute | solution.py:94
  43.3 12.5 %collective-permute-start.16 = (bf16[2,176,256]{2,1,0:T(8,128)(2,1)S(1)}, bf16[2,176,256]{2,1,0:T(8,128)(2,1)S(1)}, u32[]{:S(2)}, u32[]{:S(2)}) collective-permute-start(bf16[2,176,256]{2,1,0:T(8,128)(2,1)S(1)} %get-tuple-element.73), channel_id=1, source_target_pairs={{0,2},{1,3},{2,0},{3,1},{4,6},{5,7},{6,4},{7,5},{8,10},{9,11},{10,... | collective-permute-start | bytes 540680 | tf_op jit(solution)/shard_map/ppermute | solution.py:94
  46.8 9.0 %collective-permute-start.20 = (bf16[176,384]{1,0:T(8,128)(2,1)S(1)}, bf16[176,384]{1,0:T(8,128)(2,1)S(1)}, u32[]{:S(2)}, u32[]{:S(2)}) collective-permute-start(bf16[176,384]{1,0:T(8,128)(2,1)S(1)} %get-tuple-element.78), channel_id=1, source_target_pairs={{0,12},{1,13},{2,14},{3,15},{4,8},{5,9},{6,10},{7,11},{8,4},{9,5},... | collective-permute-start | bytes 405512 | tf_op jit(solution)/shard_map/ppermute | solution.py:94
  48.6 8.2 %collective-permute-start.21 = (bf16[176,384]{1,0:T(8,128)(2,1)S(1)}, bf16[176,384]{1,0:T(8,128)(2,1)S(1)}, u32[]{:S(2)}, u32[]{:S(2)}) collective-permute-start(bf16[176,384]{1,0:T(8,128)(2,1)S(1)} %get-tuple-element.79), channel_id=1, source_target_pairs={{0,8},{1,9},{2,10},{3,11},{4,12},{5,13},{6,14},{7,15},{8,0},{9,1},... | collective-permute-start | bytes 405512 | tf_op jit(solution)/shard_map/ppermute | solution.py:94
  48.6 13.1 %collective-permute-start.22 = (bf16[176,384]{1,0:T(8,128)(2,1)S(1)}, bf16[176,384]{1,0:T(8,128)(2,1)S(1)}, u32[]{:S(2)}, u32[]{:S(2)}) collective-permute-start(bf16[176,384]{1,0:T(8,128)(2,1)S(1)} %get-tuple-element.80), channel_id=1, source_target_pairs={{0,4},{1,5},{2,6},{3,7},{4,0},{5,1},{6,2},{7,3},{8,12},{9,13},{10,... | collective-permute-start | bytes 405512 | tf_op jit(solution)/shard_map/ppermute | solution.py:94
  49.6 13.3 %collective-permute-start.14 = (bf16[176,256]{1,0:T(8,128)(2,1)S(1)}, bf16[176,256]{1,0:T(8,128)(2,1)S(1)}, u32[]{:S(2)}, u32[]{:S(2)}) collective-permute-start(bf16[176,256]{1,0:T(8,128)(2,1)S(1)} %get-tuple-element.68), channel_id=1, source_target_pairs={{0,20},{1,28},{2,22},{3,30},{4,16},{5,24},{6,18},{7,26},{8,21},{9,... | collective-permute-start | bytes 270344 | tf_op jit(solution)/shard_map/ppermute | solution.py:94
  55.8 7.0 %collective-permute-start.15 = (bf16[176,256]{1,0:T(8,128)(2,1)S(1)}, bf16[176,256]{1,0:T(8,128)(2,1)S(1)}, u32[]{:S(2)}, u32[]{:S(2)}) collective-permute-start(bf16[176,256]{1,0:T(8,128)(2,1)S(1)} %get-tuple-element.69), channel_id=1, source_target_pairs={{0,16},{1,24},{2,18},{3,26},{4,20},{5,28},{6,22},{7,30},{8,17},{9,... | collective-permute-start | bytes 270344 | tf_op jit(solution)/shard_map/ppermute | solution.py:94
  55.9 7.4 %collective-permute-start.17 = (bf16[176,256]{1,0:T(8,128)(2,1)S(1)}, bf16[176,256]{1,0:T(8,128)(2,1)S(1)}, u32[]{:S(2)}, u32[]{:S(2)}) collective-permute-start(bf16[176,256]{1,0:T(8,128)(2,1)S(1)} %get-tuple-element.74), channel_id=1, source_target_pairs={{0,4},{1,12},{2,6},{3,14},{4,0},{5,8},{6,2},{7,10},{8,5},{9,13},{1... | collective-permute-start | bytes 270344 | tf_op jit(solution)/shard_map/ppermute | solution.py:94
  56.8 7.6 %collective-permute-start.18 = (bf16[176,256]{1,0:T(8,128)(2,1)S(1)}, bf16[176,256]{1,0:T(8,128)(2,1)S(1)}, u32[]{:S(2)}, u32[]{:S(2)}) collective-permute-start(bf16[176,256]{1,0:T(8,128)(2,1)S(1)} %get-tuple-element.75), channel_id=1, source_target_pairs={{0,0},{1,8},{2,2},{3,10},{4,4},{5,12},{6,6},{7,14},{8,1},{9,9},{10... | collective-permute-start | bytes 270344 | tf_op jit(solution)/shard_map/ppermute | solution.py:94
  (1 other events, 19.8 us)
